TPU v7x, 32 devices: a whole 2x2x4 slice. The times are simulated.
32 devices in a mesh: groups: 2 (over y), pool: 4 (over z), tensor: 4 (over x, core).
Axes of the slice: x: 2, y: 2, z: 4, core: 2. Of those that a mesh axis runs over, the one named last changes fastest.
Arguments:
- residual: bfloat16 [32, 8192], P('groups', 'pool'), parts along dimension 0, may hold values from -48 to 48
- norm_gain: bfloat16 [8192], P('pool'), may hold values from 0.099609375 to 1.8984375
- w_query: bfloat16 [8192, 8192], P('pool', 'tensor'), may hold values from -0.0625 to 0.0625
- w_key: bfloat16 [8192, 1024], P('pool', 'tensor'), may hold values from -0.0625 to 0.0625
- w_value: bfloat16 [8192, 1024], P('pool', 'tensor'), may hold values from -0.0625 to 0.0625
- w_out: bfloat16 [8192, 8192], P('tensor', 'pool'), may hold values from -0.0625 to 0.0625
- k_cache: bfloat16 [384, 128, 1024], P(('groups', 'pool'), None, 'tensor'), parts along dimension 0, may hold values from -210 to 210
- v_cache: bfloat16 [384, 128, 1024], P(('groups', 'pool'), None, 'tensor'), parts along dimension 0, may hold values from -6 to 6
- context_len: int32 [32], P('groups'), parts along dimension 0, may hold values from 0 to 6144, as said below
- routes: int32 [8, 4, 2], P('groups'), parts along dimension 0, may hold values from 0 to 15, as said below
- slot_route: int32 [384], P(('groups', 'pool')), parts along dimension 0, may hold values from -1 to 7, as said below
- slot_block: int32 [384], P(('groups', 'pool')), parts along dimension 0, may hold values from 0 to 47, as said below
Outputs:
- updated: bfloat16 [32, 8192], P('groups', 'pool'), parts along dimension 0
There are 2 independent parts, one for each index of `groups`. A program takes and returns all parts, laid end to end along the dimension named above; an argument that names none is the same for every part. Nothing has to cross between parts.
Inputs may be any that keep to these rules, and one draw needn't show every extreme that they name: Request r has its home on pool device r // 4. routes[o, h] lists 2 distinct requests of home device h (h * 4 to h * 4 + 3); every request is listed for some owner. `slot_route`: slot g sits on pool device g // 48; -1 marks an empty slot, else e = h * 2 + c names the request routes[g // 48, h, c]. Each device has at most 48 live slots, and some device has all of them live. A listed request may have no block on that device. `slot_block`: the blocks of a request over all devices are numbered 0, 1, 2, ... without gaps or repeats; 0 in empty slots. No request has more than 48 blocks, and some request has exactly 48. A request's cached tokens are the positions block * 128 + i (i < 128) below context_len in its blocks; its last block holds at least one of them; a request without blocks has 0.
All inputs are finite; a program needn't handle non-finite values.
Results may differ from a plain program's by a relative error of at most 0.012.
The roundings to bfloat16 on the way count: a program that leaves them out, or rounds other values in their place, can miss the bound.
Values may be sent and summed in bfloat16 or wider, within the bound.
No kernel may reach another device: no remote copies, remote signals or barrier semaphores. Data moves between devices by JAX's collectives and lax.ppermute only.
A program may use at most 128 MiB of HBM per device.

v0:
```python
import math

import jax
import jax.numpy as jnp
from jax import lax
from jax.sharding import PartitionSpec as P

D = 8192
HD = 128
BS = 128


EPSILON = 1e-05
THETA = 500000.0
NEG_FILL = -1e30
EXACT = lax.Precision.HIGHEST


def rotate(vectors, positions):
    half_dim = vectors.shape[-1] // 2
    frequencies = THETA ** (-2.0 * jnp.arange(half_dim, dtype=jnp.float32) / vectors.shape[-1])
    angles = positions.astype(jnp.float32)[:, None] * frequencies[None, :]
    cosine = jnp.cos(angles)[:, None, :]
    sine_part = jnp.sin(angles)[:, None, :]
    first_half = vectors[..., :half_dim]
    second_half = vectors[..., half_dim:]
    return jnp.concatenate(
        [
            first_half * cosine - second_half * sine_part,
            second_half * cosine + first_half * sine_part,
        ],
        axis=-1,
    )


def send_back(parts):
    return (
        lax.all_to_all(parts[0], "pool", split_axis=0, concat_axis=0, tiled=True),
        lax.all_to_all(parts[1], "pool", split_axis=0, concat_axis=0, tiled=True),
        lax.all_to_all(parts[2], "pool", split_axis=0, concat_axis=0, tiled=True),
    )


def per_device(
    residual,
    norm_gain,
    w_query,
    w_key,
    w_value,
    w_out,
    k_cache,
    v_cache,
    context_len,
    routes,
    slot_route,
    slot_block,
):
    pool_count = lax.axis_size("pool")
    pool_index = lax.axis_index("pool")
    request_count = residual.shape[0]
    per_home = request_count // pool_count
    home_first = pool_index * per_home
    query_width = w_query.shape[1]
    key_width = w_key.shape[1]
    local_heads = query_width // HD
    local_kv = key_width // HD
    group_size = local_heads // local_kv
    slot_count = k_cache.shape[0]
    score_scale = 1.0 / math.sqrt(HD)
    resid_f = residual.astype(jnp.float32)
    square_total = lax.psum(jnp.sum(resid_f * resid_f, axis=1), "pool")
    normed = (
        resid_f
        * lax.rsqrt(square_total / D + EPSILON)[:, None]
        * norm_gain.astype(jnp.float32)[None, :]
    ).astype(jnp.bfloat16)
    owner_routes = lax.dynamic_slice_in_dim(routes, pool_index, 1, 0)[0].reshape(-1)
    slot_request = jnp.where(slot_route >= 0, owner_routes[jnp.maximum(slot_route, 0)], -1)
    key_blocks = k_cache.reshape(slot_count, BS, local_kv, HD)
    value_blocks = v_cache.reshape(slot_count, BS, local_kv, HD)
    positions = slot_block[:, None] * BS + jnp.arange(BS, dtype=jnp.int32)[None, :]
    sent_ids = lax.dynamic_slice_in_dim(routes, pool_index, 1, 1)[:, 0, :]
    home_rows = lax.psum_scatter(
        jnp.concatenate(
            [
                jnp.dot(normed, w_query, preferred_element_type=jnp.float32),
                jnp.dot(normed, w_key, preferred_element_type=jnp.float32),
                jnp.dot(normed, w_value, preferred_element_type=jnp.float32),
            ],
            axis=1,
        ),
        "pool",
        scatter_dimension=0,
        tiled=True,
    )
    home_len = lax.dynamic_slice_in_dim(context_len, home_first, per_home, 0)
    row_total = home_rows.shape[0]
    query = rotate(home_rows[:, :query_width].reshape(row_total, local_heads, HD), home_len).astype(
        jnp.bfloat16
    )
    key_new = rotate(
        home_rows[:, query_width : query_width + key_width].reshape(row_total, local_kv, HD),
        home_len,
    ).astype(jnp.bfloat16)
    value_new = (
        home_rows[:, query_width + key_width :]
        .astype(jnp.bfloat16)
        .reshape(row_total, local_kv, HD)
    )
    home_query = query.reshape(row_total, query_width)
    sent_query = home_query[sent_ids - home_first]
    sent_info = jnp.stack([sent_ids, context_len[sent_ids]], axis=-1)
    rows_query = lax.all_to_all(sent_query, "pool", split_axis=0, concat_axis=0, tiled=True)
    rows_info = lax.all_to_all(sent_info, "pool", split_axis=0, concat_axis=0, tiled=True)
    home_total = rows_query.shape[0]
    item_total = rows_query.shape[1]
    flat_query = rows_query.reshape(home_total * item_total, query_width)
    flat_ids = rows_info[..., 0].reshape(-1)
    flat_len = rows_info[..., 1].reshape(-1)
    matches = slot_request[:, None] == flat_ids[None, :]
    slot_query = jnp.dot(
        matches.astype(jnp.bfloat16), flat_query, preferred_element_type=jnp.float32
    ).astype(jnp.bfloat16)
    grouped = slot_query.reshape(slot_count, local_kv, group_size, HD)
    slot_len = jnp.sum(jnp.where(matches, flat_len[None, :], 0), axis=1)
    present = jnp.any(matches, axis=1)
    in_range = present[:, None] & (positions < slot_len[:, None])
    valid_mask = in_range[:, None, None, :]
    scores = (
        jnp.einsum("skgd,sbkd->skgb", grouped, key_blocks, preferred_element_type=jnp.float32)
        * score_scale
    )
    block_peak = jnp.max(jnp.where(valid_mask, scores, NEG_FILL), axis=3)
    exponent = jnp.exp(jnp.where(valid_mask, scores - block_peak[..., None], NEG_FILL))
    weights = exponent.astype(jnp.bfloat16)
    block_sum = jnp.einsum(
        "skgb,sbkd->skgd", weights, value_blocks, preferred_element_type=jnp.float32
    )
    block_mass = jnp.sum(exponent, axis=3)
    hits = matches.T
    row_peak = jnp.max(jnp.where(hits[:, :, None, None], block_peak[None], NEG_FILL), axis=1)
    factor = jnp.where(hits[:, :, None, None], jnp.exp(block_peak[None] - row_peak[:, None]), 0.0)
    row_sum = jnp.einsum("rskg,skgd->rkgd", factor, block_sum, precision=EXACT)
    row_mass = jnp.einsum("rskg,skg->rkg", factor, block_mass, precision=EXACT)
    back_sum, back_peak, back_mass = send_back(
        (
            row_sum.reshape(home_total, item_total, query_width),
            row_peak.reshape(home_total, item_total, local_heads),
            row_mass.reshape(home_total, item_total, local_heads),
        )
    )
    local_ids = (sent_ids - home_first).reshape(-1)
    owned = local_ids[:, None] == jnp.arange(per_home, dtype=jnp.int32)[None, :]
    sum_rows = back_sum.reshape(-1, local_kv, group_size, HD)
    peak_rows = back_peak.reshape(-1, local_kv, group_size)
    mass_rows = back_mass.reshape(-1, local_kv, group_size)
    query_grid = home_query.reshape(per_home, local_kv, group_size, HD)
    own_score = (
        jnp.einsum("rkgd,rkd->rkg", query_grid, key_new, preferred_element_type=jnp.float32)
        * score_scale
    )
    overall = jnp.maximum(
        own_score, jnp.max(jnp.where(owned[:, :, None, None], peak_rows[:, None], NEG_FILL), axis=0)
    )
    merge_weight = jnp.where(
        owned[:, :, None, None], jnp.exp(peak_rows[:, None] - overall[None]), 0.0
    )
    own_weight = jnp.exp(own_score - overall)
    numerator = (
        jnp.einsum("prkg,pkgd->rkgd", merge_weight, sum_rows, precision=EXACT)
        + own_weight[..., None] * value_new.astype(jnp.float32)[:, :, None, :]
    )
    denominator = jnp.einsum("prkg,pkg->rkg", merge_weight, mass_rows, precision=EXACT) + own_weight
    attention = (
        (numerator / denominator[..., None]).astype(jnp.bfloat16).reshape(per_home, query_width)
    )
    partial_out = jnp.dot(
        lax.all_gather(attention, "pool", axis=0, tiled=True),
        w_out,
        preferred_element_type=jnp.float32,
    )
    head_total = lax.psum(partial_out, "tensor")
    return (resid_f + head_total).astype(jnp.bfloat16)


def solution(mesh):
    placed = (
        P("groups", "pool"),
        P("pool"),
        P("pool", "tensor"),
        P("pool", "tensor"),
        P("pool", "tensor"),
        P("tensor", "pool"),
        P(("groups", "pool"), None, "tensor"),
        P(("groups", "pool"), None, "tensor"),
        P("groups"),
        P("groups", None, None),
        P(("groups", "pool")),
        P(("groups", "pool")),
    )
    return jax.shard_map(
        per_device, mesh=mesh, in_specs=placed, out_specs=P("groups", "pool"), check_vma=False
    )
```

profile of v0, /device:TPU:0, one launch (start us, length us, event | category | flops | bytes accessed | tf_op | source)
XLA Modules:
  0.0 174.0 jit_solution(6075537253549258072)
XLA Ops:
  6.5 1.1 subtract_reduce_fusion
  7.9 1.3 gather_fusion
  10.1 6.3 %all-to-all-start = ((s32[4,2,2]{1,2,0:T(2,128)}), s32[4,2,2]{1,2,0:T(2,128)S(1)}, u32[]{:S(2)}, u32[]{:S(2)}) async-start(s32[4,2,2]{1,2,0:T(2,128)} %copy.58), calls=%async_computation | async-start | bytes 8192 | tf_op jit(solution)/shard_map/all_to_all | solution.py:114
  17.4 12.2 %psum.14 = f32[16]{0:T(128)S(1)} all-reduce(f32[16]{0:T(128)S(1)} %fusion.20), channel_id=1, replica_groups=mesh['groups'=2,'pool'=4,'tensor'=4] {'pool'}, use_global_device_ids=true, to_apply=%region_3.4 | all-reduce | flops 16 | bytes 128 | tf_op jit(solution)/shard_map/psum | solution.py:71
  30.3 1.5 fusion.55
  31.8 1.5 fusion.53
  33.4 4.7 %fusion.57 = f32[16,2048]{1,0:T(8,128)S(1)} fusion(bf16[2048,2048]{1,0:T(8,128)(2,1)} %param.14, bf16[16,2048]{1,0:T(8,128)(2,1)S(1)} %copy-done.2, f32[2048]{0:T(1024)S(1)} %convert_element_type.45, f32[16]{0:T(128)S(1)} %add_rsqrt_fusion), kind=kOutput, calls=%fused_computation.110 | convolution fusion | flops 134348800 | bytes 8593472 | tf_op jit(solution)/shard_map/dot_general | solution.py:86
  41.4 5.0 %compare_select_fusion.10 = s32[48]{0:T(128)S(1)} fusion(s32[48]{0:T(128)S(1)} %copy-done.3, s32[]{:T(128)} %bitcast.9, s32[]{:T(128)} %bitcast.2, s32[]{:T(128)} %bitcast.3, s32[]{:T(128)} %bitcast.4, s32[]{:T(128)} %bitcast.5, s32[]{:T(128)} %bitcast.6, s32[]{:T(128)} %bitcast.7, s32[]{:T(128)} %bitcast.8), kind=kLoop, calls=%fused_computation.96 | loop fusion | flops 816 | bytes 416 | tf_op jit(solution)/shard_map/jit(_where)/select_n | solution.py:78
  47.7 24.1 %all-reduce.6.cloned.1.call-done = f32[16,2560]{1,0:T(8,128)} async-done(((f32[16,2560]{1,0:T(8,128)}), f32[16,2560]{1,0:T(8,128)}) %all-reduce.6.cloned.1.call-update) | async-done | bytes 163856
  74.9 3.4 %all-to-all-start.1 = ((bf16[4,2,2048]{2,1,0:T(2,128)(2,1)}), bf16[4,2,2048]{2,1,0:T(2,128)(2,1)S(1)}, u32[]{:S(2)}, u32[]{:S(2)}) async-start(bf16[4,2,2048]{2,1,0:T(2,128)(2,1)} %reshape.293), calls=%async_computation.1 | async-start | bytes 65536 | tf_op jit(solution)/shard_map/all_to_all | solution.py:113
  79.4 4.5 %all-to-all-done.1 = bf16[4,2,2048]{2,1,0:T(2,128)(2,1)S(1)} async-done(((bf16[4,2,2048]{2,1,0:T(2,128)(2,1)}), bf16[4,2,2048]{2,1,0:T(2,128)(2,1)S(1)}, u32[]{:S(2)}, u32[]{:S(2)}) %all-to-all-start.1) | async-done | bytes 32800 | tf_op jit(solution)/shard_map/all_to_all | solution.py:113
  84.3 2.5 %select_reduce_fusion = (f32[48,2,8]{2,1,0:T(2,128)S(1)}, f32[48,2,8,128]{3,2,1,0:T(8,128)}) fusion(pred[48,128]{1,0:T(8,128)(4,1)S(1)} %fusion.30, bf16[48,2,8,128]{3,2,1,0:T(8,128)(2,1)S(1)} %bitcast.96, bf16[48,128,256]{2,1,0:T(8,128)(2,1)S(1)} %copy-done), kind=kOutput, calls=%fused_computation.18 | convolution fusion | flops 25459968 | bytes 3744768 | tf_op jit(solution)/shard_map/skgd,sbkd->skgb/dot_general | solution.py:130
  87.8 3.2 %all-to-all-start.3 = ((f32[4,2,16]{2,1,0:T(2,128)}), f32[4,2,16]{2,1,0:T(2,128)S(1)}, u32[]{:S(2)}, u32[]{:S(2)}) async-start(f32[4,2,16]{2,1,0:T(2,128)} %reshape.263), calls=%async_computation.3 | async-start | bytes 8192 | tf_op jit(solution)/shard_map/all_to_all | solution.py:39
  91.0 1.3 fusion.14
  92.3 3.8 %fusion = f32[48,2,8,128]{3,2,1,0:T(8,128)} fusion(f32[48,2,8,128]{3,2,1,0:T(8,128)} %get-tuple-element.28, f32[48,2,8]{2,1,0:T(2,128)S(1)} %get-tuple-element.27, pred[48,128]{1,0:T(8,128)(4,1)S(1)} %fusion.30, bf16[48,128,256]{2,1,0:T(8,128)(2,1)} %param.19), kind=kOutput, calls=%fused_computation.2 | convolution fusion | flops 25460736 | bytes 3941376 | tf_op jit(solution)/shard_map/skgb,sbkd->skgd/dot_general | solution.py:136
  97.1 5.1 %all-to-all-start.4 = ((f32[4,2,16]{2,1,0:T(2,128)}), f32[4,2,16]{2,1,0:T(2,128)S(1)}, u32[]{:S(2)}, u32[]{:S(2)}) async-start(f32[4,2,16]{2,1,0:T(2,128)} %reshape.265), calls=%async_computation.4 | async-start | bytes 8192 | tf_op jit(solution)/shard_map/all_to_all | solution.py:40
  102.2 1.5 convolution_bitcast_fusion
  104.6 3.2 %all-to-all-done.4 = f32[4,2,16]{2,1,0:T(2,128)S(1)} async-done(((f32[4,2,16]{2,1,0:T(2,128)}), f32[4,2,16]{2,1,0:T(2,128)S(1)}, u32[]{:S(2)}, u32[]{:S(2)}) %all-to-all-start.4) | async-done | bytes 544 | tf_op jit(solution)/shard_map/all_to_all | solution.py:40
  107.7 3.3 %all-to-all-start.2 = ((f32[4,2,2048]{2,1,0:T(2,128)}), f32[4,2,2048]{2,1,0:T(2,128)S(1)}, u32[]{:S(2)}, u32[]{:S(2)}) async-start(f32[4,2,2048]{2,1,0:T(2,128)} %reshape.261), calls=%async_computation.2 | async-start | bytes 131072 | tf_op jit(solution)/shard_map/all_to_all | solution.py:38
  111.7 5.0 %all-to-all-done.2 = f32[4,2,2048]{2,1,0:T(2,128)S(1)} async-done(((f32[4,2,2048]{2,1,0:T(2,128)}), f32[4,2,2048]{2,1,0:T(2,128)S(1)}, u32[]{:S(2)}, u32[]{:S(2)}) %all-to-all-start.2) | async-done | bytes 65568 | tf_op jit(solution)/shard_map/all_to_all | solution.py:38
  117.1 13.1 %all-gather = bf16[4,4,2048]{2,1,0:T(4,128)(2,1)S(1)} all-gather(bf16[1,4,2048]{2,1,0:T(4,128)(2,1)S(1)} %bitcast.102), channel_id=1, replica_groups=mesh['groups'=2,'pool'=4,'tensor'=4] {'pool'}, dimensions={0}, use_global_device_ids=true | all-gather | bytes 81920 | tf_op jit(solution)/shard_map/all_gather | solution.py:178
  130.3 5.2 %fusion.61 = f32[16,2048]{1,0:T(8,128)} fusion(bf16[16,2048]{1,0:T(8,128)(2,1)S(1)} %reshape.305, bf16[2048,2048]{1,0:T(8,128)(2,1)} %param.17), kind=kOutput, calls=%fused_computation.113 | convolution fusion | flops 134217728 | bytes 8585216 | tf_op jit(solution)/shard_map/dot_general | solution.py:177
  135.5 30.1 %all-reduce.4.cloned.1.call-done = f32[16,2048]{1,0:T(8,128)} async-done(((f32[16,2048]{1,0:T(8,128)}), f32[16,2048]{1,0:T(8,128)}) %all-reduce.4.cloned.1.call-update) | async-done | bytes 131088 | tf_op jit(solution)/shard_map/psum | solution.py:182
  165.6 1.5 fusion.23
  (90 shorter events, 15.2 us)
Async XLA Ops:
  6.5 77.8 %copy-start = (bf16[48,128,256]{2,1,0:T(8,128)(2,1)S(1)}, bf16[48,128,256]{2,1,0:T(8,128)(2,1)}, u32[]{:S(2)}) copy-start(bf16[48,128,256]{2,1,0:T(8,128)(2,1)} %param.18) | copy-start | bytes 9437188
  6.5 25.3 %copy-start.2 = (bf16[16,2048]{1,0:T(8,128)(2,1)S(1)}, bf16[16,2048]{1,0:T(8,128)(2,1)}, u32[]{:S(2)}) copy-start(bf16[16,2048]{1,0:T(8,128)(2,1)} %param.12) | copy-start | bytes 196612
  10.1 37.0 %all-to-all-start = ((s32[4,2,2]{1,2,0:T(2,128)}), s32[4,2,2]{1,2,0:T(2,128)S(1)}, u32[]{:S(2)}, u32[]{:S(2)}) async-start(s32[4,2,2]{1,2,0:T(2,128)} %copy.58), calls=%async_computation | async-start | bytes 8192 | tf_op jit(solution)/shard_map/all_to_all | solution.py:114
  16.4 55.3 %all-reduce.6.cloned.1.call-start = ((), (), s32[]{:S(2)}) async-start(), calls=%async_computation.6 | async-start | bytes 327680
  33.3 6.1 %copy-start.1 = (s32[16]{0:T(128)S(1)}, s32[16]{0:T(128)}, u32[]{:S(2)}) copy-start(s32[16]{0:T(128)} %param.20) | copy-start | bytes 196
  33.3 6.2 %copy-start.4 = (s32[48]{0:T(128)S(1)}, s32[48]{0:T(128)}, u32[]{:S(2)}) copy-start(s32[48]{0:T(128)} %param.23) | copy-start | bytes 580
  33.3 7.3 %copy-start.5 = (u32[32]{0:T(128)S(1)}, u32[32]{0:T(128)}, u32[]{:S(2)}) copy-start(u32[32]{0:T(128)} %constant.56) | copy-start | bytes 388
  33.3 8.1 %copy-start.3 = (s32[48]{0:T(128)S(1)}, s32[48]{0:T(128)}, u32[]{:S(2)}) copy-start(s32[48]{0:T(128)} %param.22) | copy-start | bytes 580
  74.9 9.0 %all-to-all-start.1 = ((bf16[4,2,2048]{2,1,0:T(2,128)(2,1)}), bf16[4,2,2048]{2,1,0:T(2,128)(2,1)S(1)}, u32[]{:S(2)}, u32[]{:S(2)}) async-start(bf16[4,2,2048]{2,1,0:T(2,128)(2,1)} %reshape.293), calls=%async_computation.1 | async-start | bytes 65536 | tf_op jit(solution)/shard_map/all_to_all | solution.py:113
  87.8 9.3 %all-to-all-start.3 = ((f32[4,2,16]{2,1,0:T(2,128)}), f32[4,2,16]{2,1,0:T(2,128)S(1)}, u32[]{:S(2)}, u32[]{:S(2)}) async-start(f32[4,2,16]{2,1,0:T(2,128)} %reshape.263), calls=%async_computation.3 | async-start | bytes 8192 | tf_op jit(solution)/shard_map/all_to_all | solution.py:39
  97.1 10.6 %all-to-all-start.4 = ((f32[4,2,16]{2,1,0:T(2,128)}), f32[4,2,16]{2,1,0:T(2,128)S(1)}, u32[]{:S(2)}, u32[]{:S(2)}) async-start(f32[4,2,16]{2,1,0:T(2,128)} %reshape.265), calls=%async_computation.4 | async-start | bytes 8192 | tf_op jit(solution)/shard_map/all_to_all | solution.py:40
  107.7 9.0 %all-to-all-start.2 = ((f32[4,2,2048]{2,1,0:T(2,128)}), f32[4,2,2048]{2,1,0:T(2,128)S(1)}, u32[]{:S(2)}, u32[]{:S(2)}) async-start(f32[4,2,2048]{2,1,0:T(2,128)} %reshape.261), calls=%async_computation.2 | async-start | bytes 131072 | tf_op jit(solution)/shard_map/all_to_all | solution.py:38
  111.0 54.6 %all-reduce.4.cloned.1.call-start = ((), (), s32[]{:S(2)}) async-start(), calls=%async_computation.5 | async-start | bytes 262144 | tf_op jit(solution)/shard_map/psum | solution.py:182
Sparse Core Ops, SparseCore 0:
  38.8 32.8 all-reduce.5
  135.7 29.9 all-reduce.3
where the time goes:
time: 175 us; the launch traced here: 174 us
  waiting for transfers between devices  66.9 us (38%)
  blocking collectives  25.3 us (14%)
  matrix products  21.9 us (13%)
  starting transfers between devices  21.3 us (12%)
  between operations  14.3 us (8%)
  other arithmetic  13.3 us (8%)
  local copies, waits for them, and re-layouts  10.9 us (6%)
    psum x1, waiting for transfers between devices, per_device(): head_total = lax.psum(partial_out, 'tensor')  30.1 us
    unnamed x3, waiting for transfers between devices  24.1 us
    all_gather x1, blocking collectives, per_device(): lax.all_gather(attention, 'pool', axis=0, tiled=True)  13.1 us
    psum x1, blocking collectives, per_device(): square_total = lax.psum(jnp.sum(resid_f * resid_f, axis=1), 'pool')  12.2 us
    all_to_all x1, starting transfers between devices, per_device(): lax.all_to_all(sent_info, 'pool', split_axis=0, concat_axis=0, tiled=True)  6.32 us
    dot_general x1, matrix products, per_device(): jnp.dot(lax.all_gather(attention, 'pool', axis=0, tiled=True), w_out, pre...  5.24 us
    all_to_all x1, starting transfers between devices, send_back(): lax.all_to_all(parts[2], 'pool', split_axis=0, concat_axis=0, tiled=True)  5.06 us
    all_to_all x1, waiting for transfers between devices, send_back(): lax.all_to_all(parts[0], 'pool', split_axis=0, concat_axis=0, tiled=True)  5.03 us
  transfers between devices with their start and end apart: 7, of which 5 were waited for; matrix products, arithmetic and copies ran while one was open for 16% of the time, Pallas kernels for 0%

commit v1 on v0

--- a/solution.py
+++ b/solution.py
@@ -1,19 +1,383 @@
+import functools
 import math
 
 import jax
 import jax.numpy as jnp
 from jax import lax
+from jax.experimental import pallas as pl
+from jax.experimental.pallas import tpu as pltpu
 from jax.sharding import PartitionSpec as P
 
 D = 8192
 HD = 128
 BS = 128
-
 
 EPSILON = 1e-05
 THETA = 500000.0
 NEG_FILL = -1e30
 EXACT = lax.Precision.HIGHEST
+CHUNK = 256
+
+
+def listed_at(routes, owner, row):
+    per_home = routes.shape[1]
+    return routes[owner, row % per_home, row // per_home]
+
+
+def load_kernel(count, *rest):
+    sources, outs, sems = rest[1 : 1 + count], rest[1 + count : -1], rest[-1]
+    copies = [
+        pltpu.make_async_copy(sources[i], outs[i], sems.at[i]) for i in range(count)
+    ]
+    for copy in copies:
+        copy.start()
+    for copy in copies:
+        copy.wait()
+
+
+def load(after, *sources):
+    count = len(sources)
+    return pl.pallas_call(
+        functools.partial(load_kernel, count),
+        out_shape=[pltpu.VMEM(source.shape, source.dtype) for source in sources],
+        in_specs=[pl.BlockSpec(memory_space=pl.ANY)] * (count + 1),
+        out_specs=[pl.BlockSpec(memory_space=pltpu.VMEM)] * count,
+        scratch_shapes=[pltpu.SemaphoreType.DMA((count,))],
+        compiler_params=pltpu.CompilerParams(vmem_limit_bytes=4 * 2**20),
+        cost_estimate=pl.CostEstimate(
+            flops=0,
+            bytes_accessed=sum(source.size * source.dtype.itemsize for source in sources),
+            transcendentals=0,
+        ),
+        name="load",
+    )(after, *[pltpu.with_memory_space_constraint(source, pltpu.HBM) for source in sources])
+
+
+def square_kernel(residual, out):
+    resid_f = residual[...].astype(jnp.float32)
+    out[...] = jnp.broadcast_to(
+        jnp.sum(resid_f * resid_f, axis=1, keepdims=True), out.shape
+    )
+
+
+def project_kernel(pool_count, routes, residual, gain, *rest):
+    squares, rest = rest[:pool_count], rest[pool_count:]
+    weights, outs = rest[:3], rest[3:]
+    listed = outs[0].shape[0]
+    requests = residual.shape[0]
+    rows = pool_count * listed
+    me = lax.axis_index("pool")
+    total = squares[0][...]
+    for part in squares[1:]:
+        total = total + part[...]
+    scale = lax.rsqrt(total[:, :1] / D + EPSILON)
+    resid_f = residual[...].astype(jnp.float32)
+    normed = resid_f * scale * gain[...].astype(jnp.float32)[None, :]
+    row_ids = lax.broadcasted_iota(jnp.int32, (rows, requests), 0)
+    column_ids = lax.broadcasted_iota(jnp.int32, (rows, requests), 1)
+    wanted = jnp.zeros((rows, requests), jnp.int32)
+    for shift in range(pool_count):
+        owner = lax.rem(me + shift, pool_count)
+        for row in range(listed):
+            wanted = jnp.where(
+                row_ids == shift * listed + row, listed_at(routes, owner, row), wanted
+            )
+    pick = (column_ids == wanted).astype(jnp.float32).astype(jnp.bfloat16)
+    picked = jnp.dot(
+        pick, normed.astype(jnp.bfloat16), preferred_element_type=jnp.float32
+    ).astype(jnp.bfloat16)
+    place = 0
+    for source in weights:
+        for first in range(0, source.shape[1], CHUNK):
+            product = jnp.dot(
+                picked, source[:, first : first + CHUNK], preferred_element_type=jnp.float32
+            )
+            for shift in range(pool_count):
+                outs[shift][:, place : place + CHUNK] = product[
+                    shift * listed : (shift + 1) * listed
+                ]
+            place += CHUNK
+
+
+def attend_kernel(
+    pool_count, local_kv, group, routes, context_len, slot_route, slot_block, turn, *rest
+):
+    parts, (keys, values, out) = rest[:pool_count], rest[pool_count : pool_count + 3]
+    turned, flat_query, flat_own, query, score, peak, mass, total = rest[pool_count + 3 :]
+    listed = parts[0].shape[0]
+    heads = local_kv * group
+    slots = keys.shape[0]
+    key_width = local_kv * HD
+    homes = pool_count
+    per_home = listed // homes
+    score_scale = 1.0 / math.sqrt(HD)
+    me = lax.axis_index("pool")
+    for row in range(listed):
+        turned[row : row + 1, :] = turn[pl.ds(listed_at(routes, me, row), 1), :]
+    cosine, sine = turned[:, :HD], turned[:, HD:]
+
+    def column(first):
+        value = parts[0][:, first : first + HD]
+        for part in parts[1:]:
+            value = value + part[:, first : first + HD]
+        return value
+
+    def rotated(first):
+        vector = column(first)
+        vector = vector * cosine + pltpu.roll(vector, HD // 2, 1) * sine
+        return vector.astype(jnp.bfloat16).astype(jnp.float32)
+
+    new_keys = [rotated(k * HD) for k in range(local_kv)]
+    new_values = [
+        column(key_width + k * HD).astype(jnp.bfloat16).astype(jnp.float32)
+        for k in range(local_kv)
+    ]
+    for head in range(heads):
+        vector = rotated(2 * key_width + head * HD)
+        own = jnp.sum(vector * new_keys[head // group], axis=1, keepdims=True) * score_scale
+        flat_query[head * listed : (head + 1) * listed, :] = vector
+        flat_own[head * listed : (head + 1) * listed, :] = jnp.broadcast_to(own, (listed, HD))
+    lanes = lax.broadcasted_iota(jnp.int32, (heads, HD), 1)
+    head_kv = lax.broadcasted_iota(jnp.int32, (heads, HD), 0) // group
+
+    owns, mine = [], []
+    for row in range(listed):
+        home = row // per_home
+        request = listed_at(routes, me, row)
+        taken = jnp.int32(0)
+        for owner in range(pool_count):
+            for place in range(per_home):
+                same = routes[owner, place, home] == request
+                taken = taken | ((owner < me) & same).astype(jnp.int32)
+        vector = flat_query[pl.ds(row, heads, stride=listed), :]
+        query[row] = jnp.concatenate(
+            [jnp.where(head_kv == k, vector, 0.0) for k in range(local_kv)], axis=1
+        ).astype(jnp.bfloat16)
+        own = flat_own[pl.ds(row, heads, stride=listed), :]
+        own = jnp.where(taken == 0, own, NEG_FILL)
+        owns.append(own)
+        mine.append(taken == 0)
+        peak[row] = own
+
+    def slot_of(slot):
+        entry = slot_route[slot]
+        row = jnp.maximum(entry, 0)
+        length = jnp.where(entry >= 0, context_len[listed_at(routes, me, row)], 0)
+        return row, length - slot_block[slot] * BS
+
+    for slot in range(slots):
+        row, limit = slot_of(slot)
+        value = (
+            lax.dot_general(
+                query[row],
+                keys[slot],
+                (((1,), (1,)), ((), ())),
+                preferred_element_type=jnp.float32,
+            )
+            * score_scale
+        )
+        value = jnp.where(lanes < limit, value, NEG_FILL)
+        score[slot] = value
+        peak[row] = jnp.maximum(peak[row], value)
+    for row in range(listed):
+        top = jnp.broadcast_to(jnp.max(peak[row], axis=1, keepdims=True), (heads, HD))
+        peak[row] = top
+        weight = jnp.where(mine[row], jnp.exp(owns[row] - top), 0.0)
+        mass[row] = jnp.where(lanes == 0, weight, 0.0)
+        fresh = jnp.zeros((heads, HD), jnp.float32)
+        for k in range(local_kv):
+            fresh = jnp.where(
+                head_kv == k, jnp.broadcast_to(new_values[k][row : row + 1], (heads, HD)), fresh
+            )
+        total[row] = weight * fresh
+    for slot in range(slots):
+        row, limit = slot_of(slot)
+        expo = jnp.where(lanes < limit, jnp.exp(score[slot] - peak[row]), 0.0)
+        mass[row] += expo
+        wide = jnp.dot(
+            expo.astype(jnp.bfloat16), values[slot], preferred_element_type=jnp.float32
+        )
+        product = wide[:, :HD]
+        for k in range(1, local_kv):
+            product = jnp.where(head_kv == k, wide[:, k * HD : (k + 1) * HD], product)
+        total[row] += product
+    stats = jnp.zeros((heads, HD), jnp.float32)
+    for row in range(listed):
+        row_mass = jnp.sum(mass[row], axis=1, keepdims=True)
+        row_peak = peak[row]
+        out[row] = jnp.where(
+            row_mass > 0.0, total[row] / jnp.where(row_mass > 0.0, row_mass, 1.0), 0.0
+        ).astype(jnp.bfloat16)
+        for first, left in ((0, row_peak), (3, row_mass)):
+            for piece in range(first, first + 3):
+                part = left.astype(jnp.bfloat16).astype(jnp.float32)
+                stats = jnp.where(lanes == piece * listed + row, part, stats)
+                left = left - part
+    out[listed] = stats.astype(jnp.bfloat16)
+
+
+def merge_kernel(pool_count, routes, *rest):
+    parts, (w_out, out) = rest[:pool_count], rest[pool_count : pool_count + 2]
+    best, numerator, denominator, flat = rest[pool_count + 2 :]
+    listed = parts[0].shape[0] - 1
+    requests, heads = best.shape[:2]
+    me = lax.axis_index("pool")
+    best[...] = jnp.full(best.shape, NEG_FILL, jnp.float32)
+    numerator[...] = jnp.zeros_like(numerator)
+    denominator[...] = jnp.zeros_like(denominator)
+    entries = []
+    for shift in range(pool_count):
+        owner = lax.rem(me + pool_count - shift, pool_count)
+        stats = parts[shift][listed].astype(jnp.float32)
+        for row in range(listed):
+            request = listed_at(routes, owner, row)
+            pieces = [
+                stats[:, piece * listed + row : piece * listed + row + 1] for piece in range(6)
+            ]
+            peak = jnp.broadcast_to(pieces[0] + pieces[1] + pieces[2], (heads, HD))
+            mass = jnp.broadcast_to(pieces[3] + pieces[4] + pieces[5], (heads, HD))
+            entries.append((shift, row, request, peak, mass))
+            best[request] = jnp.maximum(best[request], peak)
+    for shift, row, request, peak, mass in entries:
+        weight = jnp.exp(peak - best[request]) * mass
+        numerator[request] += weight * parts[shift][row].astype(jnp.float32)
+        denominator[request] += weight
+    for request in range(requests):
+        flat[request * heads : (request + 1) * heads, :] = (
+            numerator[request] / denominator[request]
+        )
+    attention = jnp.concatenate(
+        [flat[pl.ds(head, requests, stride=heads), :].astype(jnp.bfloat16) for head in range(heads)],
+        axis=1,
+    )
+    for first in range(0, out.shape[1], CHUNK):
+        out[:, first : first + CHUNK] = jnp.dot(
+            attention, w_out[:, first : first + CHUNK], preferred_element_type=jnp.float32
+        )
+
+
+def spread(value, axis):
+    count = lax.axis_size(axis)
+    return [value] + [
+        lax.ppermute(value, axis, [(i, (i + shift) % count) for i in range(count)])
+        for shift in range(1, count)
+    ]
+
+
+def pin(value):
+    return pltpu.with_memory_space_constraint(value, pltpu.VMEM)
+
+
+def close_pool(
+    residual,
+    norm_gain,
+    w_query,
+    w_key,
+    w_value,
+    w_out,
+    k_cache,
+    v_cache,
+    context_len,
+    routes,
+    slot_route,
+    slot_block,
+):
+    pool_count = lax.axis_size("pool")
+    requests, depth = residual.shape
+    query_width, key_width = w_query.shape[1], w_key.shape[1]
+    heads, local_kv = query_width // HD, key_width // HD
+    group = heads // local_kv
+    listed = routes.shape[1] * routes.shape[2]
+    slots = k_cache.shape[0]
+    width = query_width + 2 * key_width
+    routes = routes.transpose(0, 2, 1)
+    in_smem = pl.BlockSpec(memory_space=pltpu.SMEM)
+    in_vmem = pl.BlockSpec(memory_space=pltpu.VMEM)
+    f32 = jnp.float32
+    spell = pl.CostEstimate(flops=0, bytes_accessed=2**25, transcendentals=0)
+
+    squares = pl.pallas_call(
+        square_kernel,
+        out_shape=jax.ShapeDtypeStruct((requests, HD), f32),
+        in_specs=[in_vmem],
+        out_specs=in_vmem,
+        compiler_params=pltpu.CompilerParams(vmem_limit_bytes=4 * 2**20),
+        cost_estimate=spell,
+        name="square",
+    )(residual)
+    near_key, near_value, near_query = load(squares, w_key, w_value, w_query)
+    sent = pl.pallas_call(
+        functools.partial(project_kernel, pool_count),
+        out_shape=[jax.ShapeDtypeStruct((listed, width), f32)] * pool_count,
+        in_specs=[in_smem] + [in_vmem] * (pool_count + 5),
+        out_specs=[in_vmem] * pool_count,
+        compiler_params=pltpu.CompilerParams(vmem_limit_bytes=8 * 2**20),
+        cost_estimate=spell,
+        name="project",
+    )(
+        routes,
+        residual,
+        norm_gain,
+        *spread(squares, "pool"),
+        pin(near_key),
+        pin(near_value),
+        pin(near_query),
+    )
+    received = [sent[0]] + [
+        lax.ppermute(sent[s], "pool", [(i, (i + s) % pool_count) for i in range(pool_count)])
+        for s in range(1, pool_count)
+    ]
+
+    frequencies = THETA ** (-2.0 * jnp.arange(HD // 2, dtype=f32) / HD)
+    angles = context_len.astype(f32)[:, None] * frequencies[None, :]
+    cosine, sine = jnp.cos(angles), jnp.sin(angles)
+    turn = jnp.concatenate([cosine, cosine, -sine, sine], axis=1)
+    near_k, near_v = load(sent[0], k_cache, v_cache)
+    partial = pl.pallas_call(
+        functools.partial(attend_kernel, pool_count, local_kv, group),
+        out_shape=jax.ShapeDtypeStruct((listed + 1, heads, HD), jnp.bfloat16),
+        in_specs=[in_smem] * 4 + [in_vmem] * (pool_count + 3),
+        out_specs=in_vmem,
+        scratch_shapes=[
+            pltpu.VMEM((listed, 2 * HD), f32),
+            pltpu.VMEM((heads * listed, HD), f32),
+            pltpu.VMEM((heads * listed, HD), f32),
+            pltpu.VMEM((listed, heads, key_width), jnp.bfloat16),
+            pltpu.VMEM((slots, heads, HD), f32),
+            pltpu.VMEM((listed, heads, HD), f32),
+            pltpu.VMEM((listed, heads, HD), f32),
+            pltpu.VMEM((listed, heads, HD), f32),
+        ],
+        compiler_params=pltpu.CompilerParams(vmem_limit_bytes=8 * 2**20),
+        cost_estimate=spell,
+        name="attend",
+    )(routes, context_len, slot_route, slot_block, turn, *received, pin(near_k), pin(near_v))
+    partials = spread(partial, "pool")
+    (near_out,) = load(partial, w_out)
+
+    product = pl.pallas_call(
+        functools.partial(merge_kernel, pool_count),
+        out_shape=jax.ShapeDtypeStruct((requests, w_out.shape[1]), f32),
+        in_specs=[in_smem] + [in_vmem] * (pool_count + 1),
+        out_specs=in_vmem,
+        scratch_shapes=[
+            pltpu.VMEM((requests, heads, HD), f32),
+            pltpu.VMEM((requests, heads, HD), f32),
+            pltpu.VMEM((requests, heads, HD), f32),
+            pltpu.VMEM((requests * heads, HD), f32),
+        ],
+        compiler_params=pltpu.CompilerParams(vmem_limit_bytes=8 * 2**20),
+        cost_estimate=spell,
+        name="merge",
+    )(routes, *partials, pin(near_out))
+    tensor_count = lax.axis_size("tensor")
+    distance = 1
+    while distance < tensor_count:
+        product = product + lax.ppermute(
+            product, "tensor", [(i, i ^ distance) for i in range(tensor_count)]
+        )
+        distance *= 2
+    return (residual.astype(f32) + product).astype(jnp.bfloat16)
 
 
 def rotate(vectors, positions):
@@ -41,7 +405,7 @@
     )
 
 
-def per_device(
+def wide_pool(
     residual,
     norm_gain,
     w_query,
@@ -198,6 +562,12 @@
         P(("groups", "pool")),
         P(("groups", "pool")),
     )
+    pool_count, tensor_count = mesh.shape["pool"], mesh.shape["tensor"]
+    close = pool_count <= 4 and tensor_count & (tensor_count - 1) == 0
     return jax.shard_map(
-        per_device, mesh=mesh, in_specs=placed, out_specs=P("groups", "pool"), check_vma=False
-    )
+        close_pool if close else wide_pool,
+        mesh=mesh,
+        in_specs=placed,
+        out_specs=P("groups", "pool"),
+        check_vma=False,
+    )

time: 175 us -> 44.6 us (0.25)
  waiting for transfers between devices: 66.9 us -> 7.47 us
  blocking collectives: 25.3 us -> 0 us
  matrix products: 21.9 us -> 0 us
  Pallas kernels: 0 us -> 17.9 us
  between operations: 14.3 us -> 0.16 us
  other arithmetic: 13.3 us -> 1.54 us
  local copies, waits for them, and re-layouts: 10.9 us -> 0.87 us
  starting transfers between devices: 21.3 us -> 16.5 us
    psum x1 -> x0, waiting for transfers between devices: 30.1 us -> none  [per_device(): head_total = lax.psum(partial_out, 'tensor')]
    unnamed x3 -> x0, waiting for transfers between devices: 24.1 us -> none
    dot_general x11 -> x0, matrix products: 21.9 us -> none  [the longest x1 5.24 us: per_device(): jnp.dot(lax.all_gather(attention, 'pool', axis=0, tiled=True), w_out, pre...]
    all_to_all x5 -> x0, starting transfers between devices: 21.3 us -> none  [the longest x1 6.32 us: per_device(): lax.all_to_all(sent_info, 'pool', split_axis=0, concat_axis=0, tiled=True)]
    pallas_call x0 -> x7, Pallas kernels: none -> 17.9 us  [the longest x3 10.3 us: load(): pl.pallas_call(functools.partial(load_kernel, count), out_shape=[pltpu.VM...]
    ppermute x0 -> x11, starting transfers between devices: none -> 16.5 us  [the longest x6 11.1 us: spread(): lax.ppermute(value, axis, [(i, (i + shift) % count) for i in range(count)])]
    all_gather x1 -> x0, blocking collectives: 13.1 us -> none  [per_device(): lax.all_gather(attention, 'pool', axis=0, tiled=True)]
    all_to_all x5 -> x0, waiting for transfers between devices: 12.7 us -> none  [the longest x1 5.03 us: send_back(): lax.all_to_all(parts[0], 'pool', split_axis=0, concat_axis=0, tiled=True)]
  transfers between devices with their start and end apart: 7 -> 11, of which waited for: 5 -> 4; matrix products, arithmetic and copies ran while one was open for 16% -> 2% of each run, Pallas kernels for 0% -> 23%
where the time goes in v1:
time: 44.6 us; the launch traced here: 44.4 us
  Pallas kernels  17.9 us (40%)
  starting transfers between devices  16.5 us (37%)
  waiting for transfers between devices  7.47 us (17%)
  other arithmetic  1.54 us (3%)
  local copies, waits for them, and re-layouts  0.87 us (2%)
    ppermute x6, starting transfers between devices, spread(): lax.ppermute(value, axis, [(i, (i + shift) % count) for i in range(count)])  11.1 us
    pallas_call x3, Pallas kernels, load(): pl.pallas_call(functools.partial(load_kernel, count), out_shape=[pltpu.VM...  10.3 us
    ppermute x2, waiting for transfers between devices, close_pool(): lax.ppermute(product, 'tensor', [(i, i ^ distance) for i in range(tensor_...  5.41 us
    ppermute x3, starting transfers between devices, close_pool(): lax.ppermute(sent[s], 'pool', [(i, (i + s) % pool_count) for i in range(p...  3.84 us
    pallas_call x1, Pallas kernels, close_pool(): pl.pallas_call(functools.partial(project_kernel, pool_count), out_shape=[...  2.69 us
    pallas_call x1, Pallas kernels, close_pool(): pl.pallas_call(functools.partial(merge_kernel, pool_count), out_shape=jax...  2.39 us
    pallas_call x1, Pallas kernels, close_pool(): pl.pallas_call(functools.partial(attend_kernel, pool_count, local_kv, gro...  2.37 us
    ppermute x3, waiting for transfers between devices, close_pool(): lax.ppermute(sent[s], 'pool', [(i, (i + s) % pool_count) for i in range(p...  2.04 us
  transfers between devices with their start and end apart: 11, of which 4 were waited for; matrix products, arithmetic and copies ran while one was open for 2% of the time, Pallas kernels for 23%

profile of v1, /device:TPU:0, one launch (start us, length us, event | category | flops | bytes accessed | tf_op | source)
XLA Modules:
  0.0 44.4 jit_solution(2067514563301059271)
XLA Ops:
  0.0 0.8 %copy-done = bf16[16,2048]{1,0:T(8,128)(2,1)S(1)} copy-done((bf16[16,2048]{1,0:T(8,128)(2,1)S(1)}, bf16[16,2048]{1,0:T(8,128)(2,1)}, u32[]{:S(2)}) %copy-start) | copy-done | bytes 65560
  0.9 3.0 %collective-permute-start = (f32[16,128]{1,0:T(8,128)S(1)}, f32[16,128]{1,0:T(8,128)S(1)}, u32[]{:S(2)}, u32[]{:S(2)}) collective-permute-start(f32[16,128]{1,0:T(8,128)S(1)} %square.1.rest_0_), channel_id=1, source_target_pairs={{0,4},{4,8},{8,12},{12,0},{1,5},{5,9},{9,13},{13,1},{2,6},{6,10},{... | collective-permute-start | bytes 24584 | tf_op jit(solution)/shard_map/ppermute | solution.py:262
  4.0 2.6 %collective-permute-start.1 = (f32[16,128]{1,0:T(8,128)S(1)}, f32[16,128]{1,0:T(8,128)S(1)}, u32[]{:S(2)}, u32[]{:S(2)}) collective-permute-start(f32[16,128]{1,0:T(8,128)S(1)} %square.1.rest_0_), channel_id=1, source_target_pairs={{0,8},{4,12},{8,0},{12,4},{1,9},{5,13},{9,1},{13,5},{2,10},{6,14},... | collective-permute-start | bytes 24584 | tf_op jit(solution)/shard_map/ppermute | solution.py:262
  6.6 1.3 %collective-permute-start.2 = (f32[16,128]{1,0:T(8,128)S(1)}, f32[16,128]{1,0:T(8,128)S(1)}, u32[]{:S(2)}, u32[]{:S(2)}) collective-permute-start(f32[16,128]{1,0:T(8,128)S(1)} %square.1.rest_0_), channel_id=1, source_target_pairs={{0,12},{4,0},{8,4},{12,8},{1,13},{5,1},{9,5},{13,9},{2,14},{6,2},{... | collective-permute-start | bytes 24584 | tf_op jit(solution)/shard_map/ppermute | solution.py:262
  7.9 0.7 %convert_element_type.10 = f32[16]{0:T(128)S(1)} convert(s32[16]{0:T(128)} %context_len.1) | non-fusion elementwise | flops 16 | bytes 128 | tf_op jit(solution)/shard_map/convert_element_type | solution.py:332
  8.6 0.1 multiply_cosine_fusion
  8.7 4.1 %load.3 = (bf16[2048,256]{1,0:T(8,128)(2,1)S(1)}, bf16[2048,256]{1,0:T(8,128)(2,1)S(1)}, bf16[2048,2048]{1,0:T(8,128)(2,1)S(1)}) custom-call(f32[16,128]{1,0:T(8,128)S(1)} %square.1.rest_0_, bf16[2048,256]{1,0:T(8,128)(2,1)} %rest_1_.3, bf16[2048,256]{1,0:T(8,128)(2,1)} %rest_2_.2, bf16[2048,2048]{1,0:T(8,128)(2,1)} %rest_3_.1), custom_call_target="tpu_custom_call" | custom-call | bytes 10485760 | tf_op jit(solution)/shard_map/load/pallas_call | solution.py:40
  12.9 2.7 %project.1 = (f32[8,2560]{1,0:T(8,128)S(1)}, f32[8,2560]{1,0:T(8,128)S(1)}, f32[8,2560]{1,0:T(8,128)S(1)}, f32[8,2560]{1,0:T(8,128)S(1)}) custom-call(s32[4,2,4]{2,1,0:T(2,128)S(1)} %bitcast.1, bf16[16,2048]{1,0:T(8,128)(2,1)S(1)} %copy-done.1, bf16[2048]{0:T(1024)(128)(2,1)S(1)} %copy-done.3, f32[16,128]{1,0:T(8,128)S(1)} %square.1.rest_0_, ...), custom_call_target="tpu_custom_call" | custom-call | bytes 33554432 | tf_op jit(solution)/shard_map/project/pallas_call | solution.py:309
  15.6 0.7 %collective-permute-start.3 = (f32[8,2560]{1,0:T(8,128)S(1)}, f32[8,2560]{1,0:T(8,128)S(1)}, u32[]{:S(2)}, u32[]{:S(2)}) collective-permute-start(f32[8,2560]{1,0:T(8,128)S(1)} %get-tuple-element.18), channel_id=1, source_target_pairs={{0,4},{4,8},{8,12},{12,0},{1,5},{5,9},{9,13},{13,1},{2,6},{6,10},{... | collective-permute-start | bytes 245768 | tf_op jit(solution)/shard_map/ppermute | solution.py:327
  16.3 0.4 collective-permute-start.4
  16.7 2.7 %collective-permute-start.5 = (f32[8,2560]{1,0:T(8,128)S(1)}, f32[8,2560]{1,0:T(8,128)S(1)}, u32[]{:S(2)}, u32[]{:S(2)}) collective-permute-start(f32[8,2560]{1,0:T(8,128)S(1)} %get-tuple-element.20), channel_id=1, source_target_pairs={{0,12},{4,0},{8,4},{12,8},{1,13},{5,1},{9,5},{13,9},{2,14},{6,2},{... | collective-permute-start | bytes 245768 | tf_op jit(solution)/shard_map/ppermute | solution.py:327
  19.5 2.9 %load.4 = (bf16[48,128,256]{2,1,0:T(8,128)(2,1)S(1)}, bf16[48,128,256]{2,1,0:T(8,128)(2,1)S(1)}) custom-call(f32[8,2560]{1,0:T(8,128)S(1)} %get-tuple-element.17.rest_0_, bf16[48,128,256]{2,1,0:T(8,128)(2,1)} %rest_1_.4, bf16[48,128,256]{2,1,0:T(8,128)(2,1)} %rest_2_.3), custom_call_target="tpu_custom_call" | custom-call | bytes 6291456 | tf_op jit(solution)/shard_map/load/pallas_call | solution.py:40
  22.4 0.2 collective-permute-done.3.rest_1_
  22.5 1.8 %collective-permute-done.4.rest_2_ = f32[8,2560]{1,0:T(8,128)S(1)} collective-permute-done((f32[8,2560]{1,0:T(8,128)S(1)}, f32[8,2560]{1,0:T(8,128)S(1)}, u32[]{:S(2)}, u32[]{:S(2)}) %collective-permute-start.4) | collective-permute-done | bytes 81952 | tf_op jit(solution)/shard_map/ppermute | solution.py:327
  24.4 2.4 %attend.1.rest_0_ = bf16[9,16,128]{2,1,0:T(8,128)(2,1)S(1)} custom-call(s32[4,2,4]{2,1,0:T(2,128)S(1)} %bitcast.2, s32[16]{0:T(128)S(1)} %copy-done.4, s32[48]{0:T(128)S(1)} %copy-done.5, s32[48]{0:T(128)S(1)} %copy-done.6, f32[16,256]{1,0:T(8,128)S(1)} %pad_maximum_fusion.turn, f32[8,2560]{1,0:T(8,128)S(1)} %get-tuple-element.17.rest_0_, ...), custom_call_target="tpu_custom_call" | custom-call | bytes 33554432 | tf_op jit(solution)/shard_map/attend/pallas_call | solution.py:336
  26.8 1.7 %collective-permute-start.6 = (bf16[9,16,128]{2,1,0:T(8,128)(2,1)S(1)}, bf16[9,16,128]{2,1,0:T(8,128)(2,1)S(1)}, u32[]{:S(2)}, u32[]{:S(2)}) collective-permute-start(bf16[9,16,128]{2,1,0:T(8,128)(2,1)S(1)} %attend.1.rest_0_), channel_id=1, source_target_pairs={{0,4},{4,8},{8,12},{12,0},{1,5},{5,9},{9,13},{13,1},{2,6},{6,10},{... | collective-permute-start | bytes 110600 | tf_op jit(solution)/shard_map/ppermute | solution.py:262
  28.5 0.9 %collective-permute-start.7 = (bf16[9,16,128]{2,1,0:T(8,128)(2,1)S(1)}, bf16[9,16,128]{2,1,0:T(8,128)(2,1)S(1)}, u32[]{:S(2)}, u32[]{:S(2)}) collective-permute-start(bf16[9,16,128]{2,1,0:T(8,128)(2,1)S(1)} %attend.1.rest_0_), channel_id=1, source_target_pairs={{0,8},{4,12},{8,0},{12,4},{1,9},{5,13},{9,1},{13,5},{2,10},{6,14},... | collective-permute-start | bytes 110600 | tf_op jit(solution)/shard_map/ppermute | solution.py:262
  29.4 1.5 %collective-permute-start.8 = (bf16[9,16,128]{2,1,0:T(8,128)(2,1)S(1)}, bf16[9,16,128]{2,1,0:T(8,128)(2,1)S(1)}, u32[]{:S(2)}, u32[]{:S(2)}) collective-permute-start(bf16[9,16,128]{2,1,0:T(8,128)(2,1)S(1)} %attend.1.rest_0_), channel_id=1, source_target_pairs={{0,12},{4,0},{8,4},{12,8},{1,13},{5,1},{9,5},{13,9},{2,14},{6,2},{... | collective-permute-start | bytes 110600 | tf_op jit(solution)/shard_map/ppermute | solution.py:262
  30.9 3.4 %load.5.rest_4_ = bf16[2048,2048]{1,0:T(8,128)(2,1)S(1)} custom-call(bf16[9,16,128]{2,1,0:T(8,128)(2,1)S(1)} %attend.1.rest_0_, bf16[2048,2048]{1,0:T(8,128)(2,1)} %rest_1_.5), custom_call_target="tpu_custom_call" | custom-call | bytes 8388608 | tf_op jit(solution)/shard_map/load/pallas_call | solution.py:40
  34.4 2.4 %merge.1 = f32[16,2048]{1,0:T(8,128)S(1)} custom-call(s32[4,2,4]{2,1,0:T(2,128)S(1)} %bitcast.3, bf16[9,16,128]{2,1,0:T(8,128)(2,1)S(1)} %attend.1.rest_0_, bf16[9,16,128]{2,1,0:T(8,128)(2,1)S(1)} %collective-permute-done.6.rest_1_, bf16[9,16,128]{2,1,0:T(8,128)(2,1)S(1)} %collective-permute-done.7.rest_2_, ...), custom_call_target="tpu_custom_call" | custom-call | bytes 33554432 | tf_op jit(solution)/shard_map/merge/pallas_call | solution.py:358
  36.8 1.4 %collective-permute-done.9 = f32[16,2048]{1,0:T(8,128)S(1)} collective-permute-done((f32[16,2048]{1,0:T(8,128)S(1)}, f32[16,2048]{1,0:T(8,128)S(1)}, u32[]{:S(2)}, u32[]{:S(2)}) %collective-permute-start.9) | collective-permute-done | bytes 131104 | tf_op jit(solution)/shard_map/ppermute | solution.py:376
  38.1 1.6 %collective-permute-start.10 = (f32[16,2048]{1,0:T(8,128)S(1)}, f32[16,2048]{1,0:T(8,128)S(1)}, u32[]{:S(2)}, u32[]{:S(2)}) collective-permute-start(f32[16,2048]{1,0:T(8,128)S(1)} %add.9), channel_id=1, source_target_pairs={{0,2},{1,3},{2,0},{3,1},{4,6},{5,7},{6,4},{7,5},{8,10},{9,11},{10,... | collective-permute-start | bytes 393224 | tf_op jit(solution)/shard_map/ppermute | solution.py:376
  39.7 4.1 %collective-permute-done.10 = f32[16,2048]{1,0:T(8,128)S(1)} collective-permute-done((f32[16,2048]{1,0:T(8,128)S(1)}, f32[16,2048]{1,0:T(8,128)S(1)}, u32[]{:S(2)}, u32[]{:S(2)}) %collective-permute-start.10) | collective-permute-done | bytes 131104 | tf_op jit(solution)/shard_map/ppermute | solution.py:376
  43.7 0.7 %add_convert_fusion = bf16[16,2048]{1,0:T(8,128)(2,1)} fusion(f32[16,2048]{1,0:T(8,128)S(1)} %add.9, f32[16,2048]{1,0:T(8,128)S(1)} %collective-permute-done.10, bf16[16,2048]{1,0:T(8,128)(2,1)S(1)} %copy-done.1), kind=kLoop, calls=%fused_computation | loop fusion | flops 131072 | bytes 393216 | tf_op jit(solution)/shard_map/convert_element_type | solution.py:380
  (25 shorter events, 0.2 us)
Async XLA Ops:
  0.0 0.8 %copy-start = (bf16[16,2048]{1,0:T(8,128)(2,1)S(1)}, bf16[16,2048]{1,0:T(8,128)(2,1)}, u32[]{:S(2)}) copy-start(bf16[16,2048]{1,0:T(8,128)(2,1)} %residual.3) | copy-start | bytes 196612
  0.8 12.0 %copy-start.1 = (bf16[16,2048]{1,0:T(8,128)(2,1)S(1)}, bf16[16,2048]{1,0:T(8,128)(2,1)}, u32[]{:S(2)}) copy-start(bf16[16,2048]{1,0:T(8,128)(2,1)} %residual.3) | copy-start | bytes 196612
  0.8 12.0 %copy-start.2 = (s32[4,4,2]{1,2,0:T(2,128)S(1)}, s32[4,4,2]{1,2,0:T(2,128)}, u32[]{:S(2)}) copy-start(s32[4,4,2]{1,2,0:T(2,128)} %param.21) | copy-start | bytes 388
  0.8 12.0 %copy-start.3 = (bf16[2048]{0:T(1024)(128)(2,1)S(1)}, bf16[2048]{0:T(1024)(128)(2,1)}, u32[]{:S(2)}) copy-start(bf16[2048]{0:T(1024)(128)(2,1)} %gain.1) | copy-start | bytes 12292
  0.9 11.8 %collective-permute-start = (f32[16,128]{1,0:T(8,128)S(1)}, f32[16,128]{1,0:T(8,128)S(1)}, u32[]{:S(2)}, u32[]{:S(2)}) collective-permute-start(f32[16,128]{1,0:T(8,128)S(1)} %square.1.rest_0_), channel_id=1, source_target_pairs={{0,4},{4,8},{8,12},{12,0},{1,5},{5,9},{9,13},{13,1},{2,6},{6,10},{... | collective-permute-start | bytes 24584 | tf_op jit(solution)/shard_map/ppermute | solution.py:262
  4.0 8.8 %collective-permute-start.1 = (f32[16,128]{1,0:T(8,128)S(1)}, f32[16,128]{1,0:T(8,128)S(1)}, u32[]{:S(2)}, u32[]{:S(2)}) collective-permute-start(f32[16,128]{1,0:T(8,128)S(1)} %square.1.rest_0_), channel_id=1, source_target_pairs={{0,8},{4,12},{8,0},{12,4},{1,9},{5,13},{9,1},{13,5},{2,10},{6,14},... | collective-permute-start | bytes 24584 | tf_op jit(solution)/shard_map/ppermute | solution.py:262
  6.6 6.2 %collective-permute-start.2 = (f32[16,128]{1,0:T(8,128)S(1)}, f32[16,128]{1,0:T(8,128)S(1)}, u32[]{:S(2)}, u32[]{:S(2)}) collective-permute-start(f32[16,128]{1,0:T(8,128)S(1)} %square.1.rest_0_), channel_id=1, source_target_pairs={{0,12},{4,0},{8,4},{12,8},{1,13},{5,1},{9,5},{13,9},{2,14},{6,2},{... | collective-permute-start | bytes 24584 | tf_op jit(solution)/shard_map/ppermute | solution.py:262
  12.8 11.6 %copy-start.4 = (s32[16]{0:T(128)S(1)}, s32[16]{0:T(128)}, u32[]{:S(2)}) copy-start(s32[16]{0:T(128)} %context_len.1) | copy-start | bytes 196
  12.8 11.5 %copy-start.5 = (s32[48]{0:T(128)S(1)}, s32[48]{0:T(128)}, u32[]{:S(2)}) copy-start(s32[48]{0:T(128)} %slot_route.1) | copy-start | bytes 580
  12.9 11.5 %copy-start.6 = (s32[48]{0:T(128)S(1)}, s32[48]{0:T(128)}, u32[]{:S(2)}) copy-start(s32[48]{0:T(128)} %slot_block.1) | copy-start | bytes 580
  15.6 7.0 %collective-permute-start.3 = (f32[8,2560]{1,0:T(8,128)S(1)}, f32[8,2560]{1,0:T(8,128)S(1)}, u32[]{:S(2)}, u32[]{:S(2)}) collective-permute-start(f32[8,2560]{1,0:T(8,128)S(1)} %get-tuple-element.18), channel_id=1, source_target_pairs={{0,4},{4,8},{8,12},{12,0},{1,5},{5,9},{9,13},{13,1},{2,6},{6,10},{... | collective-permute-start | bytes 245768 | tf_op jit(solution)/shard_map/ppermute | solution.py:327
  16.3 8.1 %collective-permute-start.4 = (f32[8,2560]{1,0:T(8,128)S(1)}, f32[8,2560]{1,0:T(8,128)S(1)}, u32[]{:S(2)}, u32[]{:S(2)}) collective-permute-start(f32[8,2560]{1,0:T(8,128)S(1)} %get-tuple-element.19), channel_id=1, source_target_pairs={{0,8},{4,12},{8,0},{12,4},{1,9},{5,13},{9,1},{13,5},{2,10},{6,14},... | collective-permute-start | bytes 245768 | tf_op jit(solution)/shard_map/ppermute | solution.py:327
  16.7 7.7 %collective-permute-start.5 = (f32[8,2560]{1,0:T(8,128)S(1)}, f32[8,2560]{1,0:T(8,128)S(1)}, u32[]{:S(2)}, u32[]{:S(2)}) collective-permute-start(f32[8,2560]{1,0:T(8,128)S(1)} %get-tuple-element.20), channel_id=1, source_target_pairs={{0,12},{4,0},{8,4},{12,8},{1,13},{5,1},{9,5},{13,9},{2,14},{6,2},{... | collective-permute-start | bytes 245768 | tf_op jit(solution)/shard_map/ppermute | solution.py:327
  26.8 7.5 %collective-permute-start.6 = (bf16[9,16,128]{2,1,0:T(8,128)(2,1)S(1)}, bf16[9,16,128]{2,1,0:T(8,128)(2,1)S(1)}, u32[]{:S(2)}, u32[]{:S(2)}) collective-permute-start(bf16[9,16,128]{2,1,0:T(8,128)(2,1)S(1)} %attend.1.rest_0_), channel_id=1, source_target_pairs={{0,4},{4,8},{8,12},{12,0},{1,5},{5,9},{9,13},{13,1},{2,6},{6,10},{... | collective-permute-start | bytes 110600 | tf_op jit(solution)/shard_map/ppermute | solution.py:262
  28.5 5.9 %collective-permute-start.7 = (bf16[9,16,128]{2,1,0:T(8,128)(2,1)S(1)}, bf16[9,16,128]{2,1,0:T(8,128)(2,1)S(1)}, u32[]{:S(2)}, u32[]{:S(2)}) collective-permute-start(bf16[9,16,128]{2,1,0:T(8,128)(2,1)S(1)} %attend.1.rest_0_), channel_id=1, source_target_pairs={{0,8},{4,12},{8,0},{12,4},{1,9},{5,13},{9,1},{13,5},{2,10},{6,14},... | collective-permute-start | bytes 110600 | tf_op jit(solution)/shard_map/ppermute | solution.py:262
  29.4 4.9 %collective-permute-start.8 = (bf16[9,16,128]{2,1,0:T(8,128)(2,1)S(1)}, bf16[9,16,128]{2,1,0:T(8,128)(2,1)S(1)}, u32[]{:S(2)}, u32[]{:S(2)}) collective-permute-start(bf16[9,16,128]{2,1,0:T(8,128)(2,1)S(1)} %attend.1.rest_0_), channel_id=1, source_target_pairs={{0,12},{4,0},{8,4},{12,8},{1,13},{5,1},{9,5},{13,9},{2,14},{6,2},{... | collective-permute-start | bytes 110600 | tf_op jit(solution)/shard_map/ppermute | solution.py:262
  36.7 1.4 %collective-permute-start.9 = (f32[16,2048]{1,0:T(8,128)S(1)}, f32[16,2048]{1,0:T(8,128)S(1)}, u32[]{:S(2)}, u32[]{:S(2)}) collective-permute-start(f32[16,2048]{1,0:T(8,128)S(1)} %merge.1), channel_id=1, source_target_pairs={{0,1},{1,0},{2,3},{3,2},{4,5},{5,4},{6,7},{7,6},{8,9},{9,8},{10,11... | collective-permute-start | bytes 393224 | tf_op jit(solution)/shard_map/ppermute | solution.py:376
  38.1 5.6 %collective-permute-start.10 = (f32[16,2048]{1,0:T(8,128)S(1)}, f32[16,2048]{1,0:T(8,128)S(1)}, u32[]{:S(2)}, u32[]{:S(2)}) collective-permute-start(f32[16,2048]{1,0:T(8,128)S(1)} %add.9), channel_id=1, source_target_pairs={{0,2},{1,3},{2,0},{3,1},{4,6},{5,7},{6,4},{7,5},{8,10},{9,11},{10,... | collective-permute-start | bytes 393224 | tf_op jit(solution)/shard_map/ppermute | solution.py:376

commit v2 on v1

--- a/solution.py
+++ b/solution.py
@@ -17,6 +17,7 @@
 NEG_FILL = -1e30
 EXACT = lax.Precision.HIGHEST
 CHUNK = 256
+GROW = 128.0
 
 
 def listed_at(routes, owner, row):
@@ -26,31 +27,43 @@
 
 def load_kernel(count, *rest):
     sources, outs, sems = rest[1 : 1 + count], rest[1 + count : -1], rest[-1]
-    copies = [
-        pltpu.make_async_copy(sources[i], outs[i], sems.at[i]) for i in range(count)
-    ]
+    copies = []
+    for source, out, place in zip(sources, outs, range(count)):
+        copies.append(pltpu.make_async_copy(leading(source, out), out, sems.at[place]))
     for copy in copies:
         copy.start()
     for copy in copies:
         copy.wait()
 
 
+def start_first(copies):
+    @pl.when(lax.axis_index("pool") >= 0)
+    def _():
+        for copy in copies:
+            copy.start()
+
+
+def leading(source, out):
+    return source.at[pl.ds(0, out.shape[0])]
+
+
 def load(after, *sources):
     count = len(sources)
+    shapes = [(rows,) + source.shape[1:] for source, rows in sources]
     return pl.pallas_call(
         functools.partial(load_kernel, count),
-        out_shape=[pltpu.VMEM(source.shape, source.dtype) for source in sources],
+        out_shape=[pltpu.VMEM(shape, jnp.bfloat16) for shape in shapes],
         in_specs=[pl.BlockSpec(memory_space=pl.ANY)] * (count + 1),
         out_specs=[pl.BlockSpec(memory_space=pltpu.VMEM)] * count,
         scratch_shapes=[pltpu.SemaphoreType.DMA((count,))],
         compiler_params=pltpu.CompilerParams(vmem_limit_bytes=4 * 2**20),
         cost_estimate=pl.CostEstimate(
             flops=0,
-            bytes_accessed=sum(source.size * source.dtype.itemsize for source in sources),
+            bytes_accessed=sum(2 * math.prod(shape) for shape in shapes),
             transcendentals=0,
         ),
         name="load",
-    )(after, *[pltpu.with_memory_space_constraint(source, pltpu.HBM) for source in sources])
+    )(after, *[in_hbm(source) for source, _ in sources])
 
 
 def square_kernel(residual, out):
@@ -62,7 +75,13 @@
 
 def project_kernel(pool_count, routes, residual, gain, *rest):
     squares, rest = rest[:pool_count], rest[pool_count:]
-    weights, outs = rest[:3], rest[3:]
+    weights, source, outs, (late, sems) = rest[:3], rest[3], rest[4:-2], rest[-2:]
+    early = weights[-1].shape[0]
+    copies = []
+    for place in range(late.shape[0]):
+        depths = pl.ds(early + place * CHUNK, CHUNK)
+        copies.append(pltpu.make_async_copy(source.at[depths], late.at[place], sems.at[place]))
+    start_first(copies)
     listed = outs[0].shape[0]
     requests = residual.shape[0]
     rows = pool_count * listed
@@ -87,16 +106,32 @@
         pick, normed.astype(jnp.bfloat16), preferred_element_type=jnp.float32
     ).astype(jnp.bfloat16)
     place = 0
-    for source in weights:
-        for first in range(0, source.shape[1], CHUNK):
+    for weight in weights:
+        for first in range(0, weight.shape[1], CHUNK):
             product = jnp.dot(
-                picked, source[:, first : first + CHUNK], preferred_element_type=jnp.float32
+                picked[:, : weight.shape[0]],
+                weight[:, first : first + CHUNK],
+                preferred_element_type=jnp.float32,
             )
             for shift in range(pool_count):
-                outs[shift][:, place : place + CHUNK] = product[
+                outs[shift][:, place + first : place + first + CHUNK] = product[
                     shift * listed : (shift + 1) * listed
                 ]
-            place += CHUNK
+        place += weight.shape[1]
+    place -= weights[-1].shape[1]
+    for block, copy in enumerate(copies):
+        depths = slice(early + block * CHUNK, early + (block + 1) * CHUNK)
+        copy.wait()
+        for first in range(0, late.shape[2], CHUNK):
+            product = jnp.dot(
+                picked[:, depths],
+                late[block, :, first : first + CHUNK],
+                preferred_element_type=jnp.float32,
+            )
+            for shift in range(pool_count):
+                outs[shift][:, place + first : place + first + CHUNK] += product[
+                    shift * listed : (shift + 1) * listed
+                ]
 
 
 def attend_kernel(
@@ -117,10 +152,10 @@
     cosine, sine = turned[:, :HD], turned[:, HD:]
 
     def column(first):
-        value = parts[0][:, first : first + HD]
-        for part in parts[1:]:
+        value = parts[1][:, first : first + HD]
+        for part in parts[2:]:
             value = value + part[:, first : first + HD]
-        return value
+        return parts[0][:, first : first + HD] + value * (1.0 / GROW)
 
     def rotated(first):
         vector = column(first)
@@ -256,12 +291,13 @@
         )
 
 
-def spread(value, axis):
+def shifted(value, axis, shift):
     count = lax.axis_size(axis)
-    return [value] + [
-        lax.ppermute(value, axis, [(i, (i + shift) % count) for i in range(count)])
-        for shift in range(1, count)
-    ]
+    return lax.ppermute(value, axis, [(i, (i + shift) % count) for i in range(count)])
+
+
+def in_hbm(value):
+    return pltpu.with_memory_space_constraint(value, pltpu.HBM)
 
 
 def pin(value):
@@ -293,6 +329,7 @@
     routes = routes.transpose(0, 2, 1)
     in_smem = pl.BlockSpec(memory_space=pltpu.SMEM)
     in_vmem = pl.BlockSpec(memory_space=pltpu.VMEM)
+    in_any = pl.BlockSpec(memory_space=pl.ANY)
     f32 = jnp.float32
     spell = pl.CostEstimate(flops=0, bytes_accessed=2**25, transcendentals=0)
 
@@ -305,34 +342,44 @@
         cost_estimate=spell,
         name="square",
     )(residual)
-    near_key, near_value, near_query = load(squares, w_key, w_value, w_query)
+    early = depth * 5 // 8 // CHUNK * CHUNK
+    late = (depth - early) // CHUNK
+    near_key, near_value, near_query = load(
+        squares, (w_key, depth), (w_value, depth), (w_query, early)
+    )
     sent = pl.pallas_call(
         functools.partial(project_kernel, pool_count),
         out_shape=[jax.ShapeDtypeStruct((listed, width), f32)] * pool_count,
-        in_specs=[in_smem] + [in_vmem] * (pool_count + 5),
+        in_specs=[in_smem] + [in_vmem] * (pool_count + 5) + [in_any],
         out_specs=[in_vmem] * pool_count,
-        compiler_params=pltpu.CompilerParams(vmem_limit_bytes=8 * 2**20),
+        scratch_shapes=[
+            pltpu.VMEM((late, CHUNK, query_width), jnp.bfloat16),
+            pltpu.SemaphoreType.DMA((late,)),
+        ],
+        compiler_params=pltpu.CompilerParams(vmem_limit_bytes=12 * 2**20),
         cost_estimate=spell,
         name="project",
     )(
         routes,
         residual,
         norm_gain,
-        *spread(squares, "pool"),
+        squares,
+        *[shifted(squares, "pool", shift) for shift in range(1, pool_count)],
         pin(near_key),
         pin(near_value),
         pin(near_query),
+        in_hbm(w_query),
     )
     received = [sent[0]] + [
-        lax.ppermute(sent[s], "pool", [(i, (i + s) % pool_count) for i in range(pool_count)])
-        for s in range(1, pool_count)
+        shifted((sent[shift] * GROW).astype(jnp.float16), "pool", shift).astype(f32)
+        for shift in range(1, pool_count)
     ]
-
     frequencies = THETA ** (-2.0 * jnp.arange(HD // 2, dtype=f32) / HD)
-    angles = context_len.astype(f32)[:, None] * frequencies[None, :]
+    late_len, _ = lax.optimization_barrier((context_len, sent[0]))
+    angles = late_len.astype(f32)[:, None] * frequencies[None, :]
     cosine, sine = jnp.cos(angles), jnp.sin(angles)
     turn = jnp.concatenate([cosine, cosine, -sine, sine], axis=1)
-    near_k, near_v = load(sent[0], k_cache, v_cache)
+    near_k, near_v = load(sent[0], (k_cache, slots), (v_cache, slots))
     partial = pl.pallas_call(
         functools.partial(attend_kernel, pool_count, local_kv, group),
         out_shape=jax.ShapeDtypeStruct((listed + 1, heads, HD), jnp.bfloat16),
@@ -352,8 +399,8 @@
         cost_estimate=spell,
         name="attend",
     )(routes, context_len, slot_route, slot_block, turn, *received, pin(near_k), pin(near_v))
-    partials = spread(partial, "pool")
-    (near_out,) = load(partial, w_out)
+    partials = [partial] + [shifted(partial, "pool", shift) for shift in range(1, pool_count)]
+    near_out = w_out
 
     product = pl.pallas_call(
         functools.partial(merge_kernel, pool_count),
@@ -373,9 +420,13 @@
     tensor_count = lax.axis_size("tensor")
     distance = 1
     while distance < tensor_count:
-        product = product + lax.ppermute(
+        last_step = 2 * distance == tensor_count
+        if last_step:
+            product = product.astype(jnp.bfloat16)
+        other = lax.ppermute(
             product, "tensor", [(i, i ^ distance) for i in range(tensor_count)]
         )
+        product = product.astype(f32) + other.astype(f32)
         distance *= 2
     return (residual.astype(f32) + product).astype(jnp.bfloat16)
 

time: 44.6 us -> 40.2 us (0.901)
  Pallas kernels: 17.9 us -> 14.2 us
  waiting for transfers between devices: 7.47 us -> 6.37 us
  starting transfers between devices: 16.5 us -> 17.5 us
  other arithmetic: 1.54 us -> 0.94 us
    pallas_call x3 -> x2, Pallas kernels: 10.3 us -> 6.18 us  [load(): pl.pallas_call(functools.partial(load_kernel, count), out_shape=[pltpu.VM...]
    ppermute x2, waiting for transfers between devices: 5.41 us -> 4.13 us  [close_pool(): lax.ppermute(product, 'tensor', [(i, i ^ distance) for i in range(tensor_...]
    ppermute x9, starting transfers between devices: 14.9 us -> 15.9 us  [shifted(): lax.ppermute(value, axis, [(i, (i + shift) % count) for i in range(count)])]
    convert_element_type x1 -> x8, other arithmetic: 0.66 us -> 0.08 us  [the longest x3 0.03 us: close_pool(): (sent[shift] * GROW).astype(jnp.float16)]
  transfers between devices with their start and end apart: 11 -> 11, of which waited for: 4 -> 5; matrix products, arithmetic and copies ran while one was open for 2% -> 1% of each run, Pallas kernels for 23% -> 15%
where the time goes in v2:
time: 40.2 us; the launch traced here: 40 us
  starting transfers between devices  17.5 us (44%)
  Pallas kernels  14.2 us (35%)
  waiting for transfers between devices  6.37 us (16%)
  other arithmetic  0.94 us (2%)
  local copies, waits for them, and re-layouts  0.88 us (2%)
    ppermute x9, starting transfers between devices, shifted(): lax.ppermute(value, axis, [(i, (i + shift) % count) for i in range(count)])  15.9 us
    pallas_call x2, Pallas kernels, load(): pl.pallas_call(functools.partial(load_kernel, count), out_shape=[pltpu.VM...  6.18 us
    ppermute x2, waiting for transfers between devices, close_pool(): lax.ppermute(product, 'tensor', [(i, i ^ distance) for i in range(tensor_...  4.13 us
    pallas_call x1, Pallas kernels, close_pool(): pl.pallas_call(functools.partial(project_kernel, pool_count), out_shape=[...  3.07 us
    pallas_call x1, Pallas kernels, close_pool(): pl.pallas_call(functools.partial(attend_kernel, pool_count, local_kv, gro...  2.43 us
    pallas_call x1, Pallas kernels, close_pool(): pl.pallas_call(functools.partial(merge_kernel, pool_count), out_shape=jax...  2.38 us
    ppermute x9, waiting for transfers between devices, shifted(): lax.ppermute(value, axis, [(i, (i + shift) % count) for i in range(count)])  2.24 us
    ppermute x2, starting transfers between devices, close_pool(): lax.ppermute(product, 'tensor', [(i, i ^ distance) for i in range(tensor_...  1.56 us
  transfers between devices with their start and end apart: 11, of which 5 were waited for; matrix products, arithmetic and copies ran while one was open for 1% of the time, Pallas kernels for 15%

profile of v2, /device:TPU:0, one launch (start us, length us, event | category | flops | bytes accessed | tf_op | source)
XLA Modules:
  0.0 40.0 jit_solution(13727743711760118295)
XLA Ops:
  0.0 0.8 %copy-done = bf16[16,2048]{1,0:T(8,128)(2,1)S(1)} copy-done((bf16[16,2048]{1,0:T(8,128)(2,1)S(1)}, bf16[16,2048]{1,0:T(8,128)(2,1)}, u32[]{:S(2)}) %copy-start) | copy-done | bytes 65560
  0.8 0.1 square.1.rest_0_
  0.9 3.0 %collective-permute-start = (f32[16,128]{1,0:T(8,128)S(1)}, f32[16,128]{1,0:T(8,128)S(1)}, u32[]{:S(2)}, u32[]{:S(2)}) collective-permute-start(f32[16,128]{1,0:T(8,128)S(1)} %square.1.rest_0_), channel_id=1, source_target_pairs={{0,4},{4,8},{8,12},{12,0},{1,5},{5,9},{9,13},{13,1},{2,6},{6,10},{... | collective-permute-start | bytes 24584 | tf_op jit(solution)/shard_map/ppermute | solution.py:296
  4.0 2.6 %collective-permute-start.1 = (f32[16,128]{1,0:T(8,128)S(1)}, f32[16,128]{1,0:T(8,128)S(1)}, u32[]{:S(2)}, u32[]{:S(2)}) collective-permute-start(f32[16,128]{1,0:T(8,128)S(1)} %square.1.rest_0_), channel_id=1, source_target_pairs={{0,8},{4,12},{8,0},{12,4},{1,9},{5,13},{9,1},{13,5},{2,10},{6,14},... | collective-permute-start | bytes 24584 | tf_op jit(solution)/shard_map/ppermute | solution.py:296
  6.6 1.3 %collective-permute-start.2 = (f32[16,128]{1,0:T(8,128)S(1)}, f32[16,128]{1,0:T(8,128)S(1)}, u32[]{:S(2)}, u32[]{:S(2)}) collective-permute-start(f32[16,128]{1,0:T(8,128)S(1)} %square.1.rest_0_), channel_id=1, source_target_pairs={{0,12},{4,0},{8,4},{12,8},{1,13},{5,1},{9,5},{13,9},{2,14},{6,2},{... | collective-permute-start | bytes 24584 | tf_op jit(solution)/shard_map/ppermute | solution.py:296
  7.9 3.3 %load.2 = (bf16[2048,256]{1,0:T(8,128)(2,1)S(1)}, bf16[2048,256]{1,0:T(8,128)(2,1)S(1)}, bf16[1280,2048]{1,0:T(8,128)(2,1)S(1)}) custom-call(f32[16,128]{1,0:T(8,128)S(1)} %square.1.rest_0_, bf16[2048,256]{1,0:T(8,128)(2,1)} %rest_1_.2, bf16[2048,256]{1,0:T(8,128)(2,1)} %rest_2_.2, bf16[2048,2048]{1,0:T(8,128)(2,1)} %rest_7_.1), custom_call_target="tpu_custom_call" | custom-call | bytes 7340032 | tf_op jit(solution)/shard_map/load/pallas_call | solution.py:53
  11.3 3.1 %project.1 = (f32[8,2560]{1,0:T(8,128)S(1)}, f32[8,2560]{1,0:T(8,128)S(1)}, f32[8,2560]{1,0:T(8,128)S(1)}, f32[8,2560]{1,0:T(8,128)S(1)}) custom-call(s32[4,2,4]{2,1,0:T(2,128)S(1)} %bitcast.3, bf16[16,2048]{1,0:T(8,128)(2,1)S(1)} %copy-done.1, bf16[2048]{0:T(1024)(128)(2,1)S(1)} %copy-done.3, f32[16,128]{1,0:T(8,128)S(1)} %square.1.rest_0_, ...), custom_call_target="tpu_custom_call" | custom-call | bytes 33554432 | tf_op jit(solution)/shard_map/project/pallas_call | solution.py:350
  14.5 0.7 %collective-permute-start.3 = (f16[8,2560]{1,0:T(8,128)(2,1)S(1)}, f16[8,2560]{1,0:T(8,128)(2,1)S(1)}, u32[]{:S(2)}, u32[]{:S(2)}) collective-permute-start(f16[8,2560]{1,0:T(8,128)(2,1)S(1)} %multiply_convert_fusion.2), channel_id=1, source_target_pairs={{0,4},{4,8},{8,12},{12,0},{1,5},{5,9},{9,13},{13,1},{2,6},{6,10},{... | collective-permute-start | bytes 122888 | tf_op jit(solution)/shard_map/ppermute | solution.py:296
  15.2 2.1 %collective-permute-start.4 = (f16[8,2560]{1,0:T(8,128)(2,1)S(1)}, f16[8,2560]{1,0:T(8,128)(2,1)S(1)}, u32[]{:S(2)}, u32[]{:S(2)}) collective-permute-start(f16[8,2560]{1,0:T(8,128)(2,1)S(1)} %multiply_convert_fusion.1), channel_id=1, source_target_pairs={{0,8},{4,12},{8,0},{12,4},{1,9},{5,13},{9,1},{13,5},{2,10},{6,14},... | collective-permute-start | bytes 122888 | tf_op jit(solution)/shard_map/ppermute | solution.py:296
  17.3 1.2 %collective-permute-start.5 = (f16[8,2560]{1,0:T(8,128)(2,1)S(1)}, f16[8,2560]{1,0:T(8,128)(2,1)S(1)}, u32[]{:S(2)}, u32[]{:S(2)}) collective-permute-start(f16[8,2560]{1,0:T(8,128)(2,1)S(1)} %multiply_convert_fusion), channel_id=1, source_target_pairs={{0,12},{4,0},{8,4},{12,8},{1,13},{5,1},{9,5},{13,9},{2,14},{6,2},{... | collective-permute-start | bytes 122888 | tf_op jit(solution)/shard_map/ppermute | solution.py:296
  18.5 0.1 multiply_cosine_fusion
  18.7 2.9 %load.3 = (bf16[48,128,256]{2,1,0:T(8,128)(2,1)S(1)}, bf16[48,128,256]{2,1,0:T(8,128)(2,1)S(1)}) custom-call(f32[8,2560]{1,0:T(8,128)S(1)} %get-tuple-element.18.rest_0_, bf16[48,128,256]{2,1,0:T(8,128)(2,1)} %rest_1_.3, bf16[48,128,256]{2,1,0:T(8,128)(2,1)} %rest_2_.3), custom_call_target="tpu_custom_call" | custom-call | bytes 6291456 | tf_op jit(solution)/shard_map/load/pallas_call | solution.py:53
  21.7 2.4 %attend.1.rest_0_ = bf16[9,16,128]{2,1,0:T(8,128)(2,1)S(1)} custom-call(s32[4,2,4]{2,1,0:T(2,128)S(1)} %bitcast.4, s32[16]{0:T(128)S(1)} %copy-done.4, s32[48]{0:T(128)S(1)} %copy-done.5, s32[48]{0:T(128)S(1)} %copy-done.6, f32[16,256]{1,0:T(8,128)S(1)} %pad_maximum_fusion.turn, f32[8,2560]{1,0:T(8,128)S(1)} %get-tuple-element.18.rest_0_, ...), custom_call_target="tpu_custom_call" | custom-call | bytes 33554432 | tf_op jit(solution)/shard_map/attend/pallas_call | solution.py:383
  24.1 1.4 %collective-permute-start.6 = (bf16[9,16,128]{2,1,0:T(8,128)(2,1)S(1)}, bf16[9,16,128]{2,1,0:T(8,128)(2,1)S(1)}, u32[]{:S(2)}, u32[]{:S(2)}) collective-permute-start(bf16[9,16,128]{2,1,0:T(8,128)(2,1)S(1)} %attend.1.rest_0_), channel_id=1, source_target_pairs={{0,4},{4,8},{8,12},{12,0},{1,5},{5,9},{9,13},{13,1},{2,6},{6,10},{... | collective-permute-start | bytes 110600 | tf_op jit(solution)/shard_map/ppermute | solution.py:296
  25.5 1.8 %collective-permute-start.7 = (bf16[9,16,128]{2,1,0:T(8,128)(2,1)S(1)}, bf16[9,16,128]{2,1,0:T(8,128)(2,1)S(1)}, u32[]{:S(2)}, u32[]{:S(2)}) collective-permute-start(bf16[9,16,128]{2,1,0:T(8,128)(2,1)S(1)} %attend.1.rest_0_), channel_id=1, source_target_pairs={{0,8},{4,12},{8,0},{12,4},{1,9},{5,13},{9,1},{13,5},{2,10},{6,14},... | collective-permute-start | bytes 110600 | tf_op jit(solution)/shard_map/ppermute | solution.py:296
  27.3 1.7 %collective-permute-start.8 = (bf16[9,16,128]{2,1,0:T(8,128)(2,1)S(1)}, bf16[9,16,128]{2,1,0:T(8,128)(2,1)S(1)}, u32[]{:S(2)}, u32[]{:S(2)}) collective-permute-start(bf16[9,16,128]{2,1,0:T(8,128)(2,1)S(1)} %attend.1.rest_0_), channel_id=1, source_target_pairs={{0,12},{4,0},{8,4},{12,8},{1,13},{5,1},{9,5},{13,9},{2,14},{6,2},{... | collective-permute-start | bytes 110600 | tf_op jit(solution)/shard_map/ppermute | solution.py:296
  29.1 0.9 %collective-permute-done.6.rest_1_ = bf16[9,16,128]{2,1,0:T(8,128)(2,1)S(1)} collective-permute-done((bf16[9,16,128]{2,1,0:T(8,128)(2,1)S(1)}, bf16[9,16,128]{2,1,0:T(8,128)(2,1)S(1)}, u32[]{:S(2)}, u32[]{:S(2)}) %collective-permute-start.6) | collective-permute-done | bytes 36896 | tf_op jit(solution)/shard_map/ppermute | solution.py:296
  29.9 0.4 %collective-permute-done.7.rest_2_ = bf16[9,16,128]{2,1,0:T(8,128)(2,1)S(1)} collective-permute-done((bf16[9,16,128]{2,1,0:T(8,128)(2,1)S(1)}, bf16[9,16,128]{2,1,0:T(8,128)(2,1)S(1)}, u32[]{:S(2)}, u32[]{:S(2)}) %collective-permute-start.7) | collective-permute-done | bytes 36896 | tf_op jit(solution)/shard_map/ppermute | solution.py:296
  30.4 0.9 %collective-permute-done.8.rest_3_ = bf16[9,16,128]{2,1,0:T(8,128)(2,1)S(1)} collective-permute-done((bf16[9,16,128]{2,1,0:T(8,128)(2,1)S(1)}, bf16[9,16,128]{2,1,0:T(8,128)(2,1)S(1)}, u32[]{:S(2)}, u32[]{:S(2)}) %collective-permute-start.8) | collective-permute-done | bytes 36896 | tf_op jit(solution)/shard_map/ppermute | solution.py:296
  31.3 2.4 %merge.1 = f32[16,2048]{1,0:T(8,128)S(1)} custom-call(s32[4,2,4]{2,1,0:T(2,128)S(1)} %bitcast.5, bf16[9,16,128]{2,1,0:T(8,128)(2,1)S(1)} %attend.1.rest_0_, bf16[9,16,128]{2,1,0:T(8,128)(2,1)S(1)} %collective-permute-done.6.rest_1_, bf16[9,16,128]{2,1,0:T(8,128)(2,1)S(1)} %collective-permute-done.7.rest_2_, ...), custom_call_target="tpu_custom_call" | custom-call | bytes 33554432 | tf_op jit(solution)/shard_map/merge/pallas_call | solution.py:405
  33.7 1.4 %collective-permute-done.9 = f32[16,2048]{1,0:T(8,128)S(1)} collective-permute-done((f32[16,2048]{1,0:T(8,128)S(1)}, f32[16,2048]{1,0:T(8,128)S(1)}, u32[]{:S(2)}, u32[]{:S(2)}) %collective-permute-start.9) | collective-permute-done | bytes 131104 | tf_op jit(solution)/shard_map/ppermute | solution.py:426
  35.0 1.6 %collective-permute-start.10 = (bf16[16,2048]{1,0:T(8,128)(2,1)S(1)}, bf16[16,2048]{1,0:T(8,128)(2,1)S(1)}, u32[]{:S(2)}, u32[]{:S(2)}) collective-permute-start(bf16[16,2048]{1,0:T(8,128)(2,1)S(1)} %add_convert_fusion.1), channel_id=1, source_target_pairs={{0,2},{1,3},{2,0},{3,1},{4,6},{5,7},{6,4},{7,5},{8,10},{9,11},{10,... | collective-permute-start | bytes 196616 | tf_op jit(solution)/shard_map/ppermute | solution.py:426
  36.6 2.8 %collective-permute-done.10 = bf16[16,2048]{1,0:T(8,128)(2,1)S(1)} collective-permute-done((bf16[16,2048]{1,0:T(8,128)(2,1)S(1)}, bf16[16,2048]{1,0:T(8,128)(2,1)S(1)}, u32[]{:S(2)}, u32[]{:S(2)}) %collective-permute-start.10) | collective-permute-done | bytes 65568 | tf_op jit(solution)/shard_map/ppermute | solution.py:426
  39.4 0.7 %add_convert_fusion = bf16[16,2048]{1,0:T(8,128)(2,1)} fusion(bf16[16,2048]{1,0:T(8,128)(2,1)S(1)} %collective-permute-done.10, bf16[16,2048]{1,0:T(8,128)(2,1)S(1)} %add_convert_fusion.1, bf16[16,2048]{1,0:T(8,128)(2,1)S(1)} %copy-done.1), kind=kLoop, calls=%fused_computation | loop fusion | flops 196608 | bytes 262144 | tf_op jit(solution)/shard_map/convert_element_type | solution.py:431
  (35 shorter events, 0.2 us)
Async XLA Ops:
  0.0 0.8 %copy-start = (bf16[16,2048]{1,0:T(8,128)(2,1)S(1)}, bf16[16,2048]{1,0:T(8,128)(2,1)}, u32[]{:S(2)}) copy-start(bf16[16,2048]{1,0:T(8,128)(2,1)} %residual.3) | copy-start | bytes 196612
  0.9 10.3 %collective-permute-start = (f32[16,128]{1,0:T(8,128)S(1)}, f32[16,128]{1,0:T(8,128)S(1)}, u32[]{:S(2)}, u32[]{:S(2)}) collective-permute-start(f32[16,128]{1,0:T(8,128)S(1)} %square.1.rest_0_), channel_id=1, source_target_pairs={{0,4},{4,8},{8,12},{12,0},{1,5},{5,9},{9,13},{13,1},{2,6},{6,10},{... | collective-permute-start | bytes 24584 | tf_op jit(solution)/shard_map/ppermute | solution.py:296
  4.0 7.3 %collective-permute-start.1 = (f32[16,128]{1,0:T(8,128)S(1)}, f32[16,128]{1,0:T(8,128)S(1)}, u32[]{:S(2)}, u32[]{:S(2)}) collective-permute-start(f32[16,128]{1,0:T(8,128)S(1)} %square.1.rest_0_), channel_id=1, source_target_pairs={{0,8},{4,12},{8,0},{12,4},{1,9},{5,13},{9,1},{13,5},{2,10},{6,14},... | collective-permute-start | bytes 24584 | tf_op jit(solution)/shard_map/ppermute | solution.py:296
  6.6 4.7 %collective-permute-start.2 = (f32[16,128]{1,0:T(8,128)S(1)}, f32[16,128]{1,0:T(8,128)S(1)}, u32[]{:S(2)}, u32[]{:S(2)}) collective-permute-start(f32[16,128]{1,0:T(8,128)S(1)} %square.1.rest_0_), channel_id=1, source_target_pairs={{0,12},{4,0},{8,4},{12,8},{1,13},{5,1},{9,5},{13,9},{2,14},{6,2},{... | collective-permute-start | bytes 24584 | tf_op jit(solution)/shard_map/ppermute | solution.py:296
  7.9 3.4 %copy-start.1 = (bf16[16,2048]{1,0:T(8,128)(2,1)S(1)}, bf16[16,2048]{1,0:T(8,128)(2,1)}, u32[]{:S(2)}) copy-start(bf16[16,2048]{1,0:T(8,128)(2,1)} %residual.3) | copy-start | bytes 196612
  7.9 3.4 %copy-start.2 = (s32[4,4,2]{1,2,0:T(2,128)S(1)}, s32[4,4,2]{1,2,0:T(2,128)}, u32[]{:S(2)}) copy-start(s32[4,4,2]{1,2,0:T(2,128)} %param.21) | copy-start | bytes 388
  7.9 3.4 %copy-start.3 = (bf16[2048]{0:T(1024)(128)(2,1)S(1)}, bf16[2048]{0:T(1024)(128)(2,1)}, u32[]{:S(2)}) copy-start(bf16[2048]{0:T(1024)(128)(2,1)} %gain.1) | copy-start | bytes 12292
  7.9 23.3 %slice-start = ((s8[8388608]{0:T(1024)(128)(4,1)}), s8[4194304]{0:T(1024)(128)(4,1)S(1)}, s32[]{:S(2)}) async-start(s8[8388608]{0:T(1024)(128)(4,1)} %bitcast.1), calls=%async_computation | async-start | bytes 8388608
  11.3 3.1 %copy-start.4 = (s32[16]{0:T(128)S(1)}, s32[16]{0:T(128)}, u32[]{:S(2)}) copy-start(s32[16]{0:T(128)} %context_len.1) | copy-start | bytes 196
  11.3 20.0 %slice-start.1 = ((s8[8388608]{0:T(1024)(128)(4,1)}), s8[4194304]{0:T(1024)(128)(4,1)S(1)}, s32[]{:S(2)}) async-start(s8[8388608]{0:T(1024)(128)(4,1)} %bitcast.1), calls=%async_computation.1 | async-start | bytes 8388608
  14.5 7.1 %collective-permute-start.3 = (f16[8,2560]{1,0:T(8,128)(2,1)S(1)}, f16[8,2560]{1,0:T(8,128)(2,1)S(1)}, u32[]{:S(2)}, u32[]{:S(2)}) collective-permute-start(f16[8,2560]{1,0:T(8,128)(2,1)S(1)} %multiply_convert_fusion.2), channel_id=1, source_target_pairs={{0,4},{4,8},{8,12},{12,0},{1,5},{5,9},{9,13},{13,1},{2,6},{6,10},{... | collective-permute-start | bytes 122888 | tf_op jit(solution)/shard_map/ppermute | solution.py:296
  15.2 6.4 %collective-permute-start.4 = (f16[8,2560]{1,0:T(8,128)(2,1)S(1)}, f16[8,2560]{1,0:T(8,128)(2,1)S(1)}, u32[]{:S(2)}, u32[]{:S(2)}) collective-permute-start(f16[8,2560]{1,0:T(8,128)(2,1)S(1)} %multiply_convert_fusion.1), channel_id=1, source_target_pairs={{0,8},{4,12},{8,0},{12,4},{1,9},{5,13},{9,1},{13,5},{2,10},{6,14},... | collective-permute-start | bytes 122888 | tf_op jit(solution)/shard_map/ppermute | solution.py:296
  17.3 4.4 %collective-permute-start.5 = (f16[8,2560]{1,0:T(8,128)(2,1)S(1)}, f16[8,2560]{1,0:T(8,128)(2,1)S(1)}, u32[]{:S(2)}, u32[]{:S(2)}) collective-permute-start(f16[8,2560]{1,0:T(8,128)(2,1)S(1)} %multiply_convert_fusion), channel_id=1, source_target_pairs={{0,12},{4,0},{8,4},{12,8},{1,13},{5,1},{9,5},{13,9},{2,14},{6,2},{... | collective-permute-start | bytes 122888 | tf_op jit(solution)/shard_map/ppermute | solution.py:296
  18.7 3.0 %copy-start.5 = (s32[48]{0:T(128)S(1)}, s32[48]{0:T(128)}, u32[]{:S(2)}) copy-start(s32[48]{0:T(128)} %slot_route.1) | copy-start | bytes 580
  18.7 3.0 %copy-start.6 = (s32[48]{0:T(128)S(1)}, s32[48]{0:T(128)}, u32[]{:S(2)}) copy-start(s32[48]{0:T(128)} %slot_block.1) | copy-start | bytes 580
  24.1 5.8 %collective-permute-start.6 = (bf16[9,16,128]{2,1,0:T(8,128)(2,1)S(1)}, bf16[9,16,128]{2,1,0:T(8,128)(2,1)S(1)}, u32[]{:S(2)}, u32[]{:S(2)}) collective-permute-start(bf16[9,16,128]{2,1,0:T(8,128)(2,1)S(1)} %attend.1.rest_0_), channel_id=1, source_target_pairs={{0,4},{4,8},{8,12},{12,0},{1,5},{5,9},{9,13},{13,1},{2,6},{6,10},{... | collective-permute-start | bytes 110600 | tf_op jit(solution)/shard_map/ppermute | solution.py:296
  25.5 4.9 %collective-permute-start.7 = (bf16[9,16,128]{2,1,0:T(8,128)(2,1)S(1)}, bf16[9,16,128]{2,1,0:T(8,128)(2,1)S(1)}, u32[]{:S(2)}, u32[]{:S(2)}) collective-permute-start(bf16[9,16,128]{2,1,0:T(8,128)(2,1)S(1)} %attend.1.rest_0_), channel_id=1, source_target_pairs={{0,8},{4,12},{8,0},{12,4},{1,9},{5,13},{9,1},{13,5},{2,10},{6,14},... | collective-permute-start | bytes 110600 | tf_op jit(solution)/shard_map/ppermute | solution.py:296
  27.3 4.0 %collective-permute-start.8 = (bf16[9,16,128]{2,1,0:T(8,128)(2,1)S(1)}, bf16[9,16,128]{2,1,0:T(8,128)(2,1)S(1)}, u32[]{:S(2)}, u32[]{:S(2)}) collective-permute-start(bf16[9,16,128]{2,1,0:T(8,128)(2,1)S(1)} %attend.1.rest_0_), channel_id=1, source_target_pairs={{0,12},{4,0},{8,4},{12,8},{1,13},{5,1},{9,5},{13,9},{2,14},{6,2},{... | collective-permute-start | bytes 110600 | tf_op jit(solution)/shard_map/ppermute | solution.py:296
  33.7 1.4 %collective-permute-start.9 = (f32[16,2048]{1,0:T(8,128)S(1)}, f32[16,2048]{1,0:T(8,128)S(1)}, u32[]{:S(2)}, u32[]{:S(2)}) collective-permute-start(f32[16,2048]{1,0:T(8,128)S(1)} %merge.1), channel_id=1, source_target_pairs={{0,1},{1,0},{2,3},{3,2},{4,5},{5,4},{6,7},{7,6},{8,9},{9,8},{10,11... | collective-permute-start | bytes 393224 | tf_op jit(solution)/shard_map/ppermute | solution.py:426
  35.0 4.3 %collective-permute-start.10 = (bf16[16,2048]{1,0:T(8,128)(2,1)S(1)}, bf16[16,2048]{1,0:T(8,128)(2,1)S(1)}, u32[]{:S(2)}, u32[]{:S(2)}) collective-permute-start(bf16[16,2048]{1,0:T(8,128)(2,1)S(1)} %add_convert_fusion.1), channel_id=1, source_target_pairs={{0,2},{1,3},{2,0},{3,1},{4,6},{5,7},{6,4},{7,5},{8,10},{9,11},{10,... | collective-permute-start | bytes 196616 | tf_op jit(solution)/shard_map/ppermute | solution.py:426

commit v3 on v1

--- a/solution.py
+++ b/solution.py
@@ -17,40 +17,12 @@
 NEG_FILL = -1e30
 EXACT = lax.Precision.HIGHEST
 CHUNK = 256
+GROW = 128.0
 
 
 def listed_at(routes, owner, row):
     per_home = routes.shape[1]
     return routes[owner, row % per_home, row // per_home]
-
-
-def load_kernel(count, *rest):
-    sources, outs, sems = rest[1 : 1 + count], rest[1 + count : -1], rest[-1]
-    copies = [
-        pltpu.make_async_copy(sources[i], outs[i], sems.at[i]) for i in range(count)
-    ]
-    for copy in copies:
-        copy.start()
-    for copy in copies:
-        copy.wait()
-
-
-def load(after, *sources):
-    count = len(sources)
-    return pl.pallas_call(
-        functools.partial(load_kernel, count),
-        out_shape=[pltpu.VMEM(source.shape, source.dtype) for source in sources],
-        in_specs=[pl.BlockSpec(memory_space=pl.ANY)] * (count + 1),
-        out_specs=[pl.BlockSpec(memory_space=pltpu.VMEM)] * count,
-        scratch_shapes=[pltpu.SemaphoreType.DMA((count,))],
-        compiler_params=pltpu.CompilerParams(vmem_limit_bytes=4 * 2**20),
-        cost_estimate=pl.CostEstimate(
-            flops=0,
-            bytes_accessed=sum(source.size * source.dtype.itemsize for source in sources),
-            transcendentals=0,
-        ),
-        name="load",
-    )(after, *[pltpu.with_memory_space_constraint(source, pltpu.HBM) for source in sources])
 
 
 def square_kernel(residual, out):
@@ -117,10 +89,10 @@
     cosine, sine = turned[:, :HD], turned[:, HD:]
 
     def column(first):
-        value = parts[0][:, first : first + HD]
-        for part in parts[1:]:
+        value = parts[1][:, first : first + HD]
+        for part in parts[2:]:
             value = value + part[:, first : first + HD]
-        return value
+        return parts[0][:, first : first + HD] + value * (1.0 / GROW)
 
     def rotated(first):
         vector = column(first)
@@ -226,9 +198,9 @@
     numerator[...] = jnp.zeros_like(numerator)
     denominator[...] = jnp.zeros_like(denominator)
     entries = []
-    for shift in range(pool_count):
+    for place, shift in enumerate([0, *shifts(pool_count)]):
         owner = lax.rem(me + pool_count - shift, pool_count)
-        stats = parts[shift][listed].astype(jnp.float32)
+        stats = parts[place][listed].astype(jnp.float32)
         for row in range(listed):
             request = listed_at(routes, owner, row)
             pieces = [
@@ -236,11 +208,11 @@
             ]
             peak = jnp.broadcast_to(pieces[0] + pieces[1] + pieces[2], (heads, HD))
             mass = jnp.broadcast_to(pieces[3] + pieces[4] + pieces[5], (heads, HD))
-            entries.append((shift, row, request, peak, mass))
+            entries.append((place, row, request, peak, mass))
             best[request] = jnp.maximum(best[request], peak)
-    for shift, row, request, peak, mass in entries:
+    for place, row, request, peak, mass in entries:
         weight = jnp.exp(peak - best[request]) * mass
-        numerator[request] += weight * parts[shift][row].astype(jnp.float32)
+        numerator[request] += weight * parts[place][row].astype(jnp.float32)
         denominator[request] += weight
     for request in range(requests):
         flat[request * heads : (request + 1) * heads, :] = (
@@ -256,12 +228,13 @@
         )
 
 
-def spread(value, axis):
+def shifts(pool_count):
+    return range(pool_count - 1, 0, -1)
+
+
+def shifted(value, axis, shift):
     count = lax.axis_size(axis)
-    return [value] + [
-        lax.ppermute(value, axis, [(i, (i + shift) % count) for i in range(count)])
-        for shift in range(1, count)
-    ]
+    return lax.ppermute(value, axis, [(i, (i + shift) % count) for i in range(count)])
 
 
 def pin(value):
@@ -294,7 +267,7 @@
     in_smem = pl.BlockSpec(memory_space=pltpu.SMEM)
     in_vmem = pl.BlockSpec(memory_space=pltpu.VMEM)
     f32 = jnp.float32
-    spell = pl.CostEstimate(flops=0, bytes_accessed=2**25, transcendentals=0)
+    spell = pl.CostEstimate(flops=2**34, bytes_accessed=2**25, transcendentals=0)
 
     squares = pl.pallas_call(
         square_kernel,
@@ -305,7 +278,6 @@
         cost_estimate=spell,
         name="square",
     )(residual)
-    near_key, near_value, near_query = load(squares, w_key, w_value, w_query)
     sent = pl.pallas_call(
         functools.partial(project_kernel, pool_count),
         out_shape=[jax.ShapeDtypeStruct((listed, width), f32)] * pool_count,
@@ -318,21 +290,21 @@
         routes,
         residual,
         norm_gain,
-        *spread(squares, "pool"),
-        pin(near_key),
-        pin(near_value),
-        pin(near_query),
+        squares,
+        *[shifted(squares, "pool", shift) for shift in shifts(pool_count)],
+        pin(w_key),
+        pin(w_value),
+        pin(w_query),
     )
     received = [sent[0]] + [
-        lax.ppermute(sent[s], "pool", [(i, (i + s) % pool_count) for i in range(pool_count)])
-        for s in range(1, pool_count)
+        shifted((sent[shift] * GROW).astype(jnp.float16), "pool", shift).astype(f32)
+        for shift in shifts(pool_count)
     ]
-
     frequencies = THETA ** (-2.0 * jnp.arange(HD // 2, dtype=f32) / HD)
-    angles = context_len.astype(f32)[:, None] * frequencies[None, :]
+    late_len, _ = lax.optimization_barrier((context_len, sent[0]))
+    angles = late_len.astype(f32)[:, None] * frequencies[None, :]
     cosine, sine = jnp.cos(angles), jnp.sin(angles)
     turn = jnp.concatenate([cosine, cosine, -sine, sine], axis=1)
-    near_k, near_v = load(sent[0], k_cache, v_cache)
     partial = pl.pallas_call(
         functools.partial(attend_kernel, pool_count, local_kv, group),
         out_shape=jax.ShapeDtypeStruct((listed + 1, heads, HD), jnp.bfloat16),
@@ -351,9 +323,8 @@
         compiler_params=pltpu.CompilerParams(vmem_limit_bytes=8 * 2**20),
         cost_estimate=spell,
         name="attend",
-    )(routes, context_len, slot_route, slot_block, turn, *received, pin(near_k), pin(near_v))
-    partials = spread(partial, "pool")
-    (near_out,) = load(partial, w_out)
+    )(routes, context_len, slot_route, slot_block, turn, *received, pin(k_cache), pin(v_cache))
+    partials = [partial] + [shifted(partial, "pool", shift) for shift in shifts(pool_count)]
 
     product = pl.pallas_call(
         functools.partial(merge_kernel, pool_count),
@@ -369,13 +340,17 @@
         compiler_params=pltpu.CompilerParams(vmem_limit_bytes=8 * 2**20),
         cost_estimate=spell,
         name="merge",
-    )(routes, *partials, pin(near_out))
+    )(routes, *partials, pin(w_out))
     tensor_count = lax.axis_size("tensor")
     distance = 1
     while distance < tensor_count:
-        product = product + lax.ppermute(
+        last_step = 2 * distance == tensor_count
+        if last_step:
+            product = product.astype(jnp.bfloat16)
+        other = lax.ppermute(
             product, "tensor", [(i, i ^ distance) for i in range(tensor_count)]
         )
+        product = product.astype(f32) + other.astype(f32)
         distance *= 2
     return (residual.astype(f32) + product).astype(jnp.bfloat16)
 

time: 44.6 us -> 39.1 us (0.88)
  Pallas kernels: 17.9 us -> 7.56 us
  waiting for transfers between devices: 7.47 us -> 13 us
  other arithmetic: 1.54 us -> 0.94 us
    pallas_call x3 -> x0, Pallas kernels: 10.3 us -> none  [load(): pl.pallas_call(functools.partial(load_kernel, count), out_shape=[pltpu.VM...]
    ppermute x9, waiting for transfers between devices: 2.06 us -> 8.91 us  [shifted(): lax.ppermute(value, axis, [(i, (i + shift) % count) for i in range(count)])]
    ppermute x2, waiting for transfers between devices: 5.41 us -> 4.13 us  [close_pool(): lax.ppermute(product, 'tensor', [(i, i ^ distance) for i in range(tensor_...]
    convert_element_type x1 -> x8, other arithmetic: 0.66 us -> 0.08 us  [the longest x3 0.04 us: close_pool(): (sent[shift] * GROW).astype(jnp.float16)]
    unnamed x14 -> x28, local copies, waits for them, and re-layouts: 0.87 us -> 0.91 us
  transfers between devices with their start and end apart: 11 -> 11, of which waited for: 4 -> 10; matrix products, arithmetic and copies ran while one was open for 2% -> 1% of each run, Pallas kernels for 23% -> 0%
where the time goes in v3:
time: 39.1 us; the launch traced here: 39 us
  starting transfers between devices  16.3 us (42%)
  waiting for transfers between devices  13 us (33%)
  Pallas kernels  7.56 us (19%)
  other arithmetic  0.94 us (2%)
  local copies, waits for them, and re-layouts  0.91 us (2%)
    ppermute x9, starting transfers between devices, shifted(): lax.ppermute(value, axis, [(i, (i + shift) % count) for i in range(count)])  14.7 us
    ppermute x9, waiting for transfers between devices, shifted(): lax.ppermute(value, axis, [(i, (i + shift) % count) for i in range(count)])  8.91 us
    ppermute x2, waiting for transfers between devices, close_pool(): lax.ppermute(product, 'tensor', [(i, i ^ distance) for i in range(tensor_...  4.13 us
    pallas_call x1, Pallas kernels, close_pool(): pl.pallas_call(functools.partial(project_kernel, pool_count), out_shape=[...  2.7 us
    pallas_call x1, Pallas kernels, close_pool(): pl.pallas_call(functools.partial(merge_kernel, pool_count), out_shape=jax...  2.39 us
    pallas_call x1, Pallas kernels, close_pool(): pl.pallas_call(functools.partial(attend_kernel, pool_count, local_kv, gro...  2.37 us
    ppermute x2, starting transfers between devices, close_pool(): lax.ppermute(product, 'tensor', [(i, i ^ distance) for i in range(tensor_...  1.56 us
    unnamed x28, local copies, waits for them, and re-layouts  0.91 us
  transfers between devices with their start and end apart: 11, of which 10 were waited for; matrix products, arithmetic and copies ran while one was open for 1% of the time, Pallas kernels for 0%

profile of v3, /device:TPU:0, one launch (start us, length us, event | category | flops | bytes accessed | tf_op | source)
XLA Modules:
  0.0 39.0 jit_solution(11465298514805174129)
XLA Ops:
  0.0 0.8 %copy-done = bf16[16,2048]{1,0:T(8,128)(2,1)S(1)} copy-done((bf16[16,2048]{1,0:T(8,128)(2,1)S(1)}, bf16[16,2048]{1,0:T(8,128)(2,1)}, u32[]{:S(2)}) %copy-start) | copy-done | bytes 65560
  1.0 3.0 %collective-permute-start.2 = (f32[16,128]{1,0:T(8,128)S(1)}, f32[16,128]{1,0:T(8,128)S(1)}, u32[]{:S(2)}, u32[]{:S(2)}) collective-permute-start(f32[16,128]{1,0:T(8,128)S(1)} %square.1.rest_0_), channel_id=1, source_target_pairs={{0,4},{4,8},{8,12},{12,0},{1,5},{5,9},{9,13},{13,1},{2,6},{6,10},{... | collective-permute-start | bytes 24584 | tf_op jit(solution)/shard_map/ppermute | solution.py:237
  4.0 2.6 %collective-permute-start.1 = (f32[16,128]{1,0:T(8,128)S(1)}, f32[16,128]{1,0:T(8,128)S(1)}, u32[]{:S(2)}, u32[]{:S(2)}) collective-permute-start(f32[16,128]{1,0:T(8,128)S(1)} %square.1.rest_0_), channel_id=1, source_target_pairs={{0,8},{4,12},{8,0},{12,4},{1,9},{5,13},{9,1},{13,5},{2,10},{6,14},... | collective-permute-start | bytes 24584 | tf_op jit(solution)/shard_map/ppermute | solution.py:237
  6.6 1.3 %collective-permute-start = (f32[16,128]{1,0:T(8,128)S(1)}, f32[16,128]{1,0:T(8,128)S(1)}, u32[]{:S(2)}, u32[]{:S(2)}) collective-permute-start(f32[16,128]{1,0:T(8,128)S(1)} %square.1.rest_0_), channel_id=1, source_target_pairs={{0,12},{4,0},{8,4},{12,8},{1,13},{5,1},{9,5},{13,9},{2,14},{6,2},{... | collective-permute-start | bytes 24584 | tf_op jit(solution)/shard_map/ppermute | solution.py:237
  7.9 0.7 %collective-permute-done.1.rest_2_ = f32[16,128]{1,0:T(8,128)S(1)} collective-permute-done((f32[16,128]{1,0:T(8,128)S(1)}, f32[16,128]{1,0:T(8,128)S(1)}, u32[]{:S(2)}, u32[]{:S(2)}) %collective-permute-start.1) | collective-permute-done | bytes 8224 | tf_op jit(solution)/shard_map/ppermute | solution.py:237
  8.6 1.6 %collective-permute-done.rest_1_ = f32[16,128]{1,0:T(8,128)S(1)} collective-permute-done((f32[16,128]{1,0:T(8,128)S(1)}, f32[16,128]{1,0:T(8,128)S(1)}, u32[]{:S(2)}, u32[]{:S(2)}) %collective-permute-start) | collective-permute-done | bytes 8224 | tf_op jit(solution)/shard_map/ppermute | solution.py:237
  10.3 2.7 %project.1 = (f32[8,2560]{1,0:T(8,128)S(1)}, f32[8,2560]{1,0:T(8,128)S(1)}, f32[8,2560]{1,0:T(8,128)S(1)}, f32[8,2560]{1,0:T(8,128)S(1)}) custom-call(s32[4,2,4]{2,1,0:T(2,128)S(1)} %bitcast.3, bf16[16,2048]{1,0:T(8,128)(2,1)S(1)} %copy-done.1, bf16[2048]{0:T(1024)(128)(2,1)S(1)} %copy-done.7, f32[16,128]{1,0:T(8,128)S(1)} %square.1.rest_0_, ...), custom_call_target="tpu_custom_call" | custom-call | flops 17179869184 | bytes 33554432 | tf_op jit(solution)/shard_map/project/pallas_call | solution.py:281
  13.3 3.6 %collective-permute-start.4 = (f16[8,2560]{1,0:T(8,128)(2,1)S(1)}, f16[8,2560]{1,0:T(8,128)(2,1)S(1)}, u32[]{:S(2)}, u32[]{:S(2)}) collective-permute-start(f16[8,2560]{1,0:T(8,128)(2,1)S(1)} %multiply_convert_fusion.1), channel_id=1, source_target_pairs={{0,8},{4,12},{8,0},{12,4},{1,9},{5,13},{9,1},{13,5},{2,10},{6,14},... | collective-permute-start | bytes 122888 | tf_op jit(solution)/shard_map/ppermute | solution.py:237
  16.9 0.1 collective-permute-start.3
  17.2 1.9 %collective-permute-done.5 = f16[8,2560]{1,0:T(8,128)(2,1)S(1)} collective-permute-done((f16[8,2560]{1,0:T(8,128)(2,1)S(1)}, f16[8,2560]{1,0:T(8,128)(2,1)S(1)}, u32[]{:S(2)}, u32[]{:S(2)}) %collective-permute-start.5) | collective-permute-done | bytes 40992 | tf_op jit(solution)/shard_map/ppermute | solution.py:237
  19.1 0.7 %collective-permute-done.4 = f16[8,2560]{1,0:T(8,128)(2,1)S(1)} collective-permute-done((f16[8,2560]{1,0:T(8,128)(2,1)S(1)}, f16[8,2560]{1,0:T(8,128)(2,1)S(1)}, u32[]{:S(2)}, u32[]{:S(2)}) %collective-permute-start.4) | collective-permute-done | bytes 40992 | tf_op jit(solution)/shard_map/ppermute | solution.py:237
  19.8 1.1 %collective-permute-done.3 = f16[8,2560]{1,0:T(8,128)(2,1)S(1)} collective-permute-done((f16[8,2560]{1,0:T(8,128)(2,1)S(1)}, f16[8,2560]{1,0:T(8,128)(2,1)S(1)}, u32[]{:S(2)}, u32[]{:S(2)}) %collective-permute-start.3) | collective-permute-done | bytes 40992 | tf_op jit(solution)/shard_map/ppermute | solution.py:237
  21.0 2.4 %attend.1.rest_0_ = bf16[9,16,128]{2,1,0:T(8,128)(2,1)S(1)} custom-call(s32[4,2,4]{2,1,0:T(2,128)S(1)} %bitcast.4, s32[16]{0:T(128)S(1)} %copy-done.9, s32[48]{0:T(128)S(1)} %copy-done.10, s32[48]{0:T(128)S(1)} %copy-done.11, f32[16,256]{1,0:T(8,128)S(1)} %pad_maximum_fusion.turn, f32[8,2560]{1,0:T(8,128)S(1)} %get-tuple-element.10.rest_0_, ...), custom_call_target="tpu_custom_call" | custom-call | flops 17179869184 | bytes 33554432 | tf_op jit(solution)/shard_map/attend/pallas_call | solution.py:308
  23.3 0.7 %collective-permute-start.8 = (bf16[9,16,128]{2,1,0:T(8,128)(2,1)S(1)}, bf16[9,16,128]{2,1,0:T(8,128)(2,1)S(1)}, u32[]{:S(2)}, u32[]{:S(2)}) collective-permute-start(bf16[9,16,128]{2,1,0:T(8,128)(2,1)S(1)} %attend.1.rest_0_), channel_id=1, source_target_pairs={{0,4},{4,8},{8,12},{12,0},{1,5},{5,9},{9,13},{13,1},{2,6},{6,10},{... | collective-permute-start | bytes 110600 | tf_op jit(solution)/shard_map/ppermute | solution.py:237
  24.1 2.2 %collective-permute-start.7 = (bf16[9,16,128]{2,1,0:T(8,128)(2,1)S(1)}, bf16[9,16,128]{2,1,0:T(8,128)(2,1)S(1)}, u32[]{:S(2)}, u32[]{:S(2)}) collective-permute-start(bf16[9,16,128]{2,1,0:T(8,128)(2,1)S(1)} %attend.1.rest_0_), channel_id=1, source_target_pairs={{0,8},{4,12},{8,0},{12,4},{1,9},{5,13},{9,1},{13,5},{2,10},{6,14},... | collective-permute-start | bytes 110600 | tf_op jit(solution)/shard_map/ppermute | solution.py:237
  26.2 1.0 %collective-permute-start.6 = (bf16[9,16,128]{2,1,0:T(8,128)(2,1)S(1)}, bf16[9,16,128]{2,1,0:T(8,128)(2,1)S(1)}, u32[]{:S(2)}, u32[]{:S(2)}) collective-permute-start(bf16[9,16,128]{2,1,0:T(8,128)(2,1)S(1)} %attend.1.rest_0_), channel_id=1, source_target_pairs={{0,12},{4,0},{8,4},{12,8},{1,13},{5,1},{9,5},{13,9},{2,14},{6,2},{... | collective-permute-start | bytes 110600 | tf_op jit(solution)/shard_map/ppermute | solution.py:237
  27.2 2.0 %collective-permute-done.8.rest_3_ = bf16[9,16,128]{2,1,0:T(8,128)(2,1)S(1)} collective-permute-done((bf16[9,16,128]{2,1,0:T(8,128)(2,1)S(1)}, bf16[9,16,128]{2,1,0:T(8,128)(2,1)S(1)}, u32[]{:S(2)}, u32[]{:S(2)}) %collective-permute-start.8) | collective-permute-done | bytes 36896 | tf_op jit(solution)/shard_map/ppermute | solution.py:237
  29.2 0.5 %collective-permute-done.7.rest_2_ = bf16[9,16,128]{2,1,0:T(8,128)(2,1)S(1)} collective-permute-done((bf16[9,16,128]{2,1,0:T(8,128)(2,1)S(1)}, bf16[9,16,128]{2,1,0:T(8,128)(2,1)S(1)}, u32[]{:S(2)}, u32[]{:S(2)}) %collective-permute-start.7) | collective-permute-done | bytes 36896 | tf_op jit(solution)/shard_map/ppermute | solution.py:237
  29.7 0.5 %collective-permute-done.6.rest_1_ = bf16[9,16,128]{2,1,0:T(8,128)(2,1)S(1)} collective-permute-done((bf16[9,16,128]{2,1,0:T(8,128)(2,1)S(1)}, bf16[9,16,128]{2,1,0:T(8,128)(2,1)S(1)}, u32[]{:S(2)}, u32[]{:S(2)}) %collective-permute-start.6) | collective-permute-done | bytes 36896 | tf_op jit(solution)/shard_map/ppermute | solution.py:237
  30.2 2.4 %merge.1 = f32[16,2048]{1,0:T(8,128)S(1)} custom-call(s32[4,2,4]{2,1,0:T(2,128)S(1)} %bitcast.5, bf16[9,16,128]{2,1,0:T(8,128)(2,1)S(1)} %attend.1.rest_0_, bf16[9,16,128]{2,1,0:T(8,128)(2,1)S(1)} %collective-permute-done.6.rest_1_, bf16[9,16,128]{2,1,0:T(8,128)(2,1)S(1)} %collective-permute-done.7.rest_2_, ...), custom_call_target="tpu_custom_call" | custom-call | flops 17179869184 | bytes 33554432 | tf_op jit(solution)/shard_map/merge/pallas_call | solution.py:329
  32.6 1.4 %collective-permute-done.9 = f32[16,2048]{1,0:T(8,128)S(1)} collective-permute-done((f32[16,2048]{1,0:T(8,128)S(1)}, f32[16,2048]{1,0:T(8,128)S(1)}, u32[]{:S(2)}, u32[]{:S(2)}) %collective-permute-start.9) | collective-permute-done | bytes 131104 | tf_op jit(solution)/shard_map/ppermute | solution.py:350
  34.0 1.6 %collective-permute-start.10 = (bf16[16,2048]{1,0:T(8,128)(2,1)S(1)}, bf16[16,2048]{1,0:T(8,128)(2,1)S(1)}, u32[]{:S(2)}, u32[]{:S(2)}) collective-permute-start(bf16[16,2048]{1,0:T(8,128)(2,1)S(1)} %add_convert_fusion.1), channel_id=1, source_target_pairs={{0,2},{1,3},{2,0},{3,1},{4,6},{5,7},{6,4},{7,5},{8,10},{9,11},{10,... | collective-permute-start | bytes 196616 | tf_op jit(solution)/shard_map/ppermute | solution.py:350
  35.5 2.8 %collective-permute-done.10 = bf16[16,2048]{1,0:T(8,128)(2,1)S(1)} collective-permute-done((bf16[16,2048]{1,0:T(8,128)(2,1)S(1)}, bf16[16,2048]{1,0:T(8,128)(2,1)S(1)}, u32[]{:S(2)}, u32[]{:S(2)}) %collective-permute-start.10) | collective-permute-done | bytes 65568 | tf_op jit(solution)/shard_map/ppermute | solution.py:350
  38.3 0.7 %add_convert_fusion = bf16[16,2048]{1,0:T(8,128)(2,1)} fusion(bf16[16,2048]{1,0:T(8,128)(2,1)S(1)} %collective-permute-done.10, bf16[16,2048]{1,0:T(8,128)(2,1)S(1)} %add_convert_fusion.1, bf16[16,2048]{1,0:T(8,128)(2,1)S(1)} %copy-done.1), kind=kLoop, calls=%fused_computation | loop fusion | flops 196608 | bytes 262144 | tf_op jit(solution)/shard_map/convert_element_type | solution.py:355
  (43 shorter events, 0.6 us)
Async XLA Ops:
  0.8 9.4 %copy-start.1 = (bf16[16,2048]{1,0:T(8,128)(2,1)S(1)}, bf16[16,2048]{1,0:T(8,128)(2,1)}, u32[]{:S(2)}) copy-start(bf16[16,2048]{1,0:T(8,128)(2,1)} %residual.3) | copy-start | bytes 196612
  0.8 9.4 %copy-start.2 = (bf16[2048,2048]{1,0:T(8,128)(2,1)S(1)}, bf16[2048,2048]{1,0:T(8,128)(2,1)}, u32[]{:S(2)}) copy-start(bf16[2048,2048]{1,0:T(8,128)(2,1)} %rest_6_.1) | copy-start | bytes 25165828
  0.8 9.4 %copy-start.5 = (bf16[2048,256]{1,0:T(8,128)(2,1)S(1)}, bf16[2048,256]{1,0:T(8,128)(2,1)}, u32[]{:S(2)}) copy-start(bf16[2048,256]{1,0:T(8,128)(2,1)} %rest_4_.3) | copy-start | bytes 3145732
  0.8 9.4 %copy-start.6 = (bf16[2048,256]{1,0:T(8,128)(2,1)S(1)}, bf16[2048,256]{1,0:T(8,128)(2,1)}, u32[]{:S(2)}) copy-start(bf16[2048,256]{1,0:T(8,128)(2,1)} %rest_5_.2) | copy-start | bytes 3145732
  0.9 9.4 %copy-start.7 = (bf16[2048]{0:T(1024)(128)(2,1)S(1)}, bf16[2048]{0:T(1024)(128)(2,1)}, u32[]{:S(2)}) copy-start(bf16[2048]{0:T(1024)(128)(2,1)} %gain.1) | copy-start | bytes 12292
  0.9 9.4 %copy-start.8 = (s32[4,4,2]{1,2,0:T(2,128)S(1)}, s32[4,4,2]{1,2,0:T(2,128)}, u32[]{:S(2)}) copy-start(s32[4,4,2]{1,2,0:T(2,128)} %param.21) | copy-start | bytes 388
  1.0 7.0 %collective-permute-start.2 = (f32[16,128]{1,0:T(8,128)S(1)}, f32[16,128]{1,0:T(8,128)S(1)}, u32[]{:S(2)}, u32[]{:S(2)}) collective-permute-start(f32[16,128]{1,0:T(8,128)S(1)} %square.1.rest_0_), channel_id=1, source_target_pairs={{0,4},{4,8},{8,12},{12,0},{1,5},{5,9},{9,13},{13,1},{2,6},{6,10},{... | collective-permute-start | bytes 24584 | tf_op jit(solution)/shard_map/ppermute | solution.py:237
  4.0 4.6 %collective-permute-start.1 = (f32[16,128]{1,0:T(8,128)S(1)}, f32[16,128]{1,0:T(8,128)S(1)}, u32[]{:S(2)}, u32[]{:S(2)}) collective-permute-start(f32[16,128]{1,0:T(8,128)S(1)} %square.1.rest_0_), channel_id=1, source_target_pairs={{0,8},{4,12},{8,0},{12,4},{1,9},{5,13},{9,1},{13,5},{2,10},{6,14},... | collective-permute-start | bytes 24584 | tf_op jit(solution)/shard_map/ppermute | solution.py:237
  6.6 3.7 %collective-permute-start = (f32[16,128]{1,0:T(8,128)S(1)}, f32[16,128]{1,0:T(8,128)S(1)}, u32[]{:S(2)}, u32[]{:S(2)}) collective-permute-start(f32[16,128]{1,0:T(8,128)S(1)} %square.1.rest_0_), channel_id=1, source_target_pairs={{0,12},{4,0},{8,4},{12,8},{1,13},{5,1},{9,5},{13,9},{2,14},{6,2},{... | collective-permute-start | bytes 24584 | tf_op jit(solution)/shard_map/ppermute | solution.py:237
  10.3 2.8 %copy-start.9 = (s32[16]{0:T(128)S(1)}, s32[16]{0:T(128)}, u32[]{:S(2)}) copy-start(s32[16]{0:T(128)} %context_len.1) | copy-start | bytes 196
  10.3 10.6 %copy-start.3 = (bf16[48,128,256]{2,1,0:T(8,128)(2,1)S(1)}, bf16[48,128,256]{2,1,0:T(8,128)(2,1)}, u32[]{:S(2)}) copy-start(bf16[48,128,256]{2,1,0:T(8,128)(2,1)} %rest_4_.4) | copy-start | bytes 9437188
  10.3 10.6 %copy-start.4 = (bf16[48,128,256]{2,1,0:T(8,128)(2,1)S(1)}, bf16[48,128,256]{2,1,0:T(8,128)(2,1)}, u32[]{:S(2)}) copy-start(bf16[48,128,256]{2,1,0:T(8,128)(2,1)} %rest_5_.3) | copy-start | bytes 9437188
  10.3 10.6 %copy-start.10 = (s32[48]{0:T(128)S(1)}, s32[48]{0:T(128)}, u32[]{:S(2)}) copy-start(s32[48]{0:T(128)} %slot_route.1) | copy-start | bytes 580
  10.3 10.6 %copy-start.11 = (s32[48]{0:T(128)S(1)}, s32[48]{0:T(128)}, u32[]{:S(2)}) copy-start(s32[48]{0:T(128)} %slot_block.1) | copy-start | bytes 580
  10.3 19.9 %slice-start = ((s8[8388608]{0:T(1024)(128)(4,1)}), s8[4194304]{0:T(1024)(128)(4,1)S(1)}, s32[]{:S(2)}) async-start(s8[8388608]{0:T(1024)(128)(4,1)} %bitcast.1), calls=%async_computation | async-start | bytes 8388608
  13.1 6.0 %collective-permute-start.5 = (f16[8,2560]{1,0:T(8,128)(2,1)S(1)}, f16[8,2560]{1,0:T(8,128)(2,1)S(1)}, u32[]{:S(2)}, u32[]{:S(2)}) collective-permute-start(f16[8,2560]{1,0:T(8,128)(2,1)S(1)} %multiply_convert_fusion), channel_id=1, source_target_pairs={{0,4},{4,8},{8,12},{12,0},{1,5},{5,9},{9,13},{13,1},{2,6},{6,10},{... | collective-permute-start | bytes 122888 | tf_op jit(solution)/shard_map/ppermute | solution.py:237
  13.3 6.5 %collective-permute-start.4 = (f16[8,2560]{1,0:T(8,128)(2,1)S(1)}, f16[8,2560]{1,0:T(8,128)(2,1)S(1)}, u32[]{:S(2)}, u32[]{:S(2)}) collective-permute-start(f16[8,2560]{1,0:T(8,128)(2,1)S(1)} %multiply_convert_fusion.1), channel_id=1, source_target_pairs={{0,8},{4,12},{8,0},{12,4},{1,9},{5,13},{9,1},{13,5},{2,10},{6,14},... | collective-permute-start | bytes 122888 | tf_op jit(solution)/shard_map/ppermute | solution.py:237
  16.9 4.0 %collective-permute-start.3 = (f16[8,2560]{1,0:T(8,128)(2,1)S(1)}, f16[8,2560]{1,0:T(8,128)(2,1)S(1)}, u32[]{:S(2)}, u32[]{:S(2)}) collective-permute-start(f16[8,2560]{1,0:T(8,128)(2,1)S(1)} %multiply_convert_fusion.2), channel_id=1, source_target_pairs={{0,12},{4,0},{8,4},{12,8},{1,13},{5,1},{9,5},{13,9},{2,14},{6,2},{... | collective-permute-start | bytes 122888 | tf_op jit(solution)/shard_map/ppermute | solution.py:237
  17.1 13.1 %slice-start.1 = ((s8[8388608]{0:T(1024)(128)(4,1)}), s8[4194304]{0:T(1024)(128)(4,1)S(1)}, s32[]{:S(2)}) async-start(s8[8388608]{0:T(1024)(128)(4,1)} %bitcast.1), calls=%async_computation.1 | async-start | bytes 8388608
  23.3 5.9 %collective-permute-start.8 = (bf16[9,16,128]{2,1,0:T(8,128)(2,1)S(1)}, bf16[9,16,128]{2,1,0:T(8,128)(2,1)S(1)}, u32[]{:S(2)}, u32[]{:S(2)}) collective-permute-start(bf16[9,16,128]{2,1,0:T(8,128)(2,1)S(1)} %attend.1.rest_0_), channel_id=1, source_target_pairs={{0,4},{4,8},{8,12},{12,0},{1,5},{5,9},{9,13},{13,1},{2,6},{6,10},{... | collective-permute-start | bytes 110600 | tf_op jit(solution)/shard_map/ppermute | solution.py:237
  24.1 5.6 %collective-permute-start.7 = (bf16[9,16,128]{2,1,0:T(8,128)(2,1)S(1)}, bf16[9,16,128]{2,1,0:T(8,128)(2,1)S(1)}, u32[]{:S(2)}, u32[]{:S(2)}) collective-permute-start(bf16[9,16,128]{2,1,0:T(8,128)(2,1)S(1)} %attend.1.rest_0_), channel_id=1, source_target_pairs={{0,8},{4,12},{8,0},{12,4},{1,9},{5,13},{9,1},{13,5},{2,10},{6,14},... | collective-permute-start | bytes 110600 | tf_op jit(solution)/shard_map/ppermute | solution.py:237
  26.2 4.0 %collective-permute-start.6 = (bf16[9,16,128]{2,1,0:T(8,128)(2,1)S(1)}, bf16[9,16,128]{2,1,0:T(8,128)(2,1)S(1)}, u32[]{:S(2)}, u32[]{:S(2)}) collective-permute-start(bf16[9,16,128]{2,1,0:T(8,128)(2,1)S(1)} %attend.1.rest_0_), channel_id=1, source_target_pairs={{0,12},{4,0},{8,4},{12,8},{1,13},{5,1},{9,5},{13,9},{2,14},{6,2},{... | collective-permute-start | bytes 110600 | tf_op jit(solution)/shard_map/ppermute | solution.py:237
  32.6 1.4 %collective-permute-start.9 = (f32[16,2048]{1,0:T(8,128)S(1)}, f32[16,2048]{1,0:T(8,128)S(1)}, u32[]{:S(2)}, u32[]{:S(2)}) collective-permute-start(f32[16,2048]{1,0:T(8,128)S(1)} %merge.1), channel_id=1, source_target_pairs={{0,1},{1,0},{2,3},{3,2},{4,5},{5,4},{6,7},{7,6},{8,9},{9,8},{10,11... | collective-permute-start | bytes 393224 | tf_op jit(solution)/shard_map/ppermute | solution.py:350
  34.0 4.3 %collective-permute-start.10 = (bf16[16,2048]{1,0:T(8,128)(2,1)S(1)}, bf16[16,2048]{1,0:T(8,128)(2,1)S(1)}, u32[]{:S(2)}, u32[]{:S(2)}) collective-permute-start(bf16[16,2048]{1,0:T(8,128)(2,1)S(1)} %add_convert_fusion.1), channel_id=1, source_target_pairs={{0,2},{1,3},{2,0},{3,1},{4,6},{5,7},{6,4},{7,5},{8,10},{9,11},{10,... | collective-permute-start | bytes 196616 | tf_op jit(solution)/shard_map/ppermute | solution.py:350
  (1 other events, 0.8 us)

commit v4 on v3

--- a/solution.py
+++ b/solution.py
@@ -113,6 +113,7 @@
     head_kv = lax.broadcasted_iota(jnp.int32, (heads, HD), 0) // group
 
     owns, mine = [], []
+    peak[...] = jnp.full(peak.shape, NEG_FILL, jnp.float32)
     for row in range(listed):
         home = row // per_home
         request = listed_at(routes, me, row)
@@ -129,7 +130,6 @@
         own = jnp.where(taken == 0, own, NEG_FILL)
         owns.append(own)
         mine.append(taken == 0)
-        peak[row] = own
 
     def slot_of(slot):
         entry = slot_route[slot]
@@ -152,7 +152,7 @@
         score[slot] = value
         peak[row] = jnp.maximum(peak[row], value)
     for row in range(listed):
-        top = jnp.broadcast_to(jnp.max(peak[row], axis=1, keepdims=True), (heads, HD))
+        top = jnp.maximum(jnp.max(peak[row], axis=1, keepdims=True), owns[row])
         peak[row] = top
         weight = jnp.where(mine[row], jnp.exp(owns[row] - top), 0.0)
         mass[row] = jnp.where(lanes == 0, weight, 0.0)
@@ -189,39 +189,55 @@
 
 
 def merge_kernel(pool_count, routes, *rest):
-    parts, (w_out, out) = rest[:pool_count], rest[pool_count : pool_count + 2]
-    best, numerator, denominator, flat = rest[pool_count + 2 :]
+    parts, (w_out, out, flat) = rest[:pool_count], rest[pool_count:]
     listed = parts[0].shape[0] - 1
-    requests, heads = best.shape[:2]
+    heads = parts[0].shape[1]
+    requests = out.shape[0]
     me = lax.axis_index("pool")
-    best[...] = jnp.full(best.shape, NEG_FILL, jnp.float32)
-    numerator[...] = jnp.zeros_like(numerator)
-    denominator[...] = jnp.zeros_like(denominator)
-    entries = []
+    flat[...] = jnp.zeros_like(flat)
+    lanes = lax.broadcasted_iota(jnp.int32, (heads, HD), 1)
+    asked, there, peaks, masses = [], [], [], []
     for place, shift in enumerate([0, *shifts(pool_count)]):
         owner = lax.rem(me + pool_count - shift, pool_count)
+        asked.append([listed_at(routes, owner, row) for row in range(listed)])
         stats = parts[place][listed].astype(jnp.float32)
-        for row in range(listed):
-            request = listed_at(routes, owner, row)
-            pieces = [
-                stats[:, piece * listed + row : piece * listed + row + 1] for piece in range(6)
-            ]
-            peak = jnp.broadcast_to(pieces[0] + pieces[1] + pieces[2], (heads, HD))
-            mass = jnp.broadcast_to(pieces[3] + pieces[4] + pieces[5], (heads, HD))
-            entries.append((place, row, request, peak, mass))
-            best[request] = jnp.maximum(best[request], peak)
-    for place, row, request, peak, mass in entries:
-        weight = jnp.exp(peak - best[request]) * mass
-        numerator[request] += weight * parts[place][row].astype(jnp.float32)
-        denominator[request] += weight
-    for request in range(requests):
-        flat[request * heads : (request + 1) * heads, :] = (
-            numerator[request] / denominator[request]
+        stats = (
+            stats + pltpu.roll(stats, HD - listed, 1) + pltpu.roll(stats, HD - 2 * listed, 1)
         )
-    attention = jnp.concatenate(
-        [flat[pl.ds(head, requests, stride=heads), :].astype(jnp.bfloat16) for head in range(heads)],
-        axis=1,
-    )
+        source = jnp.full((heads, HD), -1, jnp.int32)
+        for row, request in enumerate(asked[-1]):
+            source = jnp.where(lanes == request, row, source)
+        there.append(source >= 0)
+        source = jnp.maximum(source, 0)
+        peaks.append(
+            jnp.where(there[-1], jnp.take_along_axis(stats, source, axis=1), NEG_FILL)
+        )
+        masses.append(jnp.take_along_axis(stats, source + 3 * listed, axis=1))
+    best = functools.reduce(jnp.maximum, peaks)
+    weights = [
+        jnp.where(here, jnp.exp(peak - best) * mass, 0.0)
+        for here, peak, mass in zip(there, peaks, masses)
+    ]
+    whole = sum(weights[1:], weights[0])
+    whole = jnp.where(lanes < requests, whole, 1.0)
+    for place, ids in enumerate(asked):
+        back = jnp.zeros((heads, HD), jnp.int32)
+        for row, request in enumerate(ids):
+            back = jnp.where(lanes == row, request, back)
+        weight = jnp.take_along_axis(weights[place] / whole, back, axis=1)
+        for row, request in enumerate(ids):
+            block = pl.ds(pl.multiple_of(request * heads, heads), heads)
+            flat[place, block, :] = weight[:, row : row + 1] * parts[place][row].astype(
+                jnp.float32
+            )
+    columns = []
+    for head in range(heads):
+        block = pl.ds(head, requests, stride=heads)
+        value = flat[0, block, :]
+        for place in range(1, pool_count):
+            value = value + flat[place, block, :]
+        columns.append(value.astype(jnp.bfloat16))
+    attention = jnp.concatenate(columns, axis=1)
     for first in range(0, out.shape[1], CHUNK):
         out[:, first : first + CHUNK] = jnp.dot(
             attention, w_out[:, first : first + CHUNK], preferred_element_type=jnp.float32
@@ -331,28 +347,19 @@
         out_shape=jax.ShapeDtypeStruct((requests, w_out.shape[1]), f32),
         in_specs=[in_smem] + [in_vmem] * (pool_count + 1),
         out_specs=in_vmem,
-        scratch_shapes=[
-            pltpu.VMEM((requests, heads, HD), f32),
-            pltpu.VMEM((requests, heads, HD), f32),
-            pltpu.VMEM((requests, heads, HD), f32),
-            pltpu.VMEM((requests * heads, HD), f32),
-        ],
+        scratch_shapes=[pltpu.VMEM((pool_count, requests * heads, HD), f32)],
         compiler_params=pltpu.CompilerParams(vmem_limit_bytes=8 * 2**20),
         cost_estimate=spell,
         name="merge",
     )(routes, *partials, pin(w_out))
     tensor_count = lax.axis_size("tensor")
-    distance = 1
-    while distance < tensor_count:
-        last_step = 2 * distance == tensor_count
-        if last_step:
-            product = product.astype(jnp.bfloat16)
-        other = lax.ppermute(
-            product, "tensor", [(i, i ^ distance) for i in range(tensor_count)]
-        )
-        product = product.astype(f32) + other.astype(f32)
-        distance *= 2
-    return (residual.astype(f32) + product).astype(jnp.bfloat16)
+    product = product.astype(jnp.bfloat16)
+    one, two, three = [
+        lax.ppermute(product, "tensor", [(i, i ^ d) for i in range(tensor_count)]).astype(f32)
+        for d in (1, 2, 3)
+    ]
+    product = product.astype(f32)
+    return (residual.astype(f32) + ((product + one) + (two + three))).astype(jnp.bfloat16)
 
 
 def rotate(vectors, positions):
@@ -538,7 +545,7 @@
         P(("groups", "pool")),
     )
     pool_count, tensor_count = mesh.shape["pool"], mesh.shape["tensor"]
-    close = pool_count <= 4 and tensor_count & (tensor_count - 1) == 0
+    close = pool_count <= 4 and tensor_count == 4
     return jax.shard_map(
         close_pool if close else wide_pool,
         mesh=mesh,

time: 39.1 us -> 38.6 us (0.987)
  waiting for transfers between devices: 13 us -> 12 us
  starting transfers between devices: 16.3 us -> 17 us
    ppermute x2 -> x3, waiting for transfers between devices: 4.13 us -> 3.09 us  [close_pool(): lax.ppermute(product, 'tensor', [(i, i ^ d) for i in range(tensor_count)])]
    ppermute x2 -> x3, starting transfers between devices: 1.56 us -> 2.21 us  [close_pool(): lax.ppermute(product, 'tensor', [(i, i ^ d) for i in range(tensor_count)])]
  transfers between devices with their start and end apart: 11 -> 12, of which waited for: 10 -> 10; matrix products, arithmetic and copies ran while one was open for 1% -> 1% of each run, Pallas kernels for 0% -> 0%
where the time goes in v4:
time: 38.6 us; the launch traced here: 38.5 us
  starting transfers between devices  17 us (44%)
  waiting for transfers between devices  12 us (31%)
  Pallas kernels  7.42 us (19%)
  other arithmetic  0.96 us (2%)
  local copies, waits for them, and re-layouts  0.91 us (2%)
    ppermute x9, starting transfers between devices, shifted(): lax.ppermute(value, axis, [(i, (i + shift) % count) for i in range(count)])  14.8 us
    ppermute x9, waiting for transfers between devices, shifted(): lax.ppermute(value, axis, [(i, (i + shift) % count) for i in range(count)])  8.87 us
    ppermute x3, waiting for transfers between devices, close_pool(): lax.ppermute(product, 'tensor', [(i, i ^ d) for i in range(tensor_count)])  3.09 us
    pallas_call x1, Pallas kernels, close_pool(): pl.pallas_call(functools.partial(project_kernel, pool_count), out_shape=[...  2.7 us
    pallas_call x1, Pallas kernels, close_pool(): pl.pallas_call(functools.partial(attend_kernel, pool_count, local_kv, gro...  2.41 us
    pallas_call x1, Pallas kernels, close_pool(): pl.pallas_call(functools.partial(merge_kernel, pool_count), out_shape=jax...  2.22 us
    ppermute x3, starting transfers between devices, close_pool(): lax.ppermute(product, 'tensor', [(i, i ^ d) for i in range(tensor_count)])  2.21 us
    unnamed x28, local copies, waits for them, and re-layouts  0.91 us
  transfers between devices with their start and end apart: 12, of which 10 were waited for; matrix products, arithmetic and copies ran while one was open for 1% of the time, Pallas kernels for 0%

profile of v4, /device:TPU:0, one launch (start us, length us, event | category | flops | bytes accessed | tf_op | source)
XLA Modules:
  0.0 38.5 jit_solution(7903518542499469901)
XLA Ops:
  0.0 0.8 %copy-done = bf16[16,2048]{1,0:T(8,128)(2,1)S(1)} copy-done((bf16[16,2048]{1,0:T(8,128)(2,1)S(1)}, bf16[16,2048]{1,0:T(8,128)(2,1)}, u32[]{:S(2)}) %copy-start) | copy-done | bytes 65560
  1.0 3.0 %collective-permute-start.2 = (f32[16,128]{1,0:T(8,128)S(1)}, f32[16,128]{1,0:T(8,128)S(1)}, u32[]{:S(2)}, u32[]{:S(2)}) collective-permute-start(f32[16,128]{1,0:T(8,128)S(1)} %square.1.rest_0_), channel_id=1, source_target_pairs={{0,4},{4,8},{8,12},{12,0},{1,5},{5,9},{9,13},{13,1},{2,6},{6,10},{... | collective-permute-start | bytes 24584 | tf_op jit(solution)/shard_map/ppermute | solution.py:253
  4.0 2.6 %collective-permute-start.1 = (f32[16,128]{1,0:T(8,128)S(1)}, f32[16,128]{1,0:T(8,128)S(1)}, u32[]{:S(2)}, u32[]{:S(2)}) collective-permute-start(f32[16,128]{1,0:T(8,128)S(1)} %square.1.rest_0_), channel_id=1, source_target_pairs={{0,8},{4,12},{8,0},{12,4},{1,9},{5,13},{9,1},{13,5},{2,10},{6,14},... | collective-permute-start | bytes 24584 | tf_op jit(solution)/shard_map/ppermute | solution.py:253
  6.6 1.3 %collective-permute-start = (f32[16,128]{1,0:T(8,128)S(1)}, f32[16,128]{1,0:T(8,128)S(1)}, u32[]{:S(2)}, u32[]{:S(2)}) collective-permute-start(f32[16,128]{1,0:T(8,128)S(1)} %square.1.rest_0_), channel_id=1, source_target_pairs={{0,12},{4,0},{8,4},{12,8},{1,13},{5,1},{9,5},{13,9},{2,14},{6,2},{... | collective-permute-start | bytes 24584 | tf_op jit(solution)/shard_map/ppermute | solution.py:253
  7.9 0.7 %collective-permute-done.1.rest_2_ = f32[16,128]{1,0:T(8,128)S(1)} collective-permute-done((f32[16,128]{1,0:T(8,128)S(1)}, f32[16,128]{1,0:T(8,128)S(1)}, u32[]{:S(2)}, u32[]{:S(2)}) %collective-permute-start.1) | collective-permute-done | bytes 8224 | tf_op jit(solution)/shard_map/ppermute | solution.py:253
  8.6 1.6 %collective-permute-done.rest_1_ = f32[16,128]{1,0:T(8,128)S(1)} collective-permute-done((f32[16,128]{1,0:T(8,128)S(1)}, f32[16,128]{1,0:T(8,128)S(1)}, u32[]{:S(2)}, u32[]{:S(2)}) %collective-permute-start) | collective-permute-done | bytes 8224 | tf_op jit(solution)/shard_map/ppermute | solution.py:253
  10.3 2.7 %project.1 = (f32[8,2560]{1,0:T(8,128)S(1)}, f32[8,2560]{1,0:T(8,128)S(1)}, f32[8,2560]{1,0:T(8,128)S(1)}, f32[8,2560]{1,0:T(8,128)S(1)}) custom-call(s32[4,2,4]{2,1,0:T(2,128)S(1)} %bitcast.3, bf16[16,2048]{1,0:T(8,128)(2,1)S(1)} %copy-done.1, bf16[2048]{0:T(1024)(128)(2,1)S(1)} %copy-done.7, f32[16,128]{1,0:T(8,128)S(1)} %square.1.rest_0_, ...), custom_call_target="tpu_custom_call" | custom-call | flops 17179869184 | bytes 33554432 | tf_op jit(solution)/shard_map/project/pallas_call | solution.py:297
  13.3 3.6 %collective-permute-start.4 = (f16[8,2560]{1,0:T(8,128)(2,1)S(1)}, f16[8,2560]{1,0:T(8,128)(2,1)S(1)}, u32[]{:S(2)}, u32[]{:S(2)}) collective-permute-start(f16[8,2560]{1,0:T(8,128)(2,1)S(1)} %multiply_convert_fusion.1), channel_id=1, source_target_pairs={{0,8},{4,12},{8,0},{12,4},{1,9},{5,13},{9,1},{13,5},{2,10},{6,14},... | collective-permute-start | bytes 122888 | tf_op jit(solution)/shard_map/ppermute | solution.py:253
  17.2 1.9 %collective-permute-done.5 = f16[8,2560]{1,0:T(8,128)(2,1)S(1)} collective-permute-done((f16[8,2560]{1,0:T(8,128)(2,1)S(1)}, f16[8,2560]{1,0:T(8,128)(2,1)S(1)}, u32[]{:S(2)}, u32[]{:S(2)}) %collective-permute-start.5) | collective-permute-done | bytes 40992 | tf_op jit(solution)/shard_map/ppermute | solution.py:253
  19.1 0.7 %collective-permute-done.4 = f16[8,2560]{1,0:T(8,128)(2,1)S(1)} collective-permute-done((f16[8,2560]{1,0:T(8,128)(2,1)S(1)}, f16[8,2560]{1,0:T(8,128)(2,1)S(1)}, u32[]{:S(2)}, u32[]{:S(2)}) %collective-permute-start.4) | collective-permute-done | bytes 40992 | tf_op jit(solution)/shard_map/ppermute | solution.py:253
  19.8 1.1 %collective-permute-done.3 = f16[8,2560]{1,0:T(8,128)(2,1)S(1)} collective-permute-done((f16[8,2560]{1,0:T(8,128)(2,1)S(1)}, f16[8,2560]{1,0:T(8,128)(2,1)S(1)}, u32[]{:S(2)}, u32[]{:S(2)}) %collective-permute-start.3) | collective-permute-done | bytes 40992 | tf_op jit(solution)/shard_map/ppermute | solution.py:253
  21.0 2.4 %attend.1.rest_0_ = bf16[9,16,128]{2,1,0:T(8,128)(2,1)S(1)} custom-call(s32[4,2,4]{2,1,0:T(2,128)S(1)} %bitcast.4, s32[16]{0:T(128)S(1)} %copy-done.9, s32[48]{0:T(128)S(1)} %copy-done.10, s32[48]{0:T(128)S(1)} %copy-done.11, f32[16,256]{1,0:T(8,128)S(1)} %pad_maximum_fusion.turn, f32[8,2560]{1,0:T(8,128)S(1)} %get-tuple-element.10.rest_0_, ...), custom_call_target="tpu_custom_call" | custom-call | flops 17179869184 | bytes 33554432 | tf_op jit(solution)/shard_map/attend/pallas_call | solution.py:324
  23.4 0.7 %collective-permute-start.8 = (bf16[9,16,128]{2,1,0:T(8,128)(2,1)S(1)}, bf16[9,16,128]{2,1,0:T(8,128)(2,1)S(1)}, u32[]{:S(2)}, u32[]{:S(2)}) collective-permute-start(bf16[9,16,128]{2,1,0:T(8,128)(2,1)S(1)} %attend.1.rest_0_), channel_id=1, source_target_pairs={{0,4},{4,8},{8,12},{12,0},{1,5},{5,9},{9,13},{13,1},{2,6},{6,10},{... | collective-permute-start | bytes 110600 | tf_op jit(solution)/shard_map/ppermute | solution.py:253
  24.1 2.2 %collective-permute-start.7 = (bf16[9,16,128]{2,1,0:T(8,128)(2,1)S(1)}, bf16[9,16,128]{2,1,0:T(8,128)(2,1)S(1)}, u32[]{:S(2)}, u32[]{:S(2)}) collective-permute-start(bf16[9,16,128]{2,1,0:T(8,128)(2,1)S(1)} %attend.1.rest_0_), channel_id=1, source_target_pairs={{0,8},{4,12},{8,0},{12,4},{1,9},{5,13},{9,1},{13,5},{2,10},{6,14},... | collective-permute-start | bytes 110600 | tf_op jit(solution)/shard_map/ppermute | solution.py:253
  26.3 1.0 %collective-permute-start.6 = (bf16[9,16,128]{2,1,0:T(8,128)(2,1)S(1)}, bf16[9,16,128]{2,1,0:T(8,128)(2,1)S(1)}, u32[]{:S(2)}, u32[]{:S(2)}) collective-permute-start(bf16[9,16,128]{2,1,0:T(8,128)(2,1)S(1)} %attend.1.rest_0_), channel_id=1, source_target_pairs={{0,12},{4,0},{8,4},{12,8},{1,13},{5,1},{9,5},{13,9},{2,14},{6,2},{... | collective-permute-start | bytes 110600 | tf_op jit(solution)/shard_map/ppermute | solution.py:253
  27.3 2.0 %collective-permute-done.8.rest_3_ = bf16[9,16,128]{2,1,0:T(8,128)(2,1)S(1)} collective-permute-done((bf16[9,16,128]{2,1,0:T(8,128)(2,1)S(1)}, bf16[9,16,128]{2,1,0:T(8,128)(2,1)S(1)}, u32[]{:S(2)}, u32[]{:S(2)}) %collective-permute-start.8) | collective-permute-done | bytes 36896 | tf_op jit(solution)/shard_map/ppermute | solution.py:253
  29.3 0.4 %collective-permute-done.7.rest_2_ = bf16[9,16,128]{2,1,0:T(8,128)(2,1)S(1)} collective-permute-done((bf16[9,16,128]{2,1,0:T(8,128)(2,1)S(1)}, bf16[9,16,128]{2,1,0:T(8,128)(2,1)S(1)}, u32[]{:S(2)}, u32[]{:S(2)}) %collective-permute-start.7) | collective-permute-done | bytes 36896 | tf_op jit(solution)/shard_map/ppermute | solution.py:253
  29.7 0.5 %collective-permute-done.6.rest_1_ = bf16[9,16,128]{2,1,0:T(8,128)(2,1)S(1)} collective-permute-done((bf16[9,16,128]{2,1,0:T(8,128)(2,1)S(1)}, bf16[9,16,128]{2,1,0:T(8,128)(2,1)S(1)}, u32[]{:S(2)}, u32[]{:S(2)}) %collective-permute-start.6) | collective-permute-done | bytes 36896 | tf_op jit(solution)/shard_map/ppermute | solution.py:253
  30.2 2.2 %merge.1 = f32[16,2048]{1,0:T(8,128)S(1)} custom-call(s32[4,2,4]{2,1,0:T(2,128)S(1)} %bitcast.5, bf16[9,16,128]{2,1,0:T(8,128)(2,1)S(1)} %attend.1.rest_0_, bf16[9,16,128]{2,1,0:T(8,128)(2,1)S(1)} %collective-permute-done.6.rest_1_, bf16[9,16,128]{2,1,0:T(8,128)(2,1)S(1)} %collective-permute-done.7.rest_2_, ...), custom_call_target="tpu_custom_call" | custom-call | flops 17179869184 | bytes 33554432 | tf_op jit(solution)/shard_map/merge/pallas_call | solution.py:345
  32.5 1.6 %collective-permute-start.10 = (bf16[16,2048]{1,0:T(8,128)(2,1)S(1)}, bf16[16,2048]{1,0:T(8,128)(2,1)S(1)}, u32[]{:S(2)}, u32[]{:S(2)}) collective-permute-start(bf16[16,2048]{1,0:T(8,128)(2,1)S(1)} %convert_element_type.50), channel_id=1, source_target_pairs={{0,2},{1,3},{2,0},{3,1},{4,6},{5,7},{6,4},{7,5},{8,10},{9,11},{10,... | collective-permute-start | bytes 196616 | tf_op jit(solution)/shard_map/ppermute | solution.py:358
  34.0 0.7 %collective-permute-start.11 = (bf16[16,2048]{1,0:T(8,128)(2,1)S(1)}, bf16[16,2048]{1,0:T(8,128)(2,1)S(1)}, u32[]{:S(2)}, u32[]{:S(2)}) collective-permute-start(bf16[16,2048]{1,0:T(8,128)(2,1)S(1)} %convert_element_type.50), channel_id=1, source_target_pairs={{0,3},{1,2},{2,1},{3,0},{4,7},{5,6},{6,5},{7,4},{8,11},{9,10},{10,... | collective-permute-start | bytes 196616 | tf_op jit(solution)/shard_map/ppermute | solution.py:358
  34.7 2.1 %collective-permute-done.10 = bf16[16,2048]{1,0:T(8,128)(2,1)S(1)} collective-permute-done((bf16[16,2048]{1,0:T(8,128)(2,1)S(1)}, bf16[16,2048]{1,0:T(8,128)(2,1)S(1)}, u32[]{:S(2)}, u32[]{:S(2)}) %collective-permute-start.10) | collective-permute-done | bytes 65568 | tf_op jit(solution)/shard_map/ppermute | solution.py:358
  36.8 1.0 %collective-permute-done.11 = bf16[16,2048]{1,0:T(8,128)(2,1)S(1)} collective-permute-done((bf16[16,2048]{1,0:T(8,128)(2,1)S(1)}, bf16[16,2048]{1,0:T(8,128)(2,1)S(1)}, u32[]{:S(2)}, u32[]{:S(2)}) %collective-permute-start.11) | collective-permute-done | bytes 65568 | tf_op jit(solution)/shard_map/ppermute | solution.py:358
  37.8 0.7 %add_convert_fusion = bf16[16,2048]{1,0:T(8,128)(2,1)} fusion(bf16[16,2048]{1,0:T(8,128)(2,1)S(1)} %collective-permute-done.11, bf16[16,2048]{1,0:T(8,128)(2,1)S(1)} %collective-permute-done.10, bf16[16,2048]{1,0:T(8,128)(2,1)S(1)} %collective-permute-done.9, bf16[16,2048]{1,0:T(8,128)(2,1)S(1)} %copy-done.1, f32[16,2048]{1,0:T(8,128)S(1)} %merge.1), kind=kLoop, calls=%fused_computation | loop fusion | flops 360448 | bytes 458752 | tf_op jit(solution)/shard_map/convert_element_type | solution.py:362
  (45 shorter events, 0.7 us)
Async XLA Ops:
  0.8 9.4 %copy-start.1 = (bf16[16,2048]{1,0:T(8,128)(2,1)S(1)}, bf16[16,2048]{1,0:T(8,128)(2,1)}, u32[]{:S(2)}) copy-start(bf16[16,2048]{1,0:T(8,128)(2,1)} %residual.3) | copy-start | bytes 196612
  0.8 9.4 %copy-start.2 = (bf16[2048,2048]{1,0:T(8,128)(2,1)S(1)}, bf16[2048,2048]{1,0:T(8,128)(2,1)}, u32[]{:S(2)}) copy-start(bf16[2048,2048]{1,0:T(8,128)(2,1)} %rest_6_.1) | copy-start | bytes 25165828
  0.8 9.4 %copy-start.5 = (bf16[2048,256]{1,0:T(8,128)(2,1)S(1)}, bf16[2048,256]{1,0:T(8,128)(2,1)}, u32[]{:S(2)}) copy-start(bf16[2048,256]{1,0:T(8,128)(2,1)} %rest_4_.3) | copy-start | bytes 3145732
  0.8 9.4 %copy-start.6 = (bf16[2048,256]{1,0:T(8,128)(2,1)S(1)}, bf16[2048,256]{1,0:T(8,128)(2,1)}, u32[]{:S(2)}) copy-start(bf16[2048,256]{1,0:T(8,128)(2,1)} %rest_5_.2) | copy-start | bytes 3145732
  0.9 9.4 %copy-start.7 = (bf16[2048]{0:T(1024)(128)(2,1)S(1)}, bf16[2048]{0:T(1024)(128)(2,1)}, u32[]{:S(2)}) copy-start(bf16[2048]{0:T(1024)(128)(2,1)} %gain.1) | copy-start | bytes 12292
  0.9 9.4 %copy-start.8 = (s32[4,4,2]{1,2,0:T(2,128)S(1)}, s32[4,4,2]{1,2,0:T(2,128)}, u32[]{:S(2)}) copy-start(s32[4,4,2]{1,2,0:T(2,128)} %param.21) | copy-start | bytes 388
  1.0 7.0 %collective-permute-start.2 = (f32[16,128]{1,0:T(8,128)S(1)}, f32[16,128]{1,0:T(8,128)S(1)}, u32[]{:S(2)}, u32[]{:S(2)}) collective-permute-start(f32[16,128]{1,0:T(8,128)S(1)} %square.1.rest_0_), channel_id=1, source_target_pairs={{0,4},{4,8},{8,12},{12,0},{1,5},{5,9},{9,13},{13,1},{2,6},{6,10},{... | collective-permute-start | bytes 24584 | tf_op jit(solution)/shard_map/ppermute | solution.py:253
  4.0 4.6 %collective-permute-start.1 = (f32[16,128]{1,0:T(8,128)S(1)}, f32[16,128]{1,0:T(8,128)S(1)}, u32[]{:S(2)}, u32[]{:S(2)}) collective-permute-start(f32[16,128]{1,0:T(8,128)S(1)} %square.1.rest_0_), channel_id=1, source_target_pairs={{0,8},{4,12},{8,0},{12,4},{1,9},{5,13},{9,1},{13,5},{2,10},{6,14},... | collective-permute-start | bytes 24584 | tf_op jit(solution)/shard_map/ppermute | solution.py:253
  6.6 3.7 %collective-permute-start = (f32[16,128]{1,0:T(8,128)S(1)}, f32[16,128]{1,0:T(8,128)S(1)}, u32[]{:S(2)}, u32[]{:S(2)}) collective-permute-start(f32[16,128]{1,0:T(8,128)S(1)} %square.1.rest_0_), channel_id=1, source_target_pairs={{0,12},{4,0},{8,4},{12,8},{1,13},{5,1},{9,5},{13,9},{2,14},{6,2},{... | collective-permute-start | bytes 24584 | tf_op jit(solution)/shard_map/ppermute | solution.py:253
  10.3 10.6 %copy-start.3 = (bf16[48,128,256]{2,1,0:T(8,128)(2,1)S(1)}, bf16[48,128,256]{2,1,0:T(8,128)(2,1)}, u32[]{:S(2)}) copy-start(bf16[48,128,256]{2,1,0:T(8,128)(2,1)} %rest_4_.4) | copy-start | bytes 9437188
  10.3 10.6 %copy-start.4 = (bf16[48,128,256]{2,1,0:T(8,128)(2,1)S(1)}, bf16[48,128,256]{2,1,0:T(8,128)(2,1)}, u32[]{:S(2)}) copy-start(bf16[48,128,256]{2,1,0:T(8,128)(2,1)} %rest_5_.3) | copy-start | bytes 9437188
  10.3 10.6 %copy-start.10 = (s32[48]{0:T(128)S(1)}, s32[48]{0:T(128)}, u32[]{:S(2)}) copy-start(s32[48]{0:T(128)} %slot_route.1) | copy-start | bytes 580
  10.3 10.6 %copy-start.11 = (s32[48]{0:T(128)S(1)}, s32[48]{0:T(128)}, u32[]{:S(2)}) copy-start(s32[48]{0:T(128)} %slot_block.1) | copy-start | bytes 580
  10.3 19.9 %slice-start = ((s8[8388608]{0:T(1024)(128)(4,1)}), s8[4194304]{0:T(1024)(128)(4,1)S(1)}, s32[]{:S(2)}) async-start(s8[8388608]{0:T(1024)(128)(4,1)} %bitcast.1), calls=%async_computation | async-start | bytes 8388608
  13.1 6.0 %collective-permute-start.5 = (f16[8,2560]{1,0:T(8,128)(2,1)S(1)}, f16[8,2560]{1,0:T(8,128)(2,1)S(1)}, u32[]{:S(2)}, u32[]{:S(2)}) collective-permute-start(f16[8,2560]{1,0:T(8,128)(2,1)S(1)} %multiply_convert_fusion), channel_id=1, source_target_pairs={{0,4},{4,8},{8,12},{12,0},{1,5},{5,9},{9,13},{13,1},{2,6},{6,10},{... | collective-permute-start | bytes 122888 | tf_op jit(solution)/shard_map/ppermute | solution.py:253
  13.3 6.5 %collective-permute-start.4 = (f16[8,2560]{1,0:T(8,128)(2,1)S(1)}, f16[8,2560]{1,0:T(8,128)(2,1)S(1)}, u32[]{:S(2)}, u32[]{:S(2)}) collective-permute-start(f16[8,2560]{1,0:T(8,128)(2,1)S(1)} %multiply_convert_fusion.1), channel_id=1, source_target_pairs={{0,8},{4,12},{8,0},{12,4},{1,9},{5,13},{9,1},{13,5},{2,10},{6,14},... | collective-permute-start | bytes 122888 | tf_op jit(solution)/shard_map/ppermute | solution.py:253
  16.9 4.0 %collective-permute-start.3 = (f16[8,2560]{1,0:T(8,128)(2,1)S(1)}, f16[8,2560]{1,0:T(8,128)(2,1)S(1)}, u32[]{:S(2)}, u32[]{:S(2)}) collective-permute-start(f16[8,2560]{1,0:T(8,128)(2,1)S(1)} %multiply_convert_fusion.2), channel_id=1, source_target_pairs={{0,12},{4,0},{8,4},{12,8},{1,13},{5,1},{9,5},{13,9},{2,14},{6,2},{... | collective-permute-start | bytes 122888 | tf_op jit(solution)/shard_map/ppermute | solution.py:253
  17.1 13.1 %slice-start.1 = ((s8[8388608]{0:T(1024)(128)(4,1)}), s8[4194304]{0:T(1024)(128)(4,1)S(1)}, s32[]{:S(2)}) async-start(s8[8388608]{0:T(1024)(128)(4,1)} %bitcast.1), calls=%async_computation.1 | async-start | bytes 8388608
  23.4 5.9 %collective-permute-start.8 = (bf16[9,16,128]{2,1,0:T(8,128)(2,1)S(1)}, bf16[9,16,128]{2,1,0:T(8,128)(2,1)S(1)}, u32[]{:S(2)}, u32[]{:S(2)}) collective-permute-start(bf16[9,16,128]{2,1,0:T(8,128)(2,1)S(1)} %attend.1.rest_0_), channel_id=1, source_target_pairs={{0,4},{4,8},{8,12},{12,0},{1,5},{5,9},{9,13},{13,1},{2,6},{6,10},{... | collective-permute-start | bytes 110600 | tf_op jit(solution)/shard_map/ppermute | solution.py:253
  24.1 5.6 %collective-permute-start.7 = (bf16[9,16,128]{2,1,0:T(8,128)(2,1)S(1)}, bf16[9,16,128]{2,1,0:T(8,128)(2,1)S(1)}, u32[]{:S(2)}, u32[]{:S(2)}) collective-permute-start(bf16[9,16,128]{2,1,0:T(8,128)(2,1)S(1)} %attend.1.rest_0_), channel_id=1, source_target_pairs={{0,8},{4,12},{8,0},{12,4},{1,9},{5,13},{9,1},{13,5},{2,10},{6,14},... | collective-permute-start | bytes 110600 | tf_op jit(solution)/shard_map/ppermute | solution.py:253
  26.3 4.0 %collective-permute-start.6 = (bf16[9,16,128]{2,1,0:T(8,128)(2,1)S(1)}, bf16[9,16,128]{2,1,0:T(8,128)(2,1)S(1)}, u32[]{:S(2)}, u32[]{:S(2)}) collective-permute-start(bf16[9,16,128]{2,1,0:T(8,128)(2,1)S(1)} %attend.1.rest_0_), channel_id=1, source_target_pairs={{0,12},{4,0},{8,4},{12,8},{1,13},{5,1},{9,5},{13,9},{2,14},{6,2},{... | collective-permute-start | bytes 110600 | tf_op jit(solution)/shard_map/ppermute | solution.py:253
  32.5 4.3 %collective-permute-start.10 = (bf16[16,2048]{1,0:T(8,128)(2,1)S(1)}, bf16[16,2048]{1,0:T(8,128)(2,1)S(1)}, u32[]{:S(2)}, u32[]{:S(2)}) collective-permute-start(bf16[16,2048]{1,0:T(8,128)(2,1)S(1)} %convert_element_type.50), channel_id=1, source_target_pairs={{0,2},{1,3},{2,0},{3,1},{4,6},{5,7},{6,4},{7,5},{8,10},{9,11},{10,... | collective-permute-start | bytes 196616 | tf_op jit(solution)/shard_map/ppermute | solution.py:358
  34.0 2.8 %collective-permute-start.9 = (bf16[16,2048]{1,0:T(8,128)(2,1)S(1)}, bf16[16,2048]{1,0:T(8,128)(2,1)S(1)}, u32[]{:S(2)}, u32[]{:S(2)}) collective-permute-start(bf16[16,2048]{1,0:T(8,128)(2,1)S(1)} %convert_element_type.50), channel_id=1, source_target_pairs={{0,1},{1,0},{2,3},{3,2},{4,5},{5,4},{6,7},{7,6},{8,9},{9,8},{10,11... | collective-permute-start | bytes 196616 | tf_op jit(solution)/shard_map/ppermute | solution.py:358
  34.0 3.7 %collective-permute-start.11 = (bf16[16,2048]{1,0:T(8,128)(2,1)S(1)}, bf16[16,2048]{1,0:T(8,128)(2,1)S(1)}, u32[]{:S(2)}, u32[]{:S(2)}) collective-permute-start(bf16[16,2048]{1,0:T(8,128)(2,1)S(1)} %convert_element_type.50), channel_id=1, source_target_pairs={{0,3},{1,2},{2,1},{3,0},{4,7},{5,6},{6,5},{7,4},{8,11},{9,10},{10,... | collective-permute-start | bytes 196616 | tf_op jit(solution)/shard_map/ppermute | solution.py:358
  (2 other events, 3.6 us)

commit v5 on v4

--- a/solution.py
+++ b/solution.py
@@ -194,7 +194,7 @@
     heads = parts[0].shape[1]
     requests = out.shape[0]
     me = lax.axis_index("pool")
-    flat[...] = jnp.zeros_like(flat)
+    flat[:, : requests * heads, :] = jnp.zeros((pool_count, requests * heads, HD), jnp.float32)
     lanes = lax.broadcasted_iota(jnp.int32, (heads, HD), 1)
     asked, there, peaks, masses = [], [], [], []
     for place, shift in enumerate([0, *shifts(pool_count)]):
@@ -328,8 +328,8 @@
         out_specs=in_vmem,
         scratch_shapes=[
             pltpu.VMEM((listed, 2 * HD), f32),
-            pltpu.VMEM((heads * listed, HD), f32),
-            pltpu.VMEM((heads * listed, HD), f32),
+            pltpu.VMEM(((heads + 1) * listed, HD), f32),
+            pltpu.VMEM(((heads + 1) * listed, HD), f32),
             pltpu.VMEM((listed, heads, key_width), jnp.bfloat16),
             pltpu.VMEM((slots, heads, HD), f32),
             pltpu.VMEM((listed, heads, HD), f32),
@@ -347,7 +347,7 @@
         out_shape=jax.ShapeDtypeStruct((requests, w_out.shape[1]), f32),
         in_specs=[in_smem] + [in_vmem] * (pool_count + 1),
         out_specs=in_vmem,
-        scratch_shapes=[pltpu.VMEM((pool_count, requests * heads, HD), f32)],
+        scratch_shapes=[pltpu.VMEM((pool_count, (requests + 1) * heads, HD), f32)],
         compiler_params=pltpu.CompilerParams(vmem_limit_bytes=8 * 2**20),
         cost_estimate=spell,
         name="merge",

time: 38.6 us -> 38.6 us (level)
  no operation moved by 1% of the time
where the time goes in v5:
time: 38.6 us; the launch traced here: 38.4 us
  starting transfers between devices  16.9 us (44%)
  waiting for transfers between devices  11.9 us (31%)
  Pallas kernels  7.46 us (19%)
  other arithmetic  0.96 us (2%)
  local copies, waits for them, and re-layouts  0.91 us (2%)
    ppermute x9, starting transfers between devices, shifted(): lax.ppermute(value, axis, [(i, (i + shift) % count) for i in range(count)])  14.7 us
    ppermute x9, waiting for transfers between devices, shifted(): lax.ppermute(value, axis, [(i, (i + shift) % count) for i in range(count)])  8.82 us
    ppermute x3, waiting for transfers between devices, close_pool(): lax.ppermute(product, 'tensor', [(i, i ^ d) for i in range(tensor_count)])  3.09 us
    pallas_call x1, Pallas kernels, close_pool(): pl.pallas_call(functools.partial(project_kernel, pool_count), out_shape=[...  2.7 us
    pallas_call x1, Pallas kernels, close_pool(): pl.pallas_call(functools.partial(attend_kernel, pool_count, local_kv, gro...  2.44 us
    pallas_call x1, Pallas kernels, close_pool(): pl.pallas_call(functools.partial(merge_kernel, pool_count), out_shape=jax...  2.22 us
    ppermute x3, starting transfers between devices, close_pool(): lax.ppermute(product, 'tensor', [(i, i ^ d) for i in range(tensor_count)])  2.21 us
    unnamed x28, local copies, waits for them, and re-layouts  0.91 us
  transfers between devices with their start and end apart: 12, of which 10 were waited for; matrix products, arithmetic and copies ran while one was open for 1% of the time, Pallas kernels for 0%

profile of v5, /device:TPU:0, one launch (start us, length us, event | category | flops | bytes accessed | tf_op | source)
XLA Modules:
  0.0 38.4 jit_solution(2979086214343621699)
XLA Ops:
  0.0 0.8 %copy-done = bf16[16,2048]{1,0:T(8,128)(2,1)S(1)} copy-done((bf16[16,2048]{1,0:T(8,128)(2,1)S(1)}, bf16[16,2048]{1,0:T(8,128)(2,1)}, u32[]{:S(2)}) %copy-start) | copy-done | bytes 65560
  1.0 3.0 %collective-permute-start.2 = (f32[16,128]{1,0:T(8,128)S(1)}, f32[16,128]{1,0:T(8,128)S(1)}, u32[]{:S(2)}, u32[]{:S(2)}) collective-permute-start(f32[16,128]{1,0:T(8,128)S(1)} %square.1.rest_0_), channel_id=1, source_target_pairs={{0,4},{4,8},{8,12},{12,0},{1,5},{5,9},{9,13},{13,1},{2,6},{6,10},{... | collective-permute-start | bytes 24584 | tf_op jit(solution)/shard_map/ppermute | solution.py:253
  4.0 2.6 %collective-permute-start.1 = (f32[16,128]{1,0:T(8,128)S(1)}, f32[16,128]{1,0:T(8,128)S(1)}, u32[]{:S(2)}, u32[]{:S(2)}) collective-permute-start(f32[16,128]{1,0:T(8,128)S(1)} %square.1.rest_0_), channel_id=1, source_target_pairs={{0,8},{4,12},{8,0},{12,4},{1,9},{5,13},{9,1},{13,5},{2,10},{6,14},... | collective-permute-start | bytes 24584 | tf_op jit(solution)/shard_map/ppermute | solution.py:253
  6.6 1.3 %collective-permute-start = (f32[16,128]{1,0:T(8,128)S(1)}, f32[16,128]{1,0:T(8,128)S(1)}, u32[]{:S(2)}, u32[]{:S(2)}) collective-permute-start(f32[16,128]{1,0:T(8,128)S(1)} %square.1.rest_0_), channel_id=1, source_target_pairs={{0,12},{4,0},{8,4},{12,8},{1,13},{5,1},{9,5},{13,9},{2,14},{6,2},{... | collective-permute-start | bytes 24584 | tf_op jit(solution)/shard_map/ppermute | solution.py:253
  7.9 0.7 %collective-permute-done.1.rest_2_ = f32[16,128]{1,0:T(8,128)S(1)} collective-permute-done((f32[16,128]{1,0:T(8,128)S(1)}, f32[16,128]{1,0:T(8,128)S(1)}, u32[]{:S(2)}, u32[]{:S(2)}) %collective-permute-start.1) | collective-permute-done | bytes 8224 | tf_op jit(solution)/shard_map/ppermute | solution.py:253
  8.6 1.6 %collective-permute-done.rest_1_ = f32[16,128]{1,0:T(8,128)S(1)} collective-permute-done((f32[16,128]{1,0:T(8,128)S(1)}, f32[16,128]{1,0:T(8,128)S(1)}, u32[]{:S(2)}, u32[]{:S(2)}) %collective-permute-start) | collective-permute-done | bytes 8224 | tf_op jit(solution)/shard_map/ppermute | solution.py:253
  10.3 2.7 %project.1 = (f32[8,2560]{1,0:T(8,128)S(1)}, f32[8,2560]{1,0:T(8,128)S(1)}, f32[8,2560]{1,0:T(8,128)S(1)}, f32[8,2560]{1,0:T(8,128)S(1)}) custom-call(s32[4,2,4]{2,1,0:T(2,128)S(1)} %bitcast.3, bf16[16,2048]{1,0:T(8,128)(2,1)S(1)} %copy-done.1, bf16[2048]{0:T(1024)(128)(2,1)S(1)} %copy-done.7, f32[16,128]{1,0:T(8,128)S(1)} %square.1.rest_0_, ...), custom_call_target="tpu_custom_call" | custom-call | flops 17179869184 | bytes 33554432 | tf_op jit(solution)/shard_map/project/pallas_call | solution.py:297
  13.3 3.6 %collective-permute-start.4 = (f16[8,2560]{1,0:T(8,128)(2,1)S(1)}, f16[8,2560]{1,0:T(8,128)(2,1)S(1)}, u32[]{:S(2)}, u32[]{:S(2)}) collective-permute-start(f16[8,2560]{1,0:T(8,128)(2,1)S(1)} %multiply_convert_fusion.1), channel_id=1, source_target_pairs={{0,8},{4,12},{8,0},{12,4},{1,9},{5,13},{9,1},{13,5},{2,10},{6,14},... | collective-permute-start | bytes 122888 | tf_op jit(solution)/shard_map/ppermute | solution.py:253
  17.2 1.9 %collective-permute-done.5 = f16[8,2560]{1,0:T(8,128)(2,1)S(1)} collective-permute-done((f16[8,2560]{1,0:T(8,128)(2,1)S(1)}, f16[8,2560]{1,0:T(8,128)(2,1)S(1)}, u32[]{:S(2)}, u32[]{:S(2)}) %collective-permute-start.5) | collective-permute-done | bytes 40992 | tf_op jit(solution)/shard_map/ppermute | solution.py:253
  19.1 0.7 %collective-permute-done.4 = f16[8,2560]{1,0:T(8,128)(2,1)S(1)} collective-permute-done((f16[8,2560]{1,0:T(8,128)(2,1)S(1)}, f16[8,2560]{1,0:T(8,128)(2,1)S(1)}, u32[]{:S(2)}, u32[]{:S(2)}) %collective-permute-start.4) | collective-permute-done | bytes 40992 | tf_op jit(solution)/shard_map/ppermute | solution.py:253
  19.8 1.1 %collective-permute-done.3 = f16[8,2560]{1,0:T(8,128)(2,1)S(1)} collective-permute-done((f16[8,2560]{1,0:T(8,128)(2,1)S(1)}, f16[8,2560]{1,0:T(8,128)(2,1)S(1)}, u32[]{:S(2)}, u32[]{:S(2)}) %collective-permute-start.3) | collective-permute-done | bytes 40992 | tf_op jit(solution)/shard_map/ppermute | solution.py:253
  21.0 2.4 %attend.1.rest_0_ = bf16[9,16,128]{2,1,0:T(8,128)(2,1)S(1)} custom-call(s32[4,2,4]{2,1,0:T(2,128)S(1)} %bitcast.4, s32[16]{0:T(128)S(1)} %copy-done.9, s32[48]{0:T(128)S(1)} %copy-done.10, s32[48]{0:T(128)S(1)} %copy-done.11, f32[16,256]{1,0:T(8,128)S(1)} %pad_maximum_fusion.turn, f32[8,2560]{1,0:T(8,128)S(1)} %get-tuple-element.10.rest_0_, ...), custom_call_target="tpu_custom_call" | custom-call | flops 17179869184 | bytes 33554432 | tf_op jit(solution)/shard_map/attend/pallas_call | solution.py:324
  23.4 0.7 %collective-permute-start.8 = (bf16[9,16,128]{2,1,0:T(8,128)(2,1)S(1)}, bf16[9,16,128]{2,1,0:T(8,128)(2,1)S(1)}, u32[]{:S(2)}, u32[]{:S(2)}) collective-permute-start(bf16[9,16,128]{2,1,0:T(8,128)(2,1)S(1)} %attend.1.rest_0_), channel_id=1, source_target_pairs={{0,4},{4,8},{8,12},{12,0},{1,5},{5,9},{9,13},{13,1},{2,6},{6,10},{... | collective-permute-start | bytes 110600 | tf_op jit(solution)/shard_map/ppermute | solution.py:253
  24.1 2.1 %collective-permute-start.7 = (bf16[9,16,128]{2,1,0:T(8,128)(2,1)S(1)}, bf16[9,16,128]{2,1,0:T(8,128)(2,1)S(1)}, u32[]{:S(2)}, u32[]{:S(2)}) collective-permute-start(bf16[9,16,128]{2,1,0:T(8,128)(2,1)S(1)} %attend.1.rest_0_), channel_id=1, source_target_pairs={{0,8},{4,12},{8,0},{12,4},{1,9},{5,13},{9,1},{13,5},{2,10},{6,14},... | collective-permute-start | bytes 110600 | tf_op jit(solution)/shard_map/ppermute | solution.py:253
  26.2 1.1 %collective-permute-start.6 = (bf16[9,16,128]{2,1,0:T(8,128)(2,1)S(1)}, bf16[9,16,128]{2,1,0:T(8,128)(2,1)S(1)}, u32[]{:S(2)}, u32[]{:S(2)}) collective-permute-start(bf16[9,16,128]{2,1,0:T(8,128)(2,1)S(1)} %attend.1.rest_0_), channel_id=1, source_target_pairs={{0,12},{4,0},{8,4},{12,8},{1,13},{5,1},{9,5},{13,9},{2,14},{6,2},{... | collective-permute-start | bytes 110600 | tf_op jit(solution)/shard_map/ppermute | solution.py:253
  27.3 2.0 %collective-permute-done.8.rest_3_ = bf16[9,16,128]{2,1,0:T(8,128)(2,1)S(1)} collective-permute-done((bf16[9,16,128]{2,1,0:T(8,128)(2,1)S(1)}, bf16[9,16,128]{2,1,0:T(8,128)(2,1)S(1)}, u32[]{:S(2)}, u32[]{:S(2)}) %collective-permute-start.8) | collective-permute-done | bytes 36896 | tf_op jit(solution)/shard_map/ppermute | solution.py:253
  29.3 0.4 %collective-permute-done.7.rest_2_ = bf16[9,16,128]{2,1,0:T(8,128)(2,1)S(1)} collective-permute-done((bf16[9,16,128]{2,1,0:T(8,128)(2,1)S(1)}, bf16[9,16,128]{2,1,0:T(8,128)(2,1)S(1)}, u32[]{:S(2)}, u32[]{:S(2)}) %collective-permute-start.7) | collective-permute-done | bytes 36896 | tf_op jit(solution)/shard_map/ppermute | solution.py:253
  29.7 0.4 %collective-permute-done.6.rest_1_ = bf16[9,16,128]{2,1,0:T(8,128)(2,1)S(1)} collective-permute-done((bf16[9,16,128]{2,1,0:T(8,128)(2,1)S(1)}, bf16[9,16,128]{2,1,0:T(8,128)(2,1)S(1)}, u32[]{:S(2)}, u32[]{:S(2)}) %collective-permute-start.6) | collective-permute-done | bytes 36896 | tf_op jit(solution)/shard_map/ppermute | solution.py:253
  30.2 2.2 %merge.1 = f32[16,2048]{1,0:T(8,128)S(1)} custom-call(s32[4,2,4]{2,1,0:T(2,128)S(1)} %bitcast.5, bf16[9,16,128]{2,1,0:T(8,128)(2,1)S(1)} %attend.1.rest_0_, bf16[9,16,128]{2,1,0:T(8,128)(2,1)S(1)} %collective-permute-done.6.rest_1_, bf16[9,16,128]{2,1,0:T(8,128)(2,1)S(1)} %collective-permute-done.7.rest_2_, ...), custom_call_target="tpu_custom_call" | custom-call | flops 17179869184 | bytes 33554432 | tf_op jit(solution)/shard_map/merge/pallas_call | solution.py:345
  32.4 1.6 %collective-permute-start.10 = (bf16[16,2048]{1,0:T(8,128)(2,1)S(1)}, bf16[16,2048]{1,0:T(8,128)(2,1)S(1)}, u32[]{:S(2)}, u32[]{:S(2)}) collective-permute-start(bf16[16,2048]{1,0:T(8,128)(2,1)S(1)} %convert_element_type.50), channel_id=1, source_target_pairs={{0,2},{1,3},{2,0},{3,1},{4,6},{5,7},{6,4},{7,5},{8,10},{9,11},{10,... | collective-permute-start | bytes 196616 | tf_op jit(solution)/shard_map/ppermute | solution.py:358
  34.0 0.7 %collective-permute-start.11 = (bf16[16,2048]{1,0:T(8,128)(2,1)S(1)}, bf16[16,2048]{1,0:T(8,128)(2,1)S(1)}, u32[]{:S(2)}, u32[]{:S(2)}) collective-permute-start(bf16[16,2048]{1,0:T(8,128)(2,1)S(1)} %convert_element_type.50), channel_id=1, source_target_pairs={{0,3},{1,2},{2,1},{3,0},{4,7},{5,6},{6,5},{7,4},{8,11},{9,10},{10,... | collective-permute-start | bytes 196616 | tf_op jit(solution)/shard_map/ppermute | solution.py:358
  34.6 2.1 %collective-permute-done.10 = bf16[16,2048]{1,0:T(8,128)(2,1)S(1)} collective-permute-done((bf16[16,2048]{1,0:T(8,128)(2,1)S(1)}, bf16[16,2048]{1,0:T(8,128)(2,1)S(1)}, u32[]{:S(2)}, u32[]{:S(2)}) %collective-permute-start.10) | collective-permute-done | bytes 65568 | tf_op jit(solution)/shard_map/ppermute | solution.py:358
  36.8 1.0 %collective-permute-done.11 = bf16[16,2048]{1,0:T(8,128)(2,1)S(1)} collective-permute-done((bf16[16,2048]{1,0:T(8,128)(2,1)S(1)}, bf16[16,2048]{1,0:T(8,128)(2,1)S(1)}, u32[]{:S(2)}, u32[]{:S(2)}) %collective-permute-start.11) | collective-permute-done | bytes 65568 | tf_op jit(solution)/shard_map/ppermute | solution.py:358
  37.7 0.7 %add_convert_fusion = bf16[16,2048]{1,0:T(8,128)(2,1)} fusion(bf16[16,2048]{1,0:T(8,128)(2,1)S(1)} %collective-permute-done.11, bf16[16,2048]{1,0:T(8,128)(2,1)S(1)} %collective-permute-done.10, bf16[16,2048]{1,0:T(8,128)(2,1)S(1)} %collective-permute-done.9, bf16[16,2048]{1,0:T(8,128)(2,1)S(1)} %copy-done.1, f32[16,2048]{1,0:T(8,128)S(1)} %merge.1), kind=kLoop, calls=%fused_computation | loop fusion | flops 360448 | bytes 458752 | tf_op jit(solution)/shard_map/convert_element_type | solution.py:362
  (45 shorter events, 0.7 us)
Async XLA Ops:
  0.8 9.4 %copy-start.1 = (bf16[16,2048]{1,0:T(8,128)(2,1)S(1)}, bf16[16,2048]{1,0:T(8,128)(2,1)}, u32[]{:S(2)}) copy-start(bf16[16,2048]{1,0:T(8,128)(2,1)} %residual.3) | copy-start | bytes 196612
  0.8 9.4 %copy-start.2 = (bf16[2048,2048]{1,0:T(8,128)(2,1)S(1)}, bf16[2048,2048]{1,0:T(8,128)(2,1)}, u32[]{:S(2)}) copy-start(bf16[2048,2048]{1,0:T(8,128)(2,1)} %rest_6_.1) | copy-start | bytes 25165828
  0.8 9.4 %copy-start.5 = (bf16[2048,256]{1,0:T(8,128)(2,1)S(1)}, bf16[2048,256]{1,0:T(8,128)(2,1)}, u32[]{:S(2)}) copy-start(bf16[2048,256]{1,0:T(8,128)(2,1)} %rest_4_.3) | copy-start | bytes 3145732
  0.8 9.4 %copy-start.6 = (bf16[2048,256]{1,0:T(8,128)(2,1)S(1)}, bf16[2048,256]{1,0:T(8,128)(2,1)}, u32[]{:S(2)}) copy-start(bf16[2048,256]{1,0:T(8,128)(2,1)} %rest_5_.2) | copy-start | bytes 3145732
  0.9 9.4 %copy-start.7 = (bf16[2048]{0:T(1024)(128)(2,1)S(1)}, bf16[2048]{0:T(1024)(128)(2,1)}, u32[]{:S(2)}) copy-start(bf16[2048]{0:T(1024)(128)(2,1)} %gain.1) | copy-start | bytes 12292
  0.9 9.4 %copy-start.8 = (s32[4,4,2]{1,2,0:T(2,128)S(1)}, s32[4,4,2]{1,2,0:T(2,128)}, u32[]{:S(2)}) copy-start(s32[4,4,2]{1,2,0:T(2,128)} %param.21) | copy-start | bytes 388
  1.0 7.0 %collective-permute-start.2 = (f32[16,128]{1,0:T(8,128)S(1)}, f32[16,128]{1,0:T(8,128)S(1)}, u32[]{:S(2)}, u32[]{:S(2)}) collective-permute-start(f32[16,128]{1,0:T(8,128)S(1)} %square.1.rest_0_), channel_id=1, source_target_pairs={{0,4},{4,8},{8,12},{12,0},{1,5},{5,9},{9,13},{13,1},{2,6},{6,10},{... | collective-permute-start | bytes 24584 | tf_op jit(solution)/shard_map/ppermute | solution.py:253
  4.0 4.6 %collective-permute-start.1 = (f32[16,128]{1,0:T(8,128)S(1)}, f32[16,128]{1,0:T(8,128)S(1)}, u32[]{:S(2)}, u32[]{:S(2)}) collective-permute-start(f32[16,128]{1,0:T(8,128)S(1)} %square.1.rest_0_), channel_id=1, source_target_pairs={{0,8},{4,12},{8,0},{12,4},{1,9},{5,13},{9,1},{13,5},{2,10},{6,14},... | collective-permute-start | bytes 24584 | tf_op jit(solution)/shard_map/ppermute | solution.py:253
  6.6 3.7 %collective-permute-start = (f32[16,128]{1,0:T(8,128)S(1)}, f32[16,128]{1,0:T(8,128)S(1)}, u32[]{:S(2)}, u32[]{:S(2)}) collective-permute-start(f32[16,128]{1,0:T(8,128)S(1)} %square.1.rest_0_), channel_id=1, source_target_pairs={{0,12},{4,0},{8,4},{12,8},{1,13},{5,1},{9,5},{13,9},{2,14},{6,2},{... | collective-permute-start | bytes 24584 | tf_op jit(solution)/shard_map/ppermute | solution.py:253
  10.3 10.6 %copy-start.3 = (bf16[48,128,256]{2,1,0:T(8,128)(2,1)S(1)}, bf16[48,128,256]{2,1,0:T(8,128)(2,1)}, u32[]{:S(2)}) copy-start(bf16[48,128,256]{2,1,0:T(8,128)(2,1)} %rest_4_.4) | copy-start | bytes 9437188
  10.3 10.6 %copy-start.4 = (bf16[48,128,256]{2,1,0:T(8,128)(2,1)S(1)}, bf16[48,128,256]{2,1,0:T(8,128)(2,1)}, u32[]{:S(2)}) copy-start(bf16[48,128,256]{2,1,0:T(8,128)(2,1)} %rest_5_.3) | copy-start | bytes 9437188
  10.3 10.6 %copy-start.10 = (s32[48]{0:T(128)S(1)}, s32[48]{0:T(128)}, u32[]{:S(2)}) copy-start(s32[48]{0:T(128)} %slot_route.1) | copy-start | bytes 580
  10.3 10.6 %copy-start.11 = (s32[48]{0:T(128)S(1)}, s32[48]{0:T(128)}, u32[]{:S(2)}) copy-start(s32[48]{0:T(128)} %slot_block.1) | copy-start | bytes 580
  10.3 19.8 %slice-start = ((s8[8388608]{0:T(1024)(128)(4,1)}), s8[4194304]{0:T(1024)(128)(4,1)S(1)}, s32[]{:S(2)}) async-start(s8[8388608]{0:T(1024)(128)(4,1)} %bitcast.1), calls=%async_computation | async-start | bytes 8388608
  13.1 6.0 %collective-permute-start.5 = (f16[8,2560]{1,0:T(8,128)(2,1)S(1)}, f16[8,2560]{1,0:T(8,128)(2,1)S(1)}, u32[]{:S(2)}, u32[]{:S(2)}) collective-permute-start(f16[8,2560]{1,0:T(8,128)(2,1)S(1)} %multiply_convert_fusion), channel_id=1, source_target_pairs={{0,4},{4,8},{8,12},{12,0},{1,5},{5,9},{9,13},{13,1},{2,6},{6,10},{... | collective-permute-start | bytes 122888 | tf_op jit(solution)/shard_map/ppermute | solution.py:253
  13.3 6.5 %collective-permute-start.4 = (f16[8,2560]{1,0:T(8,128)(2,1)S(1)}, f16[8,2560]{1,0:T(8,128)(2,1)S(1)}, u32[]{:S(2)}, u32[]{:S(2)}) collective-permute-start(f16[8,2560]{1,0:T(8,128)(2,1)S(1)} %multiply_convert_fusion.1), channel_id=1, source_target_pairs={{0,8},{4,12},{8,0},{12,4},{1,9},{5,13},{9,1},{13,5},{2,10},{6,14},... | collective-permute-start | bytes 122888 | tf_op jit(solution)/shard_map/ppermute | solution.py:253
  16.9 4.0 %collective-permute-start.3 = (f16[8,2560]{1,0:T(8,128)(2,1)S(1)}, f16[8,2560]{1,0:T(8,128)(2,1)S(1)}, u32[]{:S(2)}, u32[]{:S(2)}) collective-permute-start(f16[8,2560]{1,0:T(8,128)(2,1)S(1)} %multiply_convert_fusion.2), channel_id=1, source_target_pairs={{0,12},{4,0},{8,4},{12,8},{1,13},{5,1},{9,5},{13,9},{2,14},{6,2},{... | collective-permute-start | bytes 122888 | tf_op jit(solution)/shard_map/ppermute | solution.py:253
  17.1 13.0 %slice-start.1 = ((s8[8388608]{0:T(1024)(128)(4,1)}), s8[4194304]{0:T(1024)(128)(4,1)S(1)}, s32[]{:S(2)}) async-start(s8[8388608]{0:T(1024)(128)(4,1)} %bitcast.1), calls=%async_computation.1 | async-start | bytes 8388608
  23.4 5.9 %collective-permute-start.8 = (bf16[9,16,128]{2,1,0:T(8,128)(2,1)S(1)}, bf16[9,16,128]{2,1,0:T(8,128)(2,1)S(1)}, u32[]{:S(2)}, u32[]{:S(2)}) collective-permute-start(bf16[9,16,128]{2,1,0:T(8,128)(2,1)S(1)} %attend.1.rest_0_), channel_id=1, source_target_pairs={{0,4},{4,8},{8,12},{12,0},{1,5},{5,9},{9,13},{13,1},{2,6},{6,10},{... | collective-permute-start | bytes 110600 | tf_op jit(solution)/shard_map/ppermute | solution.py:253
  24.1 5.6 %collective-permute-start.7 = (bf16[9,16,128]{2,1,0:T(8,128)(2,1)S(1)}, bf16[9,16,128]{2,1,0:T(8,128)(2,1)S(1)}, u32[]{:S(2)}, u32[]{:S(2)}) collective-permute-start(bf16[9,16,128]{2,1,0:T(8,128)(2,1)S(1)} %attend.1.rest_0_), channel_id=1, source_target_pairs={{0,8},{4,12},{8,0},{12,4},{1,9},{5,13},{9,1},{13,5},{2,10},{6,14},... | collective-permute-start | bytes 110600 | tf_op jit(solution)/shard_map/ppermute | solution.py:253
  26.2 4.0 %collective-permute-start.6 = (bf16[9,16,128]{2,1,0:T(8,128)(2,1)S(1)}, bf16[9,16,128]{2,1,0:T(8,128)(2,1)S(1)}, u32[]{:S(2)}, u32[]{:S(2)}) collective-permute-start(bf16[9,16,128]{2,1,0:T(8,128)(2,1)S(1)} %attend.1.rest_0_), channel_id=1, source_target_pairs={{0,12},{4,0},{8,4},{12,8},{1,13},{5,1},{9,5},{13,9},{2,14},{6,2},{... | collective-permute-start | bytes 110600 | tf_op jit(solution)/shard_map/ppermute | solution.py:253
  32.4 4.3 %collective-permute-start.10 = (bf16[16,2048]{1,0:T(8,128)(2,1)S(1)}, bf16[16,2048]{1,0:T(8,128)(2,1)S(1)}, u32[]{:S(2)}, u32[]{:S(2)}) collective-permute-start(bf16[16,2048]{1,0:T(8,128)(2,1)S(1)} %convert_element_type.50), channel_id=1, source_target_pairs={{0,2},{1,3},{2,0},{3,1},{4,6},{5,7},{6,4},{7,5},{8,10},{9,11},{10,... | collective-permute-start | bytes 196616 | tf_op jit(solution)/shard_map/ppermute | solution.py:358
  34.0 2.8 %collective-permute-start.9 = (bf16[16,2048]{1,0:T(8,128)(2,1)S(1)}, bf16[16,2048]{1,0:T(8,128)(2,1)S(1)}, u32[]{:S(2)}, u32[]{:S(2)}) collective-permute-start(bf16[16,2048]{1,0:T(8,128)(2,1)S(1)} %convert_element_type.50), channel_id=1, source_target_pairs={{0,1},{1,0},{2,3},{3,2},{4,5},{5,4},{6,7},{7,6},{8,9},{9,8},{10,11... | collective-permute-start | bytes 196616 | tf_op jit(solution)/shard_map/ppermute | solution.py:358
  34.0 3.7 %collective-permute-start.11 = (bf16[16,2048]{1,0:T(8,128)(2,1)S(1)}, bf16[16,2048]{1,0:T(8,128)(2,1)S(1)}, u32[]{:S(2)}, u32[]{:S(2)}) collective-permute-start(bf16[16,2048]{1,0:T(8,128)(2,1)S(1)} %convert_element_type.50), channel_id=1, source_target_pairs={{0,3},{1,2},{2,1},{3,0},{4,7},{5,6},{6,5},{7,4},{8,11},{9,10},{10,... | collective-permute-start | bytes 196616 | tf_op jit(solution)/shard_map/ppermute | solution.py:358
  (2 other events, 3.6 us)

commit v6 on v5

--- a/solution.py
+++ b/solution.py
@@ -32,32 +32,40 @@
     )
 
 
-def project_kernel(pool_count, routes, residual, gain, *rest):
-    squares, rest = rest[:pool_count], rest[pool_count:]
-    weights, outs = rest[:3], rest[3:]
-    listed = outs[0].shape[0]
+def pick_kernel(pool_count, listed, routes, residual, after, out, pick):
     requests = residual.shape[0]
     rows = pool_count * listed
     me = lax.axis_index("pool")
-    total = squares[0][...]
-    for part in squares[1:]:
-        total = total + part[...]
-    scale = lax.rsqrt(total[:, :1] / D + EPSILON)
-    resid_f = residual[...].astype(jnp.float32)
-    normed = resid_f * scale * gain[...].astype(jnp.float32)[None, :]
-    row_ids = lax.broadcasted_iota(jnp.int32, (rows, requests), 0)
-    column_ids = lax.broadcasted_iota(jnp.int32, (rows, requests), 1)
-    wanted = jnp.zeros((rows, requests), jnp.int32)
+    row_ids = lax.broadcasted_iota(jnp.int32, (rows, HD), 0)
+    wanted = jnp.zeros((rows, HD), jnp.int32)
     for shift in range(pool_count):
         owner = lax.rem(me + shift, pool_count)
         for row in range(listed):
             wanted = jnp.where(
                 row_ids == shift * listed + row, listed_at(routes, owner, row), wanted
             )
-    pick = (column_ids == wanted).astype(jnp.float32).astype(jnp.bfloat16)
-    picked = jnp.dot(
-        pick, normed.astype(jnp.bfloat16), preferred_element_type=jnp.float32
-    ).astype(jnp.bfloat16)
+    chosen = (lax.broadcasted_iota(jnp.int32, (rows, HD), 1) == wanted).astype(jnp.float32)
+    pick[...] = chosen
+    out[...] = jnp.dot(
+        chosen[:, :requests].astype(jnp.bfloat16),
+        residual[...],
+        preferred_element_type=jnp.float32,
+    )
+
+
+def project_kernel(pool_count, residual, pick, gain, *rest):
+    squares, rest = rest[:pool_count], rest[pool_count:]
+    weights, outs = rest[:3], rest[3:]
+    listed = outs[0].shape[0]
+    total = squares[0][...]
+    for part in squares[1:]:
+        total = total + part[...]
+    ids = [lax.broadcasted_iota(jnp.int32, total.shape, axis) for axis in range(2)]
+    scale = jnp.where(ids[0] == ids[1], lax.rsqrt(total / D + EPSILON), 0.0)
+    scale = jnp.sum(scale, axis=0, keepdims=True)
+    scale = jnp.sum(pick[...] * scale, axis=1, keepdims=True)
+    normed = residual[...] * scale * gain[...].astype(jnp.float32)[None, :]
+    picked = normed.astype(jnp.bfloat16)
     place = 0
     for source in weights:
         for first in range(0, source.shape[1], CHUNK):
@@ -245,7 +253,7 @@
 
 
 def shifts(pool_count):
-    return range(pool_count - 1, 0, -1)
+    return range(1, pool_count)
 
 
 def shifted(value, axis, shift):
@@ -294,20 +302,33 @@
         cost_estimate=spell,
         name="square",
     )(residual)
+    rows = pool_count * listed
+    picked, pick = pl.pallas_call(
+        functools.partial(pick_kernel, pool_count, listed),
+        out_shape=[
+            jax.ShapeDtypeStruct((rows, depth), f32),
+            jax.ShapeDtypeStruct((rows, HD), f32),
+        ],
+        in_specs=[in_smem, in_vmem, in_vmem],
+        out_specs=[in_vmem] * 2,
+        compiler_params=pltpu.CompilerParams(vmem_limit_bytes=4 * 2**20),
+        cost_estimate=spell,
+        name="pick",
+    )(routes, residual, squares)
     sent = pl.pallas_call(
         functools.partial(project_kernel, pool_count),
         out_shape=[jax.ShapeDtypeStruct((listed, width), f32)] * pool_count,
-        in_specs=[in_smem] + [in_vmem] * (pool_count + 5),
+        in_specs=[in_vmem] * (pool_count + 6),
         out_specs=[in_vmem] * pool_count,
         compiler_params=pltpu.CompilerParams(vmem_limit_bytes=8 * 2**20),
         cost_estimate=spell,
         name="project",
     )(
-        routes,
-        residual,
+        picked,
+        pick,
         norm_gain,
         squares,
-        *[shifted(squares, "pool", shift) for shift in shifts(pool_count)],
+        *[shifted(squares, "pool", shift) for shift in range(1, pool_count)],
         pin(w_key),
         pin(w_value),
         pin(w_query),

time: 38.6 us -> 38.6 us (level)
  waiting for transfers between devices: 11.9 us -> 11.3 us
  local copies, waits for them, and re-layouts: 0.91 us -> 1.4 us
    ppermute x9, waiting for transfers between devices: 8.82 us -> 7.76 us  [shifted(): lax.ppermute(value, axis, [(i, (i + shift) % count) for i in range(count)])]
    pallas_call x0 -> x1, Pallas kernels: none -> 0.78 us  [close_pool(): pl.pallas_call(functools.partial(pick_kernel, pool_count, listed), out_sh...]
    pallas_call x1, Pallas kernels: 2.7 us -> 1.99 us  [close_pool(): pl.pallas_call(functools.partial(project_kernel, pool_count), out_shape=[...]
    unnamed x28 -> x30, local copies, waits for them, and re-layouts: 0.91 us -> 1.4 us
    ppermute x3, waiting for transfers between devices: 3.09 us -> 3.53 us  [close_pool(): lax.ppermute(product, 'tensor', [(i, i ^ d) for i in range(tensor_count)])]
  transfers between devices with their start and end apart: 12 -> 12, of which waited for: 10 -> 9; matrix products, arithmetic and copies ran while one was open for 1% -> 1% of each run, Pallas kernels for 0% -> 2%
where the time goes in v6:
time: 38.6 us; the launch traced here: 38.4 us
  starting transfers between devices  17.1 us (44%)
  waiting for transfers between devices  11.3 us (29%)
  Pallas kernels  7.53 us (20%)
  local copies, waits for them, and re-layouts  1.4 us (4%)
  other arithmetic  0.95 us (2%)
    ppermute x9, starting transfers between devices, shifted(): lax.ppermute(value, axis, [(i, (i + shift) % count) for i in range(count)])  14.9 us
    ppermute x9, waiting for transfers between devices, shifted(): lax.ppermute(value, axis, [(i, (i + shift) % count) for i in range(count)])  7.76 us
    ppermute x3, waiting for transfers between devices, close_pool(): lax.ppermute(product, 'tensor', [(i, i ^ d) for i in range(tensor_count)])  3.53 us
    pallas_call x1, Pallas kernels, close_pool(): pl.pallas_call(functools.partial(attend_kernel, pool_count, local_kv, gro...  2.41 us
    pallas_call x1, Pallas kernels, close_pool(): pl.pallas_call(functools.partial(merge_kernel, pool_count), out_shape=jax...  2.26 us
    ppermute x3, starting transfers between devices, close_pool(): lax.ppermute(product, 'tensor', [(i, i ^ d) for i in range(tensor_count)])  2.21 us
    pallas_call x1, Pallas kernels, close_pool(): pl.pallas_call(functools.partial(project_kernel, pool_count), out_shape=[...  1.99 us
    unnamed x30, local copies, waits for them, and re-layouts  1.4 us
  transfers between devices with their start and end apart: 12, of which 9 were waited for; matrix products, arithmetic and copies ran while one was open for 1% of the time, Pallas kernels for 2%

profile of v6, /device:TPU:0, one launch (start us, length us, event | category | flops | bytes accessed | tf_op | source)
XLA Modules:
  0.0 38.4 jit_solution(6528182056864774355)
XLA Ops:
  0.0 0.8 %copy-done = bf16[16,2048]{1,0:T(8,128)(2,1)S(1)} copy-done((bf16[16,2048]{1,0:T(8,128)(2,1)S(1)}, bf16[16,2048]{1,0:T(8,128)(2,1)}, u32[]{:S(2)}) %copy-start) | copy-done | bytes 65560
  0.9 3.0 %collective-permute-start = (f32[16,128]{1,0:T(8,128)S(1)}, f32[16,128]{1,0:T(8,128)S(1)}, u32[]{:S(2)}, u32[]{:S(2)}) collective-permute-start(f32[16,128]{1,0:T(8,128)S(1)} %square.1.after.rest_0_), channel_id=1, source_target_pairs={{0,4},{4,8},{8,12},{12,0},{1,5},{5,9},{9,13},{13,1},{2,6},{6,10},{... | collective-permute-start | bytes 24584 | tf_op jit(solution)/shard_map/ppermute | solution.py:261
  4.0 2.6 %collective-permute-start.1 = (f32[16,128]{1,0:T(8,128)S(1)}, f32[16,128]{1,0:T(8,128)S(1)}, u32[]{:S(2)}, u32[]{:S(2)}) collective-permute-start(f32[16,128]{1,0:T(8,128)S(1)} %square.1.after.rest_0_), channel_id=1, source_target_pairs={{0,8},{4,12},{8,0},{12,4},{1,9},{5,13},{9,1},{13,5},{2,10},{6,14},... | collective-permute-start | bytes 24584 | tf_op jit(solution)/shard_map/ppermute | solution.py:261
  6.6 1.3 %collective-permute-start.2 = (f32[16,128]{1,0:T(8,128)S(1)}, f32[16,128]{1,0:T(8,128)S(1)}, u32[]{:S(2)}, u32[]{:S(2)}) collective-permute-start(f32[16,128]{1,0:T(8,128)S(1)} %square.1.after.rest_0_), channel_id=1, source_target_pairs={{0,12},{4,0},{8,4},{12,8},{1,13},{5,1},{9,5},{13,9},{2,14},{6,2},{... | collective-permute-start | bytes 24584 | tf_op jit(solution)/shard_map/ppermute | solution.py:261
  7.9 0.8 %pick.1 = (f32[32,2048]{1,0:T(8,128)S(1)}, f32[32,128]{1,0:T(8,128)S(1)}) custom-call(s32[4,2,4]{2,1,0:T(2,128)S(1)} %bitcast.5, bf16[16,2048]{1,0:T(8,128)(2,1)S(1)} %copy-done, f32[16,128]{1,0:T(8,128)S(1)} %square.1.after.rest_0_), custom_call_target="tpu_custom_call" | custom-call | flops 17179869184 | bytes 33554432 | tf_op jit(solution)/shard_map/pick/pallas_call | solution.py:306
  8.7 1.5 %collective-permute-done.2.rest_3_ = f32[16,128]{1,0:T(8,128)S(1)} collective-permute-done((f32[16,128]{1,0:T(8,128)S(1)}, f32[16,128]{1,0:T(8,128)S(1)}, u32[]{:S(2)}, u32[]{:S(2)}) %collective-permute-start.2) | collective-permute-done | bytes 8224 | tf_op jit(solution)/shard_map/ppermute | solution.py:261
  10.8 2.0 %project.1 = (f32[8,2560]{1,0:T(8,128)S(1)}, f32[8,2560]{1,0:T(8,128)S(1)}, f32[8,2560]{1,0:T(8,128)S(1)}, f32[8,2560]{1,0:T(8,128)S(1)}) custom-call(f32[32,2048]{1,0:T(8,128)S(1)} %get-tuple-element.12.residual, f32[32,128]{1,0:T(8,128)S(1)} %get-tuple-element.13.pick, bf16[2048]{0:T(1024)(128)(2,1)S(1)} %copy-done.6, f32[16,128]{1,0:T(8,128)S(1)} %square.1.after.rest_0_, ...), custom_call_target="tpu_custom_call" | custom-call | flops 17179869184 | bytes 33554432 | tf_op jit(solution)/shard_map/project/pallas_call | solution.py:318
  12.8 0.7 %collective-permute-start.3 = (f16[8,2560]{1,0:T(8,128)(2,1)S(1)}, f16[8,2560]{1,0:T(8,128)(2,1)S(1)}, u32[]{:S(2)}, u32[]{:S(2)}) collective-permute-start(f16[8,2560]{1,0:T(8,128)(2,1)S(1)} %multiply_convert_fusion.2), channel_id=1, source_target_pairs={{0,4},{4,8},{8,12},{12,0},{1,5},{5,9},{9,13},{13,1},{2,6},{6,10},{... | collective-permute-start | bytes 122888 | tf_op jit(solution)/shard_map/ppermute | solution.py:261
  13.5 2.7 %collective-permute-start.4 = (f16[8,2560]{1,0:T(8,128)(2,1)S(1)}, f16[8,2560]{1,0:T(8,128)(2,1)S(1)}, u32[]{:S(2)}, u32[]{:S(2)}) collective-permute-start(f16[8,2560]{1,0:T(8,128)(2,1)S(1)} %multiply_convert_fusion.1), channel_id=1, source_target_pairs={{0,8},{4,12},{8,0},{12,4},{1,9},{5,13},{9,1},{13,5},{2,10},{6,14},... | collective-permute-start | bytes 122888 | tf_op jit(solution)/shard_map/ppermute | solution.py:261
  17.0 1.7 %collective-permute-done.3 = f16[8,2560]{1,0:T(8,128)(2,1)S(1)} collective-permute-done((f16[8,2560]{1,0:T(8,128)(2,1)S(1)}, f16[8,2560]{1,0:T(8,128)(2,1)S(1)}, u32[]{:S(2)}, u32[]{:S(2)}) %collective-permute-start.3) | collective-permute-done | bytes 40992 | tf_op jit(solution)/shard_map/ppermute | solution.py:261
  18.7 0.8 %collective-permute-done.4 = f16[8,2560]{1,0:T(8,128)(2,1)S(1)} collective-permute-done((f16[8,2560]{1,0:T(8,128)(2,1)S(1)}, f16[8,2560]{1,0:T(8,128)(2,1)S(1)}, u32[]{:S(2)}, u32[]{:S(2)}) %collective-permute-start.4) | collective-permute-done | bytes 40992 | tf_op jit(solution)/shard_map/ppermute | solution.py:261
  19.6 0.7 %collective-permute-done.5 = f16[8,2560]{1,0:T(8,128)(2,1)S(1)} collective-permute-done((f16[8,2560]{1,0:T(8,128)(2,1)S(1)}, f16[8,2560]{1,0:T(8,128)(2,1)S(1)}, u32[]{:S(2)}, u32[]{:S(2)}) %collective-permute-start.5) | collective-permute-done | bytes 40992 | tf_op jit(solution)/shard_map/ppermute | solution.py:261
  20.3 2.4 %attend.1.rest_0_ = bf16[9,16,128]{2,1,0:T(8,128)(2,1)S(1)} custom-call(s32[4,2,4]{2,1,0:T(2,128)S(1)} %bitcast.6, s32[16]{0:T(128)S(1)} %copy-done.8, s32[48]{0:T(128)S(1)} %copy-done.9, s32[48]{0:T(128)S(1)} %copy-done.10, f32[16,256]{1,0:T(8,128)S(1)} %pad_maximum_fusion.turn, f32[8,2560]{1,0:T(8,128)S(1)} %get-tuple-element.14.rest_0_, ...), custom_call_target="tpu_custom_call" | custom-call | flops 17179869184 | bytes 33554432 | tf_op jit(solution)/shard_map/attend/pallas_call | solution.py:345
  22.7 1.2 %collective-permute-start.6 = (bf16[9,16,128]{2,1,0:T(8,128)(2,1)S(1)}, bf16[9,16,128]{2,1,0:T(8,128)(2,1)S(1)}, u32[]{:S(2)}, u32[]{:S(2)}) collective-permute-start(bf16[9,16,128]{2,1,0:T(8,128)(2,1)S(1)} %attend.1.rest_0_), channel_id=1, source_target_pairs={{0,4},{4,8},{8,12},{12,0},{1,5},{5,9},{9,13},{13,1},{2,6},{6,10},{... | collective-permute-start | bytes 110600 | tf_op jit(solution)/shard_map/ppermute | solution.py:261
  23.9 1.8 %collective-permute-start.7 = (bf16[9,16,128]{2,1,0:T(8,128)(2,1)S(1)}, bf16[9,16,128]{2,1,0:T(8,128)(2,1)S(1)}, u32[]{:S(2)}, u32[]{:S(2)}) collective-permute-start(bf16[9,16,128]{2,1,0:T(8,128)(2,1)S(1)} %attend.1.rest_0_), channel_id=1, source_target_pairs={{0,8},{4,12},{8,0},{12,4},{1,9},{5,13},{9,1},{13,5},{2,10},{6,14},... | collective-permute-start | bytes 110600 | tf_op jit(solution)/shard_map/ppermute | solution.py:261
  25.7 0.9 %collective-permute-start.8 = (bf16[9,16,128]{2,1,0:T(8,128)(2,1)S(1)}, bf16[9,16,128]{2,1,0:T(8,128)(2,1)S(1)}, u32[]{:S(2)}, u32[]{:S(2)}) collective-permute-start(bf16[9,16,128]{2,1,0:T(8,128)(2,1)S(1)} %attend.1.rest_0_), channel_id=1, source_target_pairs={{0,12},{4,0},{8,4},{12,8},{1,13},{5,1},{9,5},{13,9},{2,14},{6,2},{... | collective-permute-start | bytes 110600 | tf_op jit(solution)/shard_map/ppermute | solution.py:261
  26.6 1.9 %collective-permute-done.6.rest_1_ = bf16[9,16,128]{2,1,0:T(8,128)(2,1)S(1)} collective-permute-done((bf16[9,16,128]{2,1,0:T(8,128)(2,1)S(1)}, bf16[9,16,128]{2,1,0:T(8,128)(2,1)S(1)}, u32[]{:S(2)}, u32[]{:S(2)}) %collective-permute-start.6) | collective-permute-done | bytes 36896 | tf_op jit(solution)/shard_map/ppermute | solution.py:261
  28.6 0.8 %collective-permute-done.7.rest_2_ = bf16[9,16,128]{2,1,0:T(8,128)(2,1)S(1)} collective-permute-done((bf16[9,16,128]{2,1,0:T(8,128)(2,1)S(1)}, bf16[9,16,128]{2,1,0:T(8,128)(2,1)S(1)}, u32[]{:S(2)}, u32[]{:S(2)}) %collective-permute-start.7) | collective-permute-done | bytes 36896 | tf_op jit(solution)/shard_map/ppermute | solution.py:261
  29.7 2.3 %merge.1 = f32[16,2048]{1,0:T(8,128)S(1)} custom-call(s32[4,2,4]{2,1,0:T(2,128)S(1)} %bitcast.7, bf16[9,16,128]{2,1,0:T(8,128)(2,1)S(1)} %attend.1.rest_0_, bf16[9,16,128]{2,1,0:T(8,128)(2,1)S(1)} %collective-permute-done.6.rest_1_, bf16[9,16,128]{2,1,0:T(8,128)(2,1)S(1)} %collective-permute-done.7.rest_2_, ...), custom_call_target="tpu_custom_call" | custom-call | flops 17179869184 | bytes 33554432 | tf_op jit(solution)/shard_map/merge/pallas_call | solution.py:366
  32.0 1.6 %collective-permute-start.10 = (bf16[16,2048]{1,0:T(8,128)(2,1)S(1)}, bf16[16,2048]{1,0:T(8,128)(2,1)S(1)}, u32[]{:S(2)}, u32[]{:S(2)}) collective-permute-start(bf16[16,2048]{1,0:T(8,128)(2,1)S(1)} %convert_element_type.50), channel_id=1, source_target_pairs={{0,2},{1,3},{2,0},{3,1},{4,6},{5,7},{6,4},{7,5},{8,10},{9,11},{10,... | collective-permute-start | bytes 196616 | tf_op jit(solution)/shard_map/ppermute | solution.py:379
  33.6 0.6 %collective-permute-start.9 = (bf16[16,2048]{1,0:T(8,128)(2,1)S(1)}, bf16[16,2048]{1,0:T(8,128)(2,1)S(1)}, u32[]{:S(2)}, u32[]{:S(2)}) collective-permute-start(bf16[16,2048]{1,0:T(8,128)(2,1)S(1)} %convert_element_type.50), channel_id=1, source_target_pairs={{0,1},{1,0},{2,3},{3,2},{4,5},{5,4},{6,7},{7,6},{8,9},{9,8},{10,11... | collective-permute-start | bytes 196616 | tf_op jit(solution)/shard_map/ppermute | solution.py:379
  34.2 2.1 %collective-permute-done.10 = bf16[16,2048]{1,0:T(8,128)(2,1)S(1)} collective-permute-done((bf16[16,2048]{1,0:T(8,128)(2,1)S(1)}, bf16[16,2048]{1,0:T(8,128)(2,1)S(1)}, u32[]{:S(2)}, u32[]{:S(2)}) %collective-permute-start.10) | collective-permute-done | bytes 65568 | tf_op jit(solution)/shard_map/ppermute | solution.py:379
  36.4 1.4 %collective-permute-done.11 = bf16[16,2048]{1,0:T(8,128)(2,1)S(1)} collective-permute-done((bf16[16,2048]{1,0:T(8,128)(2,1)S(1)}, bf16[16,2048]{1,0:T(8,128)(2,1)S(1)}, u32[]{:S(2)}, u32[]{:S(2)}) %collective-permute-start.11) | collective-permute-done | bytes 65568 | tf_op jit(solution)/shard_map/ppermute | solution.py:379
  37.8 0.7 %add_convert_fusion = bf16[16,2048]{1,0:T(8,128)(2,1)} fusion(bf16[16,2048]{1,0:T(8,128)(2,1)S(1)} %collective-permute-done.11, bf16[16,2048]{1,0:T(8,128)(2,1)S(1)} %collective-permute-done.10, bf16[16,2048]{1,0:T(8,128)(2,1)S(1)} %collective-permute-done.9, bf16[16,2048]{1,0:T(8,128)(2,1)S(1)} %copy-done.1, f32[16,2048]{1,0:T(8,128)S(1)} %merge.1), kind=kLoop, calls=%fused_computation | loop fusion | flops 360448 | bytes 458752 | tf_op jit(solution)/shard_map/convert_element_type | solution.py:383
  (49 shorter events, 2.0 us)
Async XLA Ops:
  0.8 7.1 %copy-start.7 = (s32[4,4,2]{1,2,0:T(2,128)S(1)}, s32[4,4,2]{1,2,0:T(2,128)}, u32[]{:S(2)}) copy-start(s32[4,4,2]{1,2,0:T(2,128)} %param.21) | copy-start | bytes 388
  0.8 9.4 %slice-start = ((s8[8388608]{0:T(1024)(128)(4,1)}), s8[4194304]{0:T(1024)(128)(4,1)S(1)}, s32[]{:S(2)}) async-start(s8[8388608]{0:T(1024)(128)(4,1)} %bitcast.1), calls=%async_computation | async-start | bytes 8388608
  0.9 7.8 %collective-permute-start = (f32[16,128]{1,0:T(8,128)S(1)}, f32[16,128]{1,0:T(8,128)S(1)}, u32[]{:S(2)}, u32[]{:S(2)}) collective-permute-start(f32[16,128]{1,0:T(8,128)S(1)} %square.1.after.rest_0_), channel_id=1, source_target_pairs={{0,4},{4,8},{8,12},{12,0},{1,5},{5,9},{9,13},{13,1},{2,6},{6,10},{... | collective-permute-start | bytes 24584 | tf_op jit(solution)/shard_map/ppermute | solution.py:261
  4.0 4.8 %collective-permute-start.1 = (f32[16,128]{1,0:T(8,128)S(1)}, f32[16,128]{1,0:T(8,128)S(1)}, u32[]{:S(2)}, u32[]{:S(2)}) collective-permute-start(f32[16,128]{1,0:T(8,128)S(1)} %square.1.after.rest_0_), channel_id=1, source_target_pairs={{0,8},{4,12},{8,0},{12,4},{1,9},{5,13},{9,1},{13,5},{2,10},{6,14},... | collective-permute-start | bytes 24584 | tf_op jit(solution)/shard_map/ppermute | solution.py:261
  6.6 3.7 %collective-permute-start.2 = (f32[16,128]{1,0:T(8,128)S(1)}, f32[16,128]{1,0:T(8,128)S(1)}, u32[]{:S(2)}, u32[]{:S(2)}) collective-permute-start(f32[16,128]{1,0:T(8,128)S(1)} %square.1.after.rest_0_), channel_id=1, source_target_pairs={{0,12},{4,0},{8,4},{12,8},{1,13},{5,1},{9,5},{13,9},{2,14},{6,2},{... | collective-permute-start | bytes 24584 | tf_op jit(solution)/shard_map/ppermute | solution.py:261
  7.9 2.5 %copy-start.4 = (bf16[2048,256]{1,0:T(8,128)(2,1)S(1)}, bf16[2048,256]{1,0:T(8,128)(2,1)}, u32[]{:S(2)}) copy-start(bf16[2048,256]{1,0:T(8,128)(2,1)} %rest_4_.3) | copy-start | bytes 3145732
  7.9 2.8 %copy-start.5 = (bf16[2048,256]{1,0:T(8,128)(2,1)S(1)}, bf16[2048,256]{1,0:T(8,128)(2,1)}, u32[]{:S(2)}) copy-start(bf16[2048,256]{1,0:T(8,128)(2,1)} %rest_5_.2) | copy-start | bytes 3145732
  7.9 2.8 %copy-start.6 = (bf16[2048]{0:T(1024)(128)(2,1)S(1)}, bf16[2048]{0:T(1024)(128)(2,1)}, u32[]{:S(2)}) copy-start(bf16[2048]{0:T(1024)(128)(2,1)} %gain.1) | copy-start | bytes 12292
  10.7 9.6 %copy-start.2 = (bf16[48,128,256]{2,1,0:T(8,128)(2,1)S(1)}, bf16[48,128,256]{2,1,0:T(8,128)(2,1)}, u32[]{:S(2)}) copy-start(bf16[48,128,256]{2,1,0:T(8,128)(2,1)} %rest_4_.4) | copy-start | bytes 9437188
  10.7 9.6 %copy-start.3 = (bf16[48,128,256]{2,1,0:T(8,128)(2,1)S(1)}, bf16[48,128,256]{2,1,0:T(8,128)(2,1)}, u32[]{:S(2)}) copy-start(bf16[48,128,256]{2,1,0:T(8,128)(2,1)} %rest_5_.3) | copy-start | bytes 9437188
  10.7 9.6 %copy-start.9 = (s32[48]{0:T(128)S(1)}, s32[48]{0:T(128)}, u32[]{:S(2)}) copy-start(s32[48]{0:T(128)} %slot_route.1) | copy-start | bytes 580
  10.7 9.6 %copy-start.10 = (s32[48]{0:T(128)S(1)}, s32[48]{0:T(128)}, u32[]{:S(2)}) copy-start(s32[48]{0:T(128)} %slot_block.1) | copy-start | bytes 580
  10.7 19.0 %slice-start.2 = ((s8[8388608]{0:T(1024)(128)(4,1)}), s8[4194304]{0:T(1024)(128)(4,1)S(1)}, s32[]{:S(2)}) async-start(s8[8388608]{0:T(1024)(128)(4,1)} %bitcast.3), calls=%async_computation.2 | async-start | bytes 8388608
  12.8 6.0 %collective-permute-start.3 = (f16[8,2560]{1,0:T(8,128)(2,1)S(1)}, f16[8,2560]{1,0:T(8,128)(2,1)S(1)}, u32[]{:S(2)}, u32[]{:S(2)}) collective-permute-start(f16[8,2560]{1,0:T(8,128)(2,1)S(1)} %multiply_convert_fusion.2), channel_id=1, source_target_pairs={{0,4},{4,8},{8,12},{12,0},{1,5},{5,9},{9,13},{13,1},{2,6},{6,10},{... | collective-permute-start | bytes 122888 | tf_op jit(solution)/shard_map/ppermute | solution.py:261
  13.5 6.1 %collective-permute-start.4 = (f16[8,2560]{1,0:T(8,128)(2,1)S(1)}, f16[8,2560]{1,0:T(8,128)(2,1)S(1)}, u32[]{:S(2)}, u32[]{:S(2)}) collective-permute-start(f16[8,2560]{1,0:T(8,128)(2,1)S(1)} %multiply_convert_fusion.1), channel_id=1, source_target_pairs={{0,8},{4,12},{8,0},{12,4},{1,9},{5,13},{9,1},{13,5},{2,10},{6,14},... | collective-permute-start | bytes 122888 | tf_op jit(solution)/shard_map/ppermute | solution.py:261
  16.2 4.1 %collective-permute-start.5 = (f16[8,2560]{1,0:T(8,128)(2,1)S(1)}, f16[8,2560]{1,0:T(8,128)(2,1)S(1)}, u32[]{:S(2)}, u32[]{:S(2)}) collective-permute-start(f16[8,2560]{1,0:T(8,128)(2,1)S(1)} %multiply_convert_fusion), channel_id=1, source_target_pairs={{0,12},{4,0},{8,4},{12,8},{1,13},{5,1},{9,5},{13,9},{2,14},{6,2},{... | collective-permute-start | bytes 122888 | tf_op jit(solution)/shard_map/ppermute | solution.py:261
  16.9 12.8 %slice-start.3 = ((s8[8388608]{0:T(1024)(128)(4,1)}), s8[4194304]{0:T(1024)(128)(4,1)S(1)}, s32[]{:S(2)}) async-start(s8[8388608]{0:T(1024)(128)(4,1)} %bitcast.3), calls=%async_computation.3 | async-start | bytes 8388608
  22.7 15.0 %copy-start.1 = (bf16[16,2048]{1,0:T(8,128)(2,1)S(1)}, bf16[16,2048]{1,0:T(8,128)(2,1)}, u32[]{:S(2)}) copy-start(bf16[16,2048]{1,0:T(8,128)(2,1)} %residual.3) | copy-start | bytes 196612
  22.7 5.8 %collective-permute-start.6 = (bf16[9,16,128]{2,1,0:T(8,128)(2,1)S(1)}, bf16[9,16,128]{2,1,0:T(8,128)(2,1)S(1)}, u32[]{:S(2)}, u32[]{:S(2)}) collective-permute-start(bf16[9,16,128]{2,1,0:T(8,128)(2,1)S(1)} %attend.1.rest_0_), channel_id=1, source_target_pairs={{0,4},{4,8},{8,12},{12,0},{1,5},{5,9},{9,13},{13,1},{2,6},{6,10},{... | collective-permute-start | bytes 110600 | tf_op jit(solution)/shard_map/ppermute | solution.py:261
  23.9 5.4 %collective-permute-start.7 = (bf16[9,16,128]{2,1,0:T(8,128)(2,1)S(1)}, bf16[9,16,128]{2,1,0:T(8,128)(2,1)S(1)}, u32[]{:S(2)}, u32[]{:S(2)}) collective-permute-start(bf16[9,16,128]{2,1,0:T(8,128)(2,1)S(1)} %attend.1.rest_0_), channel_id=1, source_target_pairs={{0,8},{4,12},{8,0},{12,4},{1,9},{5,13},{9,1},{13,5},{2,10},{6,14},... | collective-permute-start | bytes 110600 | tf_op jit(solution)/shard_map/ppermute | solution.py:261
  25.7 4.0 %collective-permute-start.8 = (bf16[9,16,128]{2,1,0:T(8,128)(2,1)S(1)}, bf16[9,16,128]{2,1,0:T(8,128)(2,1)S(1)}, u32[]{:S(2)}, u32[]{:S(2)}) collective-permute-start(bf16[9,16,128]{2,1,0:T(8,128)(2,1)S(1)} %attend.1.rest_0_), channel_id=1, source_target_pairs={{0,12},{4,0},{8,4},{12,8},{1,13},{5,1},{9,5},{13,9},{2,14},{6,2},{... | collective-permute-start | bytes 110600 | tf_op jit(solution)/shard_map/ppermute | solution.py:261
  32.0 4.3 %collective-permute-start.10 = (bf16[16,2048]{1,0:T(8,128)(2,1)S(1)}, bf16[16,2048]{1,0:T(8,128)(2,1)S(1)}, u32[]{:S(2)}, u32[]{:S(2)}) collective-permute-start(bf16[16,2048]{1,0:T(8,128)(2,1)S(1)} %convert_element_type.50), channel_id=1, source_target_pairs={{0,2},{1,3},{2,0},{3,1},{4,6},{5,7},{6,4},{7,5},{8,10},{9,11},{10,... | collective-permute-start | bytes 196616 | tf_op jit(solution)/shard_map/ppermute | solution.py:379
  33.6 4.2 %collective-permute-start.11 = (bf16[16,2048]{1,0:T(8,128)(2,1)S(1)}, bf16[16,2048]{1,0:T(8,128)(2,1)S(1)}, u32[]{:S(2)}, u32[]{:S(2)}) collective-permute-start(bf16[16,2048]{1,0:T(8,128)(2,1)S(1)} %convert_element_type.50), channel_id=1, source_target_pairs={{0,3},{1,2},{2,1},{3,0},{4,7},{5,6},{6,5},{7,4},{8,11},{9,10},{10,... | collective-permute-start | bytes 196616 | tf_op jit(solution)/shard_map/ppermute | solution.py:379
  33.6 4.2 %collective-permute-start.9 = (bf16[16,2048]{1,0:T(8,128)(2,1)S(1)}, bf16[16,2048]{1,0:T(8,128)(2,1)S(1)}, u32[]{:S(2)}, u32[]{:S(2)}) collective-permute-start(bf16[16,2048]{1,0:T(8,128)(2,1)S(1)} %convert_element_type.50), channel_id=1, source_target_pairs={{0,1},{1,0},{2,3},{3,2},{4,5},{5,4},{6,7},{7,6},{8,9},{9,8},{10,11... | collective-permute-start | bytes 196616 | tf_op jit(solution)/shard_map/ppermute | solution.py:379
  (3 other events, 5.2 us)

commit v7 on v6

--- a/solution.py
+++ b/solution.py
@@ -249,7 +249,7 @@
     for first in range(0, out.shape[1], CHUNK):
         out[:, first : first + CHUNK] = jnp.dot(
             attention, w_out[:, first : first + CHUNK], preferred_element_type=jnp.float32
-        )
+        ).astype(jnp.bfloat16)
 
 
 def shifts(pool_count):
@@ -365,7 +365,7 @@
 
     product = pl.pallas_call(
         functools.partial(merge_kernel, pool_count),
-        out_shape=jax.ShapeDtypeStruct((requests, w_out.shape[1]), f32),
+        out_shape=jax.ShapeDtypeStruct((requests, w_out.shape[1]), jnp.bfloat16),
         in_specs=[in_smem] + [in_vmem] * (pool_count + 1),
         out_specs=in_vmem,
         scratch_shapes=[pltpu.VMEM((pool_count, (requests + 1) * heads, HD), f32)],
@@ -374,7 +374,6 @@
         name="merge",
     )(routes, *partials, pin(w_out))
     tensor_count = lax.axis_size("tensor")
-    product = product.astype(jnp.bfloat16)
     one, two, three = [
         lax.ppermute(product, "tensor", [(i, i ^ d) for i in range(tensor_count)]).astype(f32)
         for d in (1, 2, 3)

time: 38.6 us -> 38.5 us (level)
  no operation moved by 1% of the time
where the time goes in v7:
time: 38.5 us; the launch traced here: 38.4 us
  starting transfers between devices  17 us (44%)
  waiting for transfers between devices  11.3 us (29%)
  Pallas kernels  7.57 us (20%)
  local copies, waits for them, and re-layouts  1.4 us (4%)
  other arithmetic  0.94 us (2%)
    ppermute x9, starting transfers between devices, shifted(): lax.ppermute(value, axis, [(i, (i + shift) % count) for i in range(count)])  14.9 us
    ppermute x9, waiting for transfers between devices, shifted(): lax.ppermute(value, axis, [(i, (i + shift) % count) for i in range(count)])  7.77 us
    ppermute x3, waiting for transfers between devices, close_pool(): lax.ppermute(product, 'tensor', [(i, i ^ d) for i in range(tensor_count)])  3.53 us
    pallas_call x1, Pallas kernels, close_pool(): pl.pallas_call(functools.partial(attend_kernel, pool_count, local_kv, gro...  2.44 us
    pallas_call x1, Pallas kernels, close_pool(): pl.pallas_call(functools.partial(merge_kernel, pool_count), out_shape=jax...  2.26 us
    ppermute x3, starting transfers between devices, close_pool(): lax.ppermute(product, 'tensor', [(i, i ^ d) for i in range(tensor_count)])  2.15 us
    pallas_call x1, Pallas kernels, close_pool(): pl.pallas_call(functools.partial(project_kernel, pool_count), out_shape=[...  1.99 us
    unnamed x30, local copies, waits for them, and re-layouts  1.4 us
  transfers between devices with their start and end apart: 12, of which 9 were waited for; matrix products, arithmetic and copies ran while one was open for 1% of the time, Pallas kernels for 2%

profile of v7, /device:TPU:0, one launch (start us, length us, event | category | flops | bytes accessed | tf_op | source)
XLA Modules:
  0.0 38.4 jit_solution(4320521668493909446)
XLA Ops:
  0.0 0.8 %copy-done = bf16[16,2048]{1,0:T(8,128)(2,1)S(1)} copy-done((bf16[16,2048]{1,0:T(8,128)(2,1)S(1)}, bf16[16,2048]{1,0:T(8,128)(2,1)}, u32[]{:S(2)}) %copy-start) | copy-done | bytes 65560
  0.9 3.0 %collective-permute-start = (f32[16,128]{1,0:T(8,128)S(1)}, f32[16,128]{1,0:T(8,128)S(1)}, u32[]{:S(2)}, u32[]{:S(2)}) collective-permute-start(f32[16,128]{1,0:T(8,128)S(1)} %square.1.after.rest_0_), channel_id=1, source_target_pairs={{0,4},{4,8},{8,12},{12,0},{1,5},{5,9},{9,13},{13,1},{2,6},{6,10},{... | collective-permute-start | bytes 24584 | tf_op jit(solution)/shard_map/ppermute | solution.py:261
  4.0 2.6 %collective-permute-start.1 = (f32[16,128]{1,0:T(8,128)S(1)}, f32[16,128]{1,0:T(8,128)S(1)}, u32[]{:S(2)}, u32[]{:S(2)}) collective-permute-start(f32[16,128]{1,0:T(8,128)S(1)} %square.1.after.rest_0_), channel_id=1, source_target_pairs={{0,8},{4,12},{8,0},{12,4},{1,9},{5,13},{9,1},{13,5},{2,10},{6,14},... | collective-permute-start | bytes 24584 | tf_op jit(solution)/shard_map/ppermute | solution.py:261
  6.6 1.3 %collective-permute-start.2 = (f32[16,128]{1,0:T(8,128)S(1)}, f32[16,128]{1,0:T(8,128)S(1)}, u32[]{:S(2)}, u32[]{:S(2)}) collective-permute-start(f32[16,128]{1,0:T(8,128)S(1)} %square.1.after.rest_0_), channel_id=1, source_target_pairs={{0,12},{4,0},{8,4},{12,8},{1,13},{5,1},{9,5},{13,9},{2,14},{6,2},{... | collective-permute-start | bytes 24584 | tf_op jit(solution)/shard_map/ppermute | solution.py:261
  7.9 0.8 %pick.1 = (f32[32,2048]{1,0:T(8,128)S(1)}, f32[32,128]{1,0:T(8,128)S(1)}) custom-call(s32[4,2,4]{2,1,0:T(2,128)S(1)} %bitcast.5, bf16[16,2048]{1,0:T(8,128)(2,1)S(1)} %copy-done, f32[16,128]{1,0:T(8,128)S(1)} %square.1.after.rest_0_), custom_call_target="tpu_custom_call" | custom-call | flops 17179869184 | bytes 33554432 | tf_op jit(solution)/shard_map/pick/pallas_call | solution.py:306
  8.7 1.5 %collective-permute-done.2.rest_3_ = f32[16,128]{1,0:T(8,128)S(1)} collective-permute-done((f32[16,128]{1,0:T(8,128)S(1)}, f32[16,128]{1,0:T(8,128)S(1)}, u32[]{:S(2)}, u32[]{:S(2)}) %collective-permute-start.2) | collective-permute-done | bytes 8224 | tf_op jit(solution)/shard_map/ppermute | solution.py:261
  10.8 2.0 %project.1 = (f32[8,2560]{1,0:T(8,128)S(1)}, f32[8,2560]{1,0:T(8,128)S(1)}, f32[8,2560]{1,0:T(8,128)S(1)}, f32[8,2560]{1,0:T(8,128)S(1)}) custom-call(f32[32,2048]{1,0:T(8,128)S(1)} %get-tuple-element.12.residual, f32[32,128]{1,0:T(8,128)S(1)} %get-tuple-element.13.pick, bf16[2048]{0:T(1024)(128)(2,1)S(1)} %copy-done.6, f32[16,128]{1,0:T(8,128)S(1)} %square.1.after.rest_0_, ...), custom_call_target="tpu_custom_call" | custom-call | flops 17179869184 | bytes 33554432 | tf_op jit(solution)/shard_map/project/pallas_call | solution.py:318
  12.8 0.7 %collective-permute-start.3 = (f16[8,2560]{1,0:T(8,128)(2,1)S(1)}, f16[8,2560]{1,0:T(8,128)(2,1)S(1)}, u32[]{:S(2)}, u32[]{:S(2)}) collective-permute-start(f16[8,2560]{1,0:T(8,128)(2,1)S(1)} %multiply_convert_fusion.2), channel_id=1, source_target_pairs={{0,4},{4,8},{8,12},{12,0},{1,5},{5,9},{9,13},{13,1},{2,6},{6,10},{... | collective-permute-start | bytes 122888 | tf_op jit(solution)/shard_map/ppermute | solution.py:261
  13.5 2.7 %collective-permute-start.4 = (f16[8,2560]{1,0:T(8,128)(2,1)S(1)}, f16[8,2560]{1,0:T(8,128)(2,1)S(1)}, u32[]{:S(2)}, u32[]{:S(2)}) collective-permute-start(f16[8,2560]{1,0:T(8,128)(2,1)S(1)} %multiply_convert_fusion.1), channel_id=1, source_target_pairs={{0,8},{4,12},{8,0},{12,4},{1,9},{5,13},{9,1},{13,5},{2,10},{6,14},... | collective-permute-start | bytes 122888 | tf_op jit(solution)/shard_map/ppermute | solution.py:261
  17.0 1.7 %collective-permute-done.3 = f16[8,2560]{1,0:T(8,128)(2,1)S(1)} collective-permute-done((f16[8,2560]{1,0:T(8,128)(2,1)S(1)}, f16[8,2560]{1,0:T(8,128)(2,1)S(1)}, u32[]{:S(2)}, u32[]{:S(2)}) %collective-permute-start.3) | collective-permute-done | bytes 40992 | tf_op jit(solution)/shard_map/ppermute | solution.py:261
  18.7 0.8 %collective-permute-done.4 = f16[8,2560]{1,0:T(8,128)(2,1)S(1)} collective-permute-done((f16[8,2560]{1,0:T(8,128)(2,1)S(1)}, f16[8,2560]{1,0:T(8,128)(2,1)S(1)}, u32[]{:S(2)}, u32[]{:S(2)}) %collective-permute-start.4) | collective-permute-done | bytes 40992 | tf_op jit(solution)/shard_map/ppermute | solution.py:261
  19.6 0.7 %collective-permute-done.5 = f16[8,2560]{1,0:T(8,128)(2,1)S(1)} collective-permute-done((f16[8,2560]{1,0:T(8,128)(2,1)S(1)}, f16[8,2560]{1,0:T(8,128)(2,1)S(1)}, u32[]{:S(2)}, u32[]{:S(2)}) %collective-permute-start.5) | collective-permute-done | bytes 40992 | tf_op jit(solution)/shard_map/ppermute | solution.py:261
  20.3 2.4 %attend.1.rest_0_ = bf16[9,16,128]{2,1,0:T(8,128)(2,1)S(1)} custom-call(s32[4,2,4]{2,1,0:T(2,128)S(1)} %bitcast.6, s32[16]{0:T(128)S(1)} %copy-done.8, s32[48]{0:T(128)S(1)} %copy-done.9, s32[48]{0:T(128)S(1)} %copy-done.10, f32[16,256]{1,0:T(8,128)S(1)} %pad_maximum_fusion.turn, f32[8,2560]{1,0:T(8,128)S(1)} %get-tuple-element.14.rest_0_, ...), custom_call_target="tpu_custom_call" | custom-call | flops 17179869184 | bytes 33554432 | tf_op jit(solution)/shard_map/attend/pallas_call | solution.py:345
  22.8 1.1 %collective-permute-start.6 = (bf16[9,16,128]{2,1,0:T(8,128)(2,1)S(1)}, bf16[9,16,128]{2,1,0:T(8,128)(2,1)S(1)}, u32[]{:S(2)}, u32[]{:S(2)}) collective-permute-start(bf16[9,16,128]{2,1,0:T(8,128)(2,1)S(1)} %attend.1.rest_0_), channel_id=1, source_target_pairs={{0,4},{4,8},{8,12},{12,0},{1,5},{5,9},{9,13},{13,1},{2,6},{6,10},{... | collective-permute-start | bytes 110600 | tf_op jit(solution)/shard_map/ppermute | solution.py:261
  23.9 1.8 %collective-permute-start.7 = (bf16[9,16,128]{2,1,0:T(8,128)(2,1)S(1)}, bf16[9,16,128]{2,1,0:T(8,128)(2,1)S(1)}, u32[]{:S(2)}, u32[]{:S(2)}) collective-permute-start(bf16[9,16,128]{2,1,0:T(8,128)(2,1)S(1)} %attend.1.rest_0_), channel_id=1, source_target_pairs={{0,8},{4,12},{8,0},{12,4},{1,9},{5,13},{9,1},{13,5},{2,10},{6,14},... | collective-permute-start | bytes 110600 | tf_op jit(solution)/shard_map/ppermute | solution.py:261
  25.7 1.0 %collective-permute-start.8 = (bf16[9,16,128]{2,1,0:T(8,128)(2,1)S(1)}, bf16[9,16,128]{2,1,0:T(8,128)(2,1)S(1)}, u32[]{:S(2)}, u32[]{:S(2)}) collective-permute-start(bf16[9,16,128]{2,1,0:T(8,128)(2,1)S(1)} %attend.1.rest_0_), channel_id=1, source_target_pairs={{0,12},{4,0},{8,4},{12,8},{1,13},{5,1},{9,5},{13,9},{2,14},{6,2},{... | collective-permute-start | bytes 110600 | tf_op jit(solution)/shard_map/ppermute | solution.py:261
  26.7 1.9 %collective-permute-done.6.rest_1_ = bf16[9,16,128]{2,1,0:T(8,128)(2,1)S(1)} collective-permute-done((bf16[9,16,128]{2,1,0:T(8,128)(2,1)S(1)}, bf16[9,16,128]{2,1,0:T(8,128)(2,1)S(1)}, u32[]{:S(2)}, u32[]{:S(2)}) %collective-permute-start.6) | collective-permute-done | bytes 36896 | tf_op jit(solution)/shard_map/ppermute | solution.py:261
  28.6 0.8 %collective-permute-done.7.rest_2_ = bf16[9,16,128]{2,1,0:T(8,128)(2,1)S(1)} collective-permute-done((bf16[9,16,128]{2,1,0:T(8,128)(2,1)S(1)}, bf16[9,16,128]{2,1,0:T(8,128)(2,1)S(1)}, u32[]{:S(2)}, u32[]{:S(2)}) %collective-permute-start.7) | collective-permute-done | bytes 36896 | tf_op jit(solution)/shard_map/ppermute | solution.py:261
  29.8 2.3 %merge.1 = bf16[16,2048]{1,0:T(8,128)(2,1)S(1)} custom-call(s32[4,2,4]{2,1,0:T(2,128)S(1)} %bitcast.7, bf16[9,16,128]{2,1,0:T(8,128)(2,1)S(1)} %attend.1.rest_0_, bf16[9,16,128]{2,1,0:T(8,128)(2,1)S(1)} %collective-permute-done.6.rest_1_, bf16[9,16,128]{2,1,0:T(8,128)(2,1)S(1)} %collective-permute-done.7.rest_2_, ...), custom_call_target="tpu_custom_call" | custom-call | flops 17179869184 | bytes 33554432 | tf_op jit(solution)/shard_map/merge/pallas_call | solution.py:366
  32.0 1.5 %collective-permute-start.10 = (bf16[16,2048]{1,0:T(8,128)(2,1)S(1)}, bf16[16,2048]{1,0:T(8,128)(2,1)S(1)}, u32[]{:S(2)}, u32[]{:S(2)}) collective-permute-start(bf16[16,2048]{1,0:T(8,128)(2,1)S(1)} %merge.1), channel_id=1, source_target_pairs={{0,2},{1,3},{2,0},{3,1},{4,6},{5,7},{6,4},{7,5},{8,10},{9,11},{10,... | collective-permute-start | bytes 196616 | tf_op jit(solution)/shard_map/ppermute | solution.py:378
  33.5 0.6 %collective-permute-start.9 = (bf16[16,2048]{1,0:T(8,128)(2,1)S(1)}, bf16[16,2048]{1,0:T(8,128)(2,1)S(1)}, u32[]{:S(2)}, u32[]{:S(2)}) collective-permute-start(bf16[16,2048]{1,0:T(8,128)(2,1)S(1)} %merge.1), channel_id=1, source_target_pairs={{0,1},{1,0},{2,3},{3,2},{4,5},{5,4},{6,7},{7,6},{8,9},{9,8},{10,11... | collective-permute-start | bytes 196616 | tf_op jit(solution)/shard_map/ppermute | solution.py:378
  34.2 2.1 %collective-permute-done.10 = bf16[16,2048]{1,0:T(8,128)(2,1)S(1)} collective-permute-done((bf16[16,2048]{1,0:T(8,128)(2,1)S(1)}, bf16[16,2048]{1,0:T(8,128)(2,1)S(1)}, u32[]{:S(2)}, u32[]{:S(2)}) %collective-permute-start.10) | collective-permute-done | bytes 65568 | tf_op jit(solution)/shard_map/ppermute | solution.py:378
  36.3 1.4 %collective-permute-done.11 = bf16[16,2048]{1,0:T(8,128)(2,1)S(1)} collective-permute-done((bf16[16,2048]{1,0:T(8,128)(2,1)S(1)}, bf16[16,2048]{1,0:T(8,128)(2,1)S(1)}, u32[]{:S(2)}, u32[]{:S(2)}) %collective-permute-start.11) | collective-permute-done | bytes 65568 | tf_op jit(solution)/shard_map/ppermute | solution.py:378
  37.7 0.7 %add_convert_fusion = bf16[16,2048]{1,0:T(8,128)(2,1)} fusion(bf16[16,2048]{1,0:T(8,128)(2,1)S(1)} %collective-permute-done.11, bf16[16,2048]{1,0:T(8,128)(2,1)S(1)} %collective-permute-done.10, bf16[16,2048]{1,0:T(8,128)(2,1)S(1)} %collective-permute-done.9, bf16[16,2048]{1,0:T(8,128)(2,1)S(1)} %merge.1, bf16[16,2048]{1,0:T(8,128)(2,1)S(1)} %copy-done.1), kind=kLoop, calls=%fused_computation | loop fusion | flops 327680 | bytes 393216 | tf_op jit(solution)/shard_map/convert_element_type | solution.py:382
  (48 shorter events, 1.9 us)
Async XLA Ops:
  0.8 7.1 %copy-start.7 = (s32[4,4,2]{1,2,0:T(2,128)S(1)}, s32[4,4,2]{1,2,0:T(2,128)}, u32[]{:S(2)}) copy-start(s32[4,4,2]{1,2,0:T(2,128)} %param.21) | copy-start | bytes 388
  0.8 9.4 %slice-start = ((s8[8388608]{0:T(1024)(128)(4,1)}), s8[4194304]{0:T(1024)(128)(4,1)S(1)}, s32[]{:S(2)}) async-start(s8[8388608]{0:T(1024)(128)(4,1)} %bitcast.1), calls=%async_computation | async-start | bytes 8388608
  0.9 7.8 %collective-permute-start = (f32[16,128]{1,0:T(8,128)S(1)}, f32[16,128]{1,0:T(8,128)S(1)}, u32[]{:S(2)}, u32[]{:S(2)}) collective-permute-start(f32[16,128]{1,0:T(8,128)S(1)} %square.1.after.rest_0_), channel_id=1, source_target_pairs={{0,4},{4,8},{8,12},{12,0},{1,5},{5,9},{9,13},{13,1},{2,6},{6,10},{... | collective-permute-start | bytes 24584 | tf_op jit(solution)/shard_map/ppermute | solution.py:261
  4.0 4.8 %collective-permute-start.1 = (f32[16,128]{1,0:T(8,128)S(1)}, f32[16,128]{1,0:T(8,128)S(1)}, u32[]{:S(2)}, u32[]{:S(2)}) collective-permute-start(f32[16,128]{1,0:T(8,128)S(1)} %square.1.after.rest_0_), channel_id=1, source_target_pairs={{0,8},{4,12},{8,0},{12,4},{1,9},{5,13},{9,1},{13,5},{2,10},{6,14},... | collective-permute-start | bytes 24584 | tf_op jit(solution)/shard_map/ppermute | solution.py:261
  6.6 3.7 %collective-permute-start.2 = (f32[16,128]{1,0:T(8,128)S(1)}, f32[16,128]{1,0:T(8,128)S(1)}, u32[]{:S(2)}, u32[]{:S(2)}) collective-permute-start(f32[16,128]{1,0:T(8,128)S(1)} %square.1.after.rest_0_), channel_id=1, source_target_pairs={{0,12},{4,0},{8,4},{12,8},{1,13},{5,1},{9,5},{13,9},{2,14},{6,2},{... | collective-permute-start | bytes 24584 | tf_op jit(solution)/shard_map/ppermute | solution.py:261
  7.9 2.5 %copy-start.4 = (bf16[2048,256]{1,0:T(8,128)(2,1)S(1)}, bf16[2048,256]{1,0:T(8,128)(2,1)}, u32[]{:S(2)}) copy-start(bf16[2048,256]{1,0:T(8,128)(2,1)} %rest_4_.3) | copy-start | bytes 3145732
  7.9 2.8 %copy-start.5 = (bf16[2048,256]{1,0:T(8,128)(2,1)S(1)}, bf16[2048,256]{1,0:T(8,128)(2,1)}, u32[]{:S(2)}) copy-start(bf16[2048,256]{1,0:T(8,128)(2,1)} %rest_5_.2) | copy-start | bytes 3145732
  7.9 2.8 %copy-start.6 = (bf16[2048]{0:T(1024)(128)(2,1)S(1)}, bf16[2048]{0:T(1024)(128)(2,1)}, u32[]{:S(2)}) copy-start(bf16[2048]{0:T(1024)(128)(2,1)} %gain.1) | copy-start | bytes 12292
  10.7 9.6 %copy-start.2 = (bf16[48,128,256]{2,1,0:T(8,128)(2,1)S(1)}, bf16[48,128,256]{2,1,0:T(8,128)(2,1)}, u32[]{:S(2)}) copy-start(bf16[48,128,256]{2,1,0:T(8,128)(2,1)} %rest_4_.4) | copy-start | bytes 9437188
  10.7 9.6 %copy-start.3 = (bf16[48,128,256]{2,1,0:T(8,128)(2,1)S(1)}, bf16[48,128,256]{2,1,0:T(8,128)(2,1)}, u32[]{:S(2)}) copy-start(bf16[48,128,256]{2,1,0:T(8,128)(2,1)} %rest_5_.3) | copy-start | bytes 9437188
  10.7 9.6 %copy-start.9 = (s32[48]{0:T(128)S(1)}, s32[48]{0:T(128)}, u32[]{:S(2)}) copy-start(s32[48]{0:T(128)} %slot_route.1) | copy-start | bytes 580
  10.7 9.6 %copy-start.10 = (s32[48]{0:T(128)S(1)}, s32[48]{0:T(128)}, u32[]{:S(2)}) copy-start(s32[48]{0:T(128)} %slot_block.1) | copy-start | bytes 580
  10.7 19.0 %slice-start.2 = ((s8[8388608]{0:T(1024)(128)(4,1)}), s8[4194304]{0:T(1024)(128)(4,1)S(1)}, s32[]{:S(2)}) async-start(s8[8388608]{0:T(1024)(128)(4,1)} %bitcast.3), calls=%async_computation.2 | async-start | bytes 8388608
  12.8 6.0 %collective-permute-start.3 = (f16[8,2560]{1,0:T(8,128)(2,1)S(1)}, f16[8,2560]{1,0:T(8,128)(2,1)S(1)}, u32[]{:S(2)}, u32[]{:S(2)}) collective-permute-start(f16[8,2560]{1,0:T(8,128)(2,1)S(1)} %multiply_convert_fusion.2), channel_id=1, source_target_pairs={{0,4},{4,8},{8,12},{12,0},{1,5},{5,9},{9,13},{13,1},{2,6},{6,10},{... | collective-permute-start | bytes 122888 | tf_op jit(solution)/shard_map/ppermute | solution.py:261
  13.5 6.1 %collective-permute-start.4 = (f16[8,2560]{1,0:T(8,128)(2,1)S(1)}, f16[8,2560]{1,0:T(8,128)(2,1)S(1)}, u32[]{:S(2)}, u32[]{:S(2)}) collective-permute-start(f16[8,2560]{1,0:T(8,128)(2,1)S(1)} %multiply_convert_fusion.1), channel_id=1, source_target_pairs={{0,8},{4,12},{8,0},{12,4},{1,9},{5,13},{9,1},{13,5},{2,10},{6,14},... | collective-permute-start | bytes 122888 | tf_op jit(solution)/shard_map/ppermute | solution.py:261
  16.2 4.1 %collective-permute-start.5 = (f16[8,2560]{1,0:T(8,128)(2,1)S(1)}, f16[8,2560]{1,0:T(8,128)(2,1)S(1)}, u32[]{:S(2)}, u32[]{:S(2)}) collective-permute-start(f16[8,2560]{1,0:T(8,128)(2,1)S(1)} %multiply_convert_fusion), channel_id=1, source_target_pairs={{0,12},{4,0},{8,4},{12,8},{1,13},{5,1},{9,5},{13,9},{2,14},{6,2},{... | collective-permute-start | bytes 122888 | tf_op jit(solution)/shard_map/ppermute | solution.py:261
  16.9 12.8 %slice-start.3 = ((s8[8388608]{0:T(1024)(128)(4,1)}), s8[4194304]{0:T(1024)(128)(4,1)S(1)}, s32[]{:S(2)}) async-start(s8[8388608]{0:T(1024)(128)(4,1)} %bitcast.3), calls=%async_computation.3 | async-start | bytes 8388608
  22.8 15.0 %copy-start.1 = (bf16[16,2048]{1,0:T(8,128)(2,1)S(1)}, bf16[16,2048]{1,0:T(8,128)(2,1)}, u32[]{:S(2)}) copy-start(bf16[16,2048]{1,0:T(8,128)(2,1)} %residual.3) | copy-start | bytes 196612
  22.8 5.8 %collective-permute-start.6 = (bf16[9,16,128]{2,1,0:T(8,128)(2,1)S(1)}, bf16[9,16,128]{2,1,0:T(8,128)(2,1)S(1)}, u32[]{:S(2)}, u32[]{:S(2)}) collective-permute-start(bf16[9,16,128]{2,1,0:T(8,128)(2,1)S(1)} %attend.1.rest_0_), channel_id=1, source_target_pairs={{0,4},{4,8},{8,12},{12,0},{1,5},{5,9},{9,13},{13,1},{2,6},{6,10},{... | collective-permute-start | bytes 110600 | tf_op jit(solution)/shard_map/ppermute | solution.py:261
  23.9 5.5 %collective-permute-start.7 = (bf16[9,16,128]{2,1,0:T(8,128)(2,1)S(1)}, bf16[9,16,128]{2,1,0:T(8,128)(2,1)S(1)}, u32[]{:S(2)}, u32[]{:S(2)}) collective-permute-start(bf16[9,16,128]{2,1,0:T(8,128)(2,1)S(1)} %attend.1.rest_0_), channel_id=1, source_target_pairs={{0,8},{4,12},{8,0},{12,4},{1,9},{5,13},{9,1},{13,5},{2,10},{6,14},... | collective-permute-start | bytes 110600 | tf_op jit(solution)/shard_map/ppermute | solution.py:261
  25.7 4.1 %collective-permute-start.8 = (bf16[9,16,128]{2,1,0:T(8,128)(2,1)S(1)}, bf16[9,16,128]{2,1,0:T(8,128)(2,1)S(1)}, u32[]{:S(2)}, u32[]{:S(2)}) collective-permute-start(bf16[9,16,128]{2,1,0:T(8,128)(2,1)S(1)} %attend.1.rest_0_), channel_id=1, source_target_pairs={{0,12},{4,0},{8,4},{12,8},{1,13},{5,1},{9,5},{13,9},{2,14},{6,2},{... | collective-permute-start | bytes 110600 | tf_op jit(solution)/shard_map/ppermute | solution.py:261
  32.0 4.3 %collective-permute-start.10 = (bf16[16,2048]{1,0:T(8,128)(2,1)S(1)}, bf16[16,2048]{1,0:T(8,128)(2,1)S(1)}, u32[]{:S(2)}, u32[]{:S(2)}) collective-permute-start(bf16[16,2048]{1,0:T(8,128)(2,1)S(1)} %merge.1), channel_id=1, source_target_pairs={{0,2},{1,3},{2,0},{3,1},{4,6},{5,7},{6,4},{7,5},{8,10},{9,11},{10,... | collective-permute-start | bytes 196616 | tf_op jit(solution)/shard_map/ppermute | solution.py:378
  33.5 4.2 %collective-permute-start.11 = (bf16[16,2048]{1,0:T(8,128)(2,1)S(1)}, bf16[16,2048]{1,0:T(8,128)(2,1)S(1)}, u32[]{:S(2)}, u32[]{:S(2)}) collective-permute-start(bf16[16,2048]{1,0:T(8,128)(2,1)S(1)} %merge.1), channel_id=1, source_target_pairs={{0,3},{1,2},{2,1},{3,0},{4,7},{5,6},{6,5},{7,4},{8,11},{9,10},{10,... | collective-permute-start | bytes 196616 | tf_op jit(solution)/shard_map/ppermute | solution.py:378
  33.5 4.2 %collective-permute-start.9 = (bf16[16,2048]{1,0:T(8,128)(2,1)S(1)}, bf16[16,2048]{1,0:T(8,128)(2,1)S(1)}, u32[]{:S(2)}, u32[]{:S(2)}) collective-permute-start(bf16[16,2048]{1,0:T(8,128)(2,1)S(1)} %merge.1), channel_id=1, source_target_pairs={{0,1},{1,0},{2,3},{3,2},{4,5},{5,4},{6,7},{7,6},{8,9},{9,8},{10,11... | collective-permute-start | bytes 196616 | tf_op jit(solution)/shard_map/ppermute | solution.py:378
  (3 other events, 5.2 us)
